TPU v7x, 32 devices: a whole 2x2x4 slice. The times are simulated.
32 devices in a mesh: dp: 8 (over y, x, core), shard: 4 (over z).
Axes of the slice: x: 2, y: 2, z: 4, core: 2. Of those that a mesh axis runs over, the one named last changes fastest.
Arguments:
- tokens: bfloat16 [8192, 2048], P(('dp', 'shard')), may hold values from -6 to 6
- out_grad: bfloat16 [8192, 2048], P(('dp', 'shard')), may hold values from -6 to 6
- routes: int32 [8192, 2], P(('dp', 'shard')), may hold values from 0 to 3, all different within a row; in each aligned block of 256 rows (0 to 255, 256 to 511, ...) at most 170 rows name the same one
- gate_weights: float32 [8192, 2], P(('dp', 'shard')), may hold values from 0.2 to 1
- prefix: int32 [8], P('dp'), may hold values from 102 to 512
- query_weight: bfloat16 [2048, 2048], P(None, 'shard'), may hold values from -0.125 to 0.125
- key_weight: bfloat16 [2048, 2048], P(None, 'shard'), may hold values from -0.125 to 0.125
- value_weight: bfloat16 [2048, 2048], P(None, 'shard'), may hold values from -0.125 to 0.125
- output_weight: bfloat16 [2048, 2048], P(None, 'shard'), may hold values from -2 to 2
- norm_gains: bfloat16 [4, 2048], P(None, 'shard'), may hold values from 0.5 to 1.5
- expert_gate: bfloat16 [4, 2048, 1024], P(None, None, 'shard'), may hold values from -0.125 to 0.125
- expert_up: bfloat16 [4, 2048, 1024], P(None, None, 'shard'), may hold values from -0.125 to 0.125
- expert_down: bfloat16 [4, 1024, 2048], P(None, 'shard'), may hold values from -0.375 to 0.375
Outputs:
- layer_out: bfloat16 [8192, 2048], P(('dp', 'shard'))
- grad_tokens: float32 [8192, 2048], P(('dp', 'shard'))
- root_means: float32 [3, 8192], P(None, ('dp', 'shard'))
- grad_query: float32 [2048, 2048], P(None, 'shard')
- grad_key: float32 [2048, 2048], P(None, 'shard')
- grad_value: float32 [2048, 2048], P(None, 'shard')
- grad_output: float32 [2048, 2048], P(None, 'shard')
- grad_gains: float32 [4, 2048], P(None, 'shard')
- grad_gate: float32 [4, 2048, 1024], P(None, None, 'shard')
- grad_up: float32 [4, 2048, 1024], P(None, None, 'shard')
- grad_down: float32 [4, 1024, 2048], P(None, 'shard')
Inputs may be any that keep to these rules, and one draw needn't show every extreme that they name: `routes`: each row names 2 different experts; among the rows of one device each expert is named by at most 170 rows, and on some devices one expert is named by exactly 170 rows.
All inputs are finite; a program needn't handle non-finite values.
Results may differ from a plain program's by a relative error of at most 0.023.
Values may be sent and summed in bfloat16 or wider, within the bound.
A program may use at most 384 MiB of HBM per device.

v0:
```python
import jax
import jax.numpy as jnp
from jax import lax
from jax.sharding import PartitionSpec as P

HEAD_DIM = 128
CAP = 170


EPSILON = 1e-05
ROPE_BASE = 10000.0
MASKED = -1e30


def rotary_tables(positions, half_dim):
    inverse = ROPE_BASE ** (-jnp.arange(half_dim, dtype=jnp.float32) / half_dim)
    angles = positions.astype(jnp.float32)[:, None] * inverse[None, :]
    return (jnp.cos(angles), jnp.sin(angles))


def rotate(values, cosine, sine):
    row_count = values.shape[0]
    half_dim = cosine.shape[1]
    halves = values.reshape(row_count, -1, 2, half_dim)
    leading = halves[:, :, 0, :]
    trailing = halves[:, :, 1, :]
    cos_wide = cosine[:, None, :]
    sin_wide = sine[:, None, :]
    turned = jnp.stack(
        [leading * cos_wide - trailing * sin_wide, trailing * cos_wide + leading * sin_wide], axis=2
    )
    return turned.reshape(row_count, -1)


def norm_stats(values):
    factor = lax.rsqrt(jnp.mean(values * values, axis=-1, keepdims=True) + EPSILON)
    return (values * factor, factor)


def norm_back(grad_unit, unit_rows, factor):
    return factor * (
        grad_unit - unit_rows * jnp.mean(grad_unit * unit_rows, axis=-1, keepdims=True)
    )


def root_mean(values):
    return jnp.sqrt(jnp.mean(values * values, axis=-1))


def per_device(
    tokens,
    out_grad,
    routes,
    gate_weights,
    prefix,
    query_weight,
    key_weight,
    value_weight,
    output_weight,
    norm_gains,
    expert_gate,
    expert_up,
    expert_down,
):
    row_count = tokens.shape[0]
    width = tokens.shape[1]
    shard_count = lax.axis_size("shard")
    place = lax.axis_index("shard")
    seq_length = row_count * shard_count
    key_block = min(512, seq_length)
    head_count = width // HEAD_DIM
    half_dim = HEAD_DIM // 2
    scale = HEAD_DIM ** (-0.5)
    expert_count = expert_gate.shape[0]
    slot_count = CAP
    bf16 = jnp.bfloat16
    f32 = jnp.float32
    full_query, full_key, full_value, full_output, full_gains = (
        lax.all_gather(query_weight, "shard", axis=1, tiled=True),
        lax.all_gather(key_weight, "shard", axis=1, tiled=True),
        lax.all_gather(value_weight, "shard", axis=1, tiled=True),
        lax.all_gather(output_weight, "shard", axis=1, tiled=True),
        lax.all_gather(norm_gains, "shard", axis=1, tiled=True),
    )
    gains_fwd = full_gains.astype(f32)
    inputs = tokens.astype(f32)
    positions = place * row_count + jnp.arange(row_count, dtype=jnp.int32)
    cosine, sine = rotary_tables(positions, half_dim)
    unit_x, factor_x = norm_stats(inputs)
    normed = (unit_x * gains_fwd[0]).astype(bf16)
    query_raw = jnp.dot(normed, full_query, preferred_element_type=f32)
    key_raw = jnp.dot(normed, full_key, preferred_element_type=f32)
    value_raw = jnp.dot(normed, full_value, preferred_element_type=f32)
    unit_query, factor_query = norm_stats(query_raw)
    queries = rotate(unit_query * gains_fwd[1], cosine, sine).astype(bf16)
    unit_key, factor_key = norm_stats(key_raw)
    keys = rotate(unit_key * gains_fwd[2], cosine, sine).astype(bf16)
    values = value_raw.astype(bf16)
    keys_all, values_all = (
        lax.all_gather(keys, "shard", axis=0, tiled=True),
        lax.all_gather(values, "shard", axis=0, tiled=True),
    )
    query_heads = queries.reshape(row_count, head_count, HEAD_DIM)
    key_heads = keys_all.reshape(seq_length, head_count, HEAD_DIM)
    value_heads = values_all.reshape(seq_length, head_count, HEAD_DIM)
    limit = prefix[0]
    last_row = place * row_count + row_count
    block_total = (jnp.maximum(last_row, limit) + key_block - 1) // key_block

    def scores_at(start):
        key_slab = lax.dynamic_slice_in_dim(key_heads, start, key_block, 0)
        raw_scores = (
            jnp.einsum("thd,khd->htk", query_heads, key_slab, preferred_element_type=f32) * scale
        )
        key_pos = start + jnp.arange(key_block, dtype=jnp.int32)
        visible = (key_pos[None, :] <= positions[:, None]) | (key_pos[None, :] < limit)
        return jnp.where(visible[None], raw_scores, MASKED)

    def normalizer_pass(block_index, running):
        running_max, running_sum = running
        scores = scores_at(block_index * key_block)
        new_max = jnp.maximum(running_max, jnp.max(scores, axis=-1))
        running_sum = running_sum * jnp.exp(running_max - new_max) + jnp.sum(
            jnp.exp(scores - new_max[..., None]), axis=-1
        )
        return (new_max, running_sum)

    start_max = jnp.full((head_count, row_count), MASKED, f32)
    start_sum = jnp.zeros((head_count, row_count), f32)
    final_max, final_sum = lax.fori_loop(0, block_total, normalizer_pass, (start_max, start_sum))
    log_total = final_max + jnp.log(final_sum)

    def mixing_pass(block_index, running):
        start = block_index * key_block
        probs = jnp.exp(scores_at(start) - log_total[..., None]).astype(bf16)
        value_slab = lax.dynamic_slice_in_dim(value_heads, start, key_block, 0)
        return running + jnp.einsum("htk,khd->htd", probs, value_slab, preferred_element_type=f32)

    mixed = lax.fori_loop(
        0, block_total, mixing_pass, jnp.zeros((head_count, row_count, HEAD_DIM), f32)
    )
    mixed_b = mixed.transpose(1, 0, 2).reshape(row_count, width).astype(bf16)
    attended = jnp.dot(mixed_b, full_output, preferred_element_type=f32)
    residual = inputs + attended
    unit_res, factor_res = norm_stats(residual)
    expert_in = (unit_res * gains_fwd[3]).astype(bf16)
    flat_routes = routes.reshape(-1)
    onehot = (flat_routes[:, None] == jnp.arange(expert_count, dtype=jnp.int32)[None, :]).astype(
        jnp.int32
    )
    rank = jnp.sum((jnp.cumsum(onehot, axis=0) - 1) * onehot, axis=1)
    slot_ids = flat_routes * slot_count + rank
    token_ids = jnp.arange(flat_routes.shape[0], dtype=jnp.int32) // routes.shape[1]
    owner = (
        jnp.zeros(expert_count * slot_count, jnp.int32)
        .at[slot_ids]
        .set(token_ids)
        .reshape(expert_count, slot_count)
    )
    slot_gate = (
        jnp.zeros(expert_count * slot_count, f32)
        .at[slot_ids]
        .set(gate_weights.reshape(-1))
        .reshape(expert_count, slot_count)
    )
    owner_flat = owner.reshape(-1)
    taken = expert_in[owner]
    use_gate, use_up, use_down = (
        lax.all_gather(expert_gate, "shard", axis=2, tiled=True),
        lax.all_gather(expert_up, "shard", axis=2, tiled=True),
        lax.all_gather(expert_down, "shard", axis=1, tiled=True),
    )
    gate_part = jnp.einsum("ecd,edf->ecf", taken, use_gate, preferred_element_type=f32)
    up_part = jnp.einsum("ecd,edf->ecf", taken, use_up, preferred_element_type=f32)
    sigmoid_gate = jax.nn.sigmoid(gate_part)
    hidden_units = (gate_part * sigmoid_gate * up_part).astype(bf16)
    made = jnp.einsum("ecf,efd->ecd", hidden_units, use_down, preferred_element_type=f32)
    expert_sum = (
        jnp.zeros((row_count, width), f32)
        .at[owner_flat]
        .add((made * slot_gate[..., None]).reshape(-1, width))
    )
    output = residual + expert_sum
    root_means = jnp.stack([root_mean(attended), root_mean(expert_sum), root_mean(output)])
    cotangent = out_grad.astype(f32)
    made_grad = (cotangent[owner] * slot_gate[..., None]).astype(bf16)
    grad_down_part = jnp.einsum("ecf,ecd->efd", hidden_units, made_grad, preferred_element_type=f32)
    hidden_grad = jnp.einsum("ecd,efd->ecf", made_grad, use_down, preferred_element_type=f32)
    up_grad = (hidden_grad * gate_part * sigmoid_gate).astype(bf16)
    gate_grad = (
        hidden_grad * up_part * sigmoid_gate * (1.0 + gate_part * (1.0 - sigmoid_gate))
    ).astype(bf16)
    grad_gate_part = jnp.einsum("ecd,ecf->edf", taken, gate_grad, preferred_element_type=f32)
    grad_up_part = jnp.einsum("ecd,ecf->edf", taken, up_grad, preferred_element_type=f32)
    taken_grad = jnp.einsum(
        "ecf,edf->ecd", gate_grad, use_gate, preferred_element_type=f32
    ) + jnp.einsum("ecf,edf->ecd", up_grad, use_up, preferred_element_type=f32)
    owned_gate, owned_up, owned_down = (
        lax.psum_scatter(
            grad_gate_part.astype(jnp.bfloat16), "shard", scatter_dimension=2, tiled=True
        ).astype(jnp.float32),
        lax.psum_scatter(
            grad_up_part.astype(jnp.bfloat16), "shard", scatter_dimension=2, tiled=True
        ).astype(jnp.float32),
        lax.psum_scatter(
            grad_down_part.astype(jnp.bfloat16), "shard", scatter_dimension=1, tiled=True
        ).astype(jnp.float32),
    )
    expert_in_grad = (
        jnp.zeros((row_count, width), f32).at[owner_flat].add(taken_grad.reshape(-1, width))
    )
    gain_grad_res = jnp.sum(expert_in_grad * unit_res, axis=0)
    residual_grad = cotangent + norm_back(expert_in_grad * gains_fwd[3], unit_res, factor_res)
    attended_grad = residual_grad.astype(bf16)
    grad_output_full = jnp.einsum("td,te->de", mixed_b, attended_grad, preferred_element_type=f32)
    mixed_grad = jnp.einsum(
        "te,de->td", attended_grad, full_output, preferred_element_type=f32
    ).astype(bf16)
    grad_heads = mixed_grad.reshape(row_count, head_count, HEAD_DIM)
    delta = jnp.sum(grad_heads.astype(f32).transpose(1, 0, 2) * mixed, axis=-1)

    def backward_pass(block_index, running):
        query_acc, key_acc, value_acc = running
        start = block_index * key_block
        probs = jnp.exp(scores_at(start) - log_total[..., None])
        key_slab = lax.dynamic_slice_in_dim(key_heads, start, key_block, 0)
        value_slab = lax.dynamic_slice_in_dim(value_heads, start, key_block, 0)
        prob_grad = jnp.einsum("thd,khd->htk", grad_heads, value_slab, preferred_element_type=f32)
        score_grad = (probs * (prob_grad - delta[..., None])).astype(bf16)
        query_acc = query_acc + jnp.einsum(
            "htk,khd->thd", score_grad, key_slab, preferred_element_type=f32
        )
        key_piece = jnp.einsum("htk,thd->khd", score_grad, query_heads, preferred_element_type=f32)
        value_piece = jnp.einsum(
            "htk,thd->khd", probs.astype(bf16), grad_heads, preferred_element_type=f32
        )
        key_acc = lax.dynamic_update_slice_in_dim(key_acc, key_piece, start, 0)
        value_acc = lax.dynamic_update_slice_in_dim(value_acc, value_piece, start, 0)
        return (query_acc, key_acc, value_acc)

    start_query = jnp.zeros((row_count, head_count, HEAD_DIM), f32)
    start_keys = jnp.zeros((seq_length, head_count, HEAD_DIM), f32)
    query_acc, key_acc, value_acc = lax.fori_loop(
        0, block_total, backward_pass, (start_query, start_keys, start_keys)
    )
    key_own, value_own = (
        lax.psum_scatter(
            key_acc.reshape(seq_length, width).astype(jnp.bfloat16),
            "shard",
            scatter_dimension=0,
            tiled=True,
        ).astype(jnp.float32),
        lax.psum_scatter(
            value_acc.reshape(seq_length, width).astype(jnp.bfloat16),
            "shard",
            scatter_dimension=0,
            tiled=True,
        ).astype(jnp.float32),
    )
    query_norm_grad = rotate(query_acc.reshape(row_count, width) * scale, cosine, -sine)
    key_norm_grad = rotate(key_own * scale, cosine, -sine)
    gain_grad_query = jnp.sum(query_norm_grad * unit_query, axis=0)
    gain_grad_key = jnp.sum(key_norm_grad * unit_key, axis=0)
    query_raw_grad = norm_back(query_norm_grad * gains_fwd[1], unit_query, factor_query).astype(
        bf16
    )
    key_raw_grad = norm_back(key_norm_grad * gains_fwd[2], unit_key, factor_key).astype(bf16)
    value_raw_grad = value_own.astype(bf16)
    grad_query_full = jnp.einsum("td,te->de", normed, query_raw_grad, preferred_element_type=f32)
    grad_key_full = jnp.einsum("td,te->de", normed, key_raw_grad, preferred_element_type=f32)
    grad_value_full = jnp.einsum("td,te->de", normed, value_raw_grad, preferred_element_type=f32)
    normed_grad = jnp.einsum("te,de->td", query_raw_grad, full_query, preferred_element_type=f32)
    normed_grad = normed_grad + jnp.einsum(
        "te,de->td", key_raw_grad, full_key, preferred_element_type=f32
    )
    normed_grad = normed_grad + jnp.einsum(
        "te,de->td", value_raw_grad, full_value, preferred_element_type=f32
    )
    gain_grad_x = jnp.sum(normed_grad * unit_x, axis=0)
    grad_tokens = residual_grad + norm_back(normed_grad * gains_fwd[0], unit_x, factor_x)
    gain_grads = jnp.stack([gain_grad_x, gain_grad_query, gain_grad_key, gain_grad_res])
    owned_query, owned_key, owned_value, owned_output, owned_gains = (
        lax.psum_scatter(
            grad_query_full.astype(jnp.bfloat16), "shard", scatter_dimension=1, tiled=True
        ).astype(jnp.float32),
        lax.psum_scatter(
            grad_key_full.astype(jnp.bfloat16), "shard", scatter_dimension=1, tiled=True
        ).astype(jnp.float32),
        lax.psum_scatter(
            grad_value_full.astype(jnp.bfloat16), "shard", scatter_dimension=1, tiled=True
        ).astype(jnp.float32),
        lax.psum_scatter(
            grad_output_full.astype(jnp.bfloat16), "shard", scatter_dimension=1, tiled=True
        ).astype(jnp.float32),
        lax.psum_scatter(
            gain_grads.astype(jnp.bfloat16), "shard", scatter_dimension=1, tiled=True
        ).astype(jnp.float32),
    )
    (
        owned_query,
        owned_key,
        owned_value,
        owned_output,
        owned_gains,
        owned_gate,
        owned_up,
        owned_down,
    ) = (
        lax.psum(owned_query.astype(jnp.bfloat16), "dp").astype(jnp.float32),
        lax.psum(owned_key.astype(jnp.bfloat16), "dp").astype(jnp.float32),
        lax.psum(owned_value.astype(jnp.bfloat16), "dp").astype(jnp.float32),
        lax.psum(owned_output.astype(jnp.bfloat16), "dp").astype(jnp.float32),
        lax.psum(owned_gains.astype(jnp.bfloat16), "dp").astype(jnp.float32),
        lax.psum(owned_gate.astype(jnp.bfloat16), "dp").astype(jnp.float32),
        lax.psum(owned_up.astype(jnp.bfloat16), "dp").astype(jnp.float32),
        lax.psum(owned_down.astype(jnp.bfloat16), "dp").astype(jnp.float32),
    )
    return (
        output.astype(bf16),
        grad_tokens,
        root_means,
        owned_query,
        owned_key,
        owned_value,
        owned_output,
        owned_gains,
        owned_gate,
        owned_up,
        owned_down,
    )


def solution(mesh):
    placed = (
        P(("dp", "shard"), None),
        P(("dp", "shard"), None),
        P(("dp", "shard"), None),
        P(("dp", "shard"), None),
        P("dp"),
        P(None, "shard"),
        P(None, "shard"),
        P(None, "shard"),
        P(None, "shard"),
        P(None, "shard"),
        P(None, None, "shard"),
        P(None, None, "shard"),
        P(None, "shard", None),
    )
    return jax.shard_map(
        per_device,
        mesh=mesh,
        in_specs=placed,
        out_specs=(
            P(("dp", "shard"), None),
            P(("dp", "shard"), None),
            P(None, ("dp", "shard")),
            P(None, "shard"),
            P(None, "shard"),
            P(None, "shard"),
            P(None, "shard"),
            P(None, "shard"),
            P(None, None, "shard"),
            P(None, None, "shard"),
            P(None, "shard", None),
        ),
        check_vma=False,
    )
```

profile of v0, /device:TPU:12, one launch (start us, length us, event | category | flops | bytes accessed | tf_op | source)
XLA Modules:
  0.0 3736.8 jit_solution(17624853789911697138)
XLA Ops:
  9.5 13.4 all_gather.30
  24.2 133.5 %all-gather.10.cloned.1.call-done = bf16[2048,2048]{1,0:T(8,128)(2,1)} async-done(((bf16[2048,512]{1,0:T(8,128)(2,1)}), bf16[2048,2048]{1,0:T(8,128)(2,1)}) %all-gather.10.cloned.1.call-update) | async-done | bytes 8388624 | tf_op jit(solution)/shard_map/all_gather | solution.py:80
  168.6 138.5 %all-gather.14.cloned.1.call-done = bf16[2048,2048]{1,0:T(8,128)(2,1)} async-done(((bf16[2048,512]{1,0:T(8,128)(2,1)}), bf16[2048,2048]{1,0:T(8,128)(2,1)}) %all-gather.14.cloned.1.call-update) | async-done | bytes 8388624 | tf_op jit(solution)/shard_map/all_gather | solution.py:79
  323.3 133.1 %all-gather.16.cloned.1.call-done = bf16[2048,2048]{1,0:T(8,128)(2,1)} async-done(((bf16[2048,512]{1,0:T(8,128)(2,1)}), bf16[2048,2048]{1,0:T(8,128)(2,1)}) %all-gather.16.cloned.1.call-update) | async-done | bytes 8388624 | tf_op jit(solution)/shard_map/all_gather | solution.py:81
  487.8 49.5 %all-gather.12.cloned.1.call-done = bf16[1024,2048]{0,1:T(8,128)(2,1)} async-done(((bf16[256,2048]{0,1:T(8,128)(2,1)}), bf16[1024,2048]{0,1:T(8,128)(2,1)}) %all-gather.12.cloned.1.call-update) | async-done | bytes 4194320 | tf_op jit(solution)/shard_map/all_gather | solution.py:100
  549.3 69.2 %all-gather.18.cloned.1.call-done = bf16[1024,2048]{1,0:T(8,128)(2,1)} async-done(((bf16[256,2048]{1,0:T(8,128)(2,1)}), bf16[1024,2048]{1,0:T(8,128)(2,1)}) %all-gather.18.cloned.1.call-update) | async-done | bytes 4194320 | tf_op jit(solution)/shard_map/all_gather | solution.py:101
  636.6 131.3 %all-gather.20.cloned.1.call-done = bf16[2048,2048]{1,0:T(8,128)(2,1)} async-done(((bf16[2048,512]{1,0:T(8,128)(2,1)}), bf16[2048,2048]{1,0:T(8,128)(2,1)}) %all-gather.20.cloned.1.call-update) | async-done | bytes 8388624 | tf_op jit(solution)/shard_map/all_gather | solution.py:82
  784.8 269.2 %all-gather.22.cloned.1.call-done = bf16[4,2048,1024]{2,1,0:T(8,128)(2,1)} async-done(((bf16[4,2048,256]{2,1,0:T(8,128)(2,1)}), bf16[4,2048,1024]{2,1,0:T(8,128)(2,1)}) %all-gather.22.cloned.1.call-update) | async-done | bytes 16777232 | tf_op jit(solution)/shard_map/all_gather | solution.py:169
  1053.9 11.4 fusion.100
  1065.3 274.7 %all-gather.24.cloned.1.call-done = bf16[4,2048,1024]{2,1,0:T(8,128)(2,1)} async-done(((bf16[4,2048,256]{2,1,0:T(8,128)(2,1)}), bf16[4,2048,1024]{2,1,0:T(8,128)(2,1)}) %all-gather.24.cloned.1.call-update) | async-done | bytes 16777232 | tf_op jit(solution)/shard_map/all_gather | solution.py:170
  1340.0 11.4 fusion.101
  1351.4 275.2 %all-gather.26.cloned.1.call-done = bf16[4,1024,2048]{2,1,0:T(8,128)(2,1)} async-done(((bf16[4,256,2048]{2,1,0:T(8,128)(2,1)}), bf16[4,1024,2048]{2,1,0:T(8,128)(2,1)}) %all-gather.26.cloned.1.call-update) | async-done | bytes 16777232 | tf_op jit(solution)/shard_map/all_gather | solution.py:171
  1626.6 13.9 multiply_convert_fusion.1
  1640.5 14.9 fusion.102
  1655.5 12.3 convolution_add_fusion
  1673.6 11.5 convolution_multiply_fusion
  1690.9 16.2 scatter_custom_fusion.3
  1707.1 16.3 scatter_custom_fusion.2
  1742.7 33.5 while.41
  1787.0 100.3 %reduce-scatter.13.cloned.1.call-done = bf16[256,2048]{0,1:T(8,128)(2,1)} async-done(((bf16[1024,2048]{0,1:T(8,128)(2,1)}), bf16[256,2048]{0,1:T(8,128)(2,1)}) %reduce-scatter.13.cloned.1.call-update) | async-done | bytes 1048592 | tf_op jit(solution)/shard_map/reduce_scatter | solution.py:247
  1917.7 49.8 %reduce-scatter.15.cloned.1.call-done = bf16[256,2048]{0,1:T(8,128)(2,1)} async-done(((bf16[1024,2048]{0,1:T(8,128)(2,1)}), bf16[256,2048]{0,1:T(8,128)(2,1)}) %reduce-scatter.15.cloned.1.call-update) | async-done | bytes 1048592 | tf_op jit(solution)/shard_map/reduce_scatter | solution.py:253
  1997.5 10.9 convolution_convert_fusion
  2027.1 87.4 %reduce-scatter.23.cloned.1.call-done = bf16[2048,512]{1,0:T(8,128)(2,1)} async-done(((bf16[2048,2048]{1,0:T(8,128)(2,1)}), bf16[2048,512]{1,0:T(8,128)(2,1)}) %reduce-scatter.23.cloned.1.call-update) | async-done | bytes 2097168 | tf_op jit(solution)/shard_map/reduce_scatter | solution.py:292
  2114.4 148.2 %reduce-scatter.19.cloned.1.call-done = bf16[2048,512]{1,0:T(8,128)(2,1)} async-done(((bf16[2048,2048]{1,0:T(8,128)(2,1)}), bf16[2048,512]{1,0:T(8,128)(2,1)}) %reduce-scatter.19.cloned.1.call-update) | async-done | bytes 2097168 | tf_op jit(solution)/shard_map/reduce_scatter | solution.py:286
  2262.6 148.0 %reduce-scatter.17.cloned.1.call-done = bf16[2048,512]{1,0:T(8,128)(2,1)} async-done(((bf16[2048,2048]{1,0:T(8,128)(2,1)}), bf16[2048,512]{1,0:T(8,128)(2,1)}) %reduce-scatter.17.cloned.1.call-update) | async-done | bytes 2097168 | tf_op jit(solution)/shard_map/reduce_scatter | solution.py:283
  2410.6 148.0 %reduce-scatter.21.cloned.1.call-done = bf16[2048,512]{1,0:T(8,128)(2,1)} async-done(((bf16[2048,2048]{1,0:T(8,128)(2,1)}), bf16[2048,512]{1,0:T(8,128)(2,1)}) %reduce-scatter.21.cloned.1.call-update) | async-done | bytes 2097168 | tf_op jit(solution)/shard_map/reduce_scatter | solution.py:289
  2558.6 280.8 %reduce-scatter.25.cloned.1.call-done = bf16[4,2048,256]{2,1,0:T(8,128)(2,1)} async-done(((bf16[4,2048,1024]{2,1,0:T(8,128)(2,1)}), bf16[4,2048,256]{2,1,0:T(8,128)(2,1)}) %reduce-scatter.25.cloned.1.call-update) | async-done | bytes 4194320 | tf_op jit(solution)/shard_map/reduce_scatter | solution.py:199
  2839.4 283.4 %reduce-scatter.27.cloned.1.call-done = bf16[4,2048,256]{2,1,0:T(8,128)(2,1)} async-done(((bf16[4,2048,1024]{2,1,0:T(8,128)(2,1)}), bf16[4,2048,256]{2,1,0:T(8,128)(2,1)}) %reduce-scatter.27.cloned.1.call-update) | async-done | bytes 4194320 | tf_op jit(solution)/shard_map/reduce_scatter | solution.py:202
  3122.8 283.3 %reduce-scatter.29.cloned.1.call-done = bf16[4,256,2048]{2,1,0:T(8,128)(2,1)} async-done(((bf16[4,1024,2048]{2,1,0:T(8,128)(2,1)}), bf16[4,256,2048]{2,1,0:T(8,128)(2,1)}) %reduce-scatter.29.cloned.1.call-update) | async-done | bytes 4194320 | tf_op jit(solution)/shard_map/reduce_scatter | solution.py:205
  3411.1 20.0 reduce-scatter.31.cloned.1.call-done
  3432.1 11.9 psum.60
  3444.6 259.6 %all-reduce.3.cloned.1.call-done = (bf16[2048,512]{1,0:T(8,128)(2,1)}, bf16[2048,512]{1,0:T(8,128)(2,1)}, bf16[2048,512]{1,0:T(8,128)(2,1)}, bf16[2048,512]{1,0:...) async-done(((bf16[2048,512]{1,0:T(8,128)(2,1)}, bf16[2048,512]{1,0:T(8,128)(2,1)}, ...) | async-done | bytes 20971536 | tf_op jit(solution)/shard_map/psum | solution.py:309
  (323 shorter events, 308.0 us)
Async XLA Ops:
  7.2 150.5 %all-gather.10.cloned.1.call-start = ((), (), s32[]{:S(2)}) async-start(), calls=%async_computation.10 | async-start | bytes 10485760 | tf_op jit(solution)/shard_map/all_gather | solution.py:80
  7.9 299.1 %all-gather.14.cloned.1.call-start = ((), (), s32[]{:S(2)}) async-start(), calls=%async_computation.12 | async-start | bytes 10485760 | tf_op jit(solution)/shard_map/all_gather | solution.py:79
  8.7 447.8 %all-gather.16.cloned.1.call-start = ((), (), s32[]{:S(2)}) async-start(), calls=%async_computation.13 | async-start | bytes 10485760 | tf_op jit(solution)/shard_map/all_gather | solution.py:81
  9.4 527.8 %all-gather.12.cloned.1.call-start = ((), (), s32[]{:S(2)}) async-start(), calls=%async_computation.11 | async-start | bytes 5242880 | tf_op jit(solution)/shard_map/all_gather | solution.py:100
  23.2 433.3 %copy-start.57 = (f32[256]{0:T(256)}, f32[256]{0:T(256)S(1)}, u32[]{:S(2)}) copy-start(f32[256]{0:T(256)S(1)} %add_rsqrt_fusion.3) | copy-start | bytes 3076
  24.1 294.8 %copy-start.48 = (f32[256,64]{0,1:T(8,128)}, f32[256,64]{0,1:T(8,128)S(1)}, u32[]{:S(2)}) copy-start(f32[256,64]{0,1:T(8,128)S(1)} %get-tuple-element.439) | copy-start | bytes 196612
  24.1 139.4 %copy-start.55 = (f32[1,2048]{1,0:T(1,128)}, f32[1,2048]{1,0:T(1,128)S(1)}, u32[]{:S(2)}) copy-start(f32[1,2048]{1,0:T(1,128)S(1)} %get-tuple-element.435) | copy-start | bytes 24580
  24.1 288.8 %copy-start.53 = (f32[1,2048]{1,0:T(1,128)}, f32[1,2048]{1,0:T(1,128)S(1)}, u32[]{:S(2)}) copy-start(f32[1,2048]{1,0:T(1,128)S(1)} %get-tuple-element.434) | copy-start | bytes 24580
  24.1 432.3 %copy-start.46 = (f32[1,2048]{1,0:T(1,128)}, f32[1,2048]{1,0:T(1,128)S(1)}, u32[]{:S(2)}) copy-start(f32[1,2048]{1,0:T(1,128)S(1)} %get-tuple-element.436) | copy-start | bytes 24580
  323.3 295.3 %all-gather.18.cloned.1.call-start = ((), (), s32[]{:S(2)}) async-start(), calls=%async_computation.14 | async-start | bytes 5242880 | tf_op jit(solution)/shard_map/all_gather | solution.py:101
  463.3 304.6 %all-gather.20.cloned.1.call-start = ((), (), s32[]{:S(2)}) async-start(), calls=%async_computation.15 | async-start | bytes 10485760 | tf_op jit(solution)/shard_map/all_gather | solution.py:82
  463.8 590.1 %all-gather.22.cloned.1.call-start = ((), (), s32[]{:S(2)}) async-start(), calls=%async_computation.16 | async-start | bytes 20971520 | tf_op jit(solution)/shard_map/all_gather | solution.py:169
  464.6 875.4 %all-gather.24.cloned.1.call-start = ((), (), s32[]{:S(2)}) async-start(), calls=%async_computation.17 | async-start | bytes 20971520 | tf_op jit(solution)/shard_map/all_gather | solution.py:170
  465.3 1161.2 %all-gather.26.cloned.1.call-start = ((), (), s32[]{:S(2)}) async-start(), calls=%async_computation.18 | async-start | bytes 20971520 | tf_op jit(solution)/shard_map/all_gather | solution.py:171
  466.1 1421.2 %reduce-scatter.13.cloned.1.call-start = ((), (), s32[]{:S(2)}) async-start(), calls=%async_computation.19 | async-start | bytes 5242880 | tf_op jit(solution)/shard_map/reduce_scatter | solution.py:247
  487.0 1186.7 %copy-start.50 = (f32[4,170]{1,0:T(4,128)}, f32[4,170]{1,0:T(4,128)S(1)}, u32[]{:S(2)}) copy-start(f32[4,170]{1,0:T(4,128)S(1)} %mul.491) | copy-start | bytes 8164
  636.6 137.9 %copy-start.23 = (bf16[16,256,128]{1,2,0:T(8,128)(2,1)}, bf16[16,256,128]{1,2,0:T(8,128)(2,1)S(1)}, u32[]{:S(2)}) copy-start(bf16[16,256,128]{1,2,0:T(8,128)(2,1)S(1)} %copy.70) | copy-start | bytes 3145732
  1640.5 15.0 copy-start.26
  1690.9 32.5 copy-start.11
  1776.3 191.3 %reduce-scatter.15.cloned.1.call-start = ((), (), s32[]{:S(2)}) async-start(), calls=%async_computation.20 | async-start | bytes 5242880 | tf_op jit(solution)/shard_map/reduce_scatter | solution.py:253
  1777.0 337.4 %reduce-scatter.23.cloned.1.call-start = ((), (), s32[]{:S(2)}) async-start(), calls=%async_computation.24 | async-start | bytes 10485760 | tf_op jit(solution)/shard_map/reduce_scatter | solution.py:292
  1783.9 478.7 %reduce-scatter.19.cloned.1.call-start = ((), (), s32[]{:S(2)}) async-start(), calls=%async_computation.22 | async-start | bytes 10485760 | tf_op jit(solution)/shard_map/reduce_scatter | solution.py:286
  1787.0 101.7 %copy-start.25 = (f32[256,16,128]{0,2,1:T(8,128)S(1)}, f32[256,16,128]{0,2,1:T(8,128)}, u32[]{:S(2)}) copy-start(f32[256,16,128]{0,2,1:T(8,128)} %broadcast_multiply_fusion) | copy-start | bytes 6291460
  1787.0 101.7 %copy-start.49 = (f32[256,64]{0,1:T(8,128)S(1)}, f32[256,64]{0,1:T(8,128)}, u32[]{:S(2)}) copy-start(f32[256,64]{0,1:T(8,128)} %copy-done.48) | copy-start | bytes 196612
  1787.0 101.7 %copy-start.52 = (f32[256,64]{0,1:T(8,128)S(1)}, f32[256,64]{0,1:T(8,128)}, u32[]{:S(2)}) copy-start(f32[256,64]{0,1:T(8,128)} %get-tuple-element.437) | copy-start | bytes 196612
  1904.7 505.9 %reduce-scatter.17.cloned.1.call-start = ((), (), s32[]{:S(2)}) async-start(), calls=%async_computation.21 | async-start | bytes 10485760 | tf_op jit(solution)/shard_map/reduce_scatter | solution.py:283
  1917.5 641.1 %reduce-scatter.21.cloned.1.call-start = ((), (), s32[]{:S(2)}) async-start(), calls=%async_computation.23 | async-start | bytes 10485760 | tf_op jit(solution)/shard_map/reduce_scatter | solution.py:289
  1974.7 864.7 %reduce-scatter.25.cloned.1.call-start = ((), (), s32[]{:S(2)}) async-start(), calls=%async_computation.25 | async-start | bytes 20971520 | tf_op jit(solution)/shard_map/reduce_scatter | solution.py:199
  1986.4 1136.4 %reduce-scatter.27.cloned.1.call-start = ((), (), s32[]{:S(2)}) async-start(), calls=%async_computation.26 | async-start | bytes 20971520 | tf_op jit(solution)/shard_map/reduce_scatter | solution.py:202
  1996.1 1410.0 %reduce-scatter.29.cloned.1.call-start = ((), (), s32[]{:S(2)}) async-start(), calls=%async_computation.27 | async-start | bytes 20971520 | tf_op jit(solution)/shard_map/reduce_scatter | solution.py:205
  2008.4 1422.7 %reduce-scatter.31.cloned.1.call-start = ((), (), s32[]{:S(2)}) async-start(), calls=%async_computation.28 | async-start | bytes 655360
  2027.0 1677.2 %all-reduce.3.cloned.1.call-start = ((), (), s32[]{:S(2)}) async-start(), calls=%async_computation.29 | async-start | bytes 41943040 | tf_op jit(solution)/shard_map/psum | solution.py:309
  (60 other events, 211.6 us)
Sparse Core Ops, SparseCore 0:
  9.6 148.0 all-gather.9
  159.2 147.7 all-gather.13
  308.6 147.8 all-gather.15
  458.5 78.7 all-gather.11
  539.2 79.2 all-gather.17
  620.0 147.8 all-gather.19
  769.4 284.4 all-gather.21
  1055.5 284.4 all-gather.23
  1341.6 284.9 all-gather.25
  1776.4 110.8 reduce-scatter.12
  1890.2 77.2 reduce-scatter.14
  1969.7 144.6 reduce-scatter.22
  2117.4 145.1 reduce-scatter.18
  2265.4 145.1 reduce-scatter.16
  2413.4 145.1 reduce-scatter.20
  2560.8 278.5 reduce-scatter.24
  2841.7 281.0 reduce-scatter.26
  3125.0 281.0 reduce-scatter.28
  3409.0 22.0 reduce-scatter.30
  3436.9 267.2 all-reduce.2
where the time goes:
time: 3750 us; the launch traced here: 3740 us
  waiting for transfers between devices  3290 us (88%)
  matrix products  207 us (6%)
  local copies, waits for them, and re-layouts  101 us (3%)
  other arithmetic  96.8 us (3%)
    reduce_scatter x1, waiting for transfers between devices, per_device(): lax.psum_scatter(grad_up_part.astype(jnp.bfloat16), 'shard', scatter_dime...  283 us
    reduce_scatter x1, waiting for transfers between devices, per_device(): lax.psum_scatter(grad_down_part.astype(jnp.bfloat16), 'shard', scatter_di...  283 us
    reduce_scatter x1, waiting for transfers between devices, per_device(): lax.psum_scatter(grad_gate_part.astype(jnp.bfloat16), 'shard', scatter_di...  281 us
    all_gather x1, waiting for transfers between devices, per_device(): lax.all_gather(expert_down, 'shard', axis=1, tiled=True)  275 us
    all_gather x1, waiting for transfers between devices, per_device(): lax.all_gather(expert_up, 'shard', axis=2, tiled=True)  275 us
    all_gather x1, waiting for transfers between devices, per_device(): lax.all_gather(expert_gate, 'shard', axis=2, tiled=True)  269 us
    psum x1, waiting for transfers between devices, per_device(): lax.psum(owned_query.astype(jnp.bfloat16), 'dp').astype(jnp.float32)  260 us
    reduce_scatter x1, waiting for transfers between devices, per_device(): lax.psum_scatter(grad_key_full.astype(jnp.bfloat16), 'shard', scatter_dim...  148 us
  transfers between devices with their start and end apart: 20, of which 20 were waited for; matrix products, arithmetic and copies ran while one was open for 6% of the time, Pallas kernels for 0%

commit v1 on v0

v1 whole, which is shorter than its diff:
```python
import jax
import jax.numpy as jnp
from jax import lax
from jax.sharding import PartitionSpec as P

HEAD_DIM = 128
EPSILON = 1e-05
ROPE_BASE = 10000.0
MASKED = -1e30

f32 = jnp.float32
bf16 = jnp.bfloat16


def rotary_tables(row_count):
    half_dim = HEAD_DIM // 2
    positions = jnp.arange(row_count, dtype=jnp.int32)
    inverse = ROPE_BASE ** (-jnp.arange(half_dim, dtype=f32) / half_dim)
    angles = positions.astype(f32)[:, None] * inverse[None, :]
    return (jnp.cos(angles), jnp.sin(angles))


def rotate(values, cosine, sine):
    row_count = values.shape[0]
    half_dim = cosine.shape[1]
    halves = values.reshape(row_count, -1, 2, half_dim)
    leading = halves[:, :, 0, :]
    trailing = halves[:, :, 1, :]
    cos_wide = cosine[:, None, :]
    sin_wide = sine[:, None, :]
    turned = jnp.stack(
        [leading * cos_wide - trailing * sin_wide, trailing * cos_wide + leading * sin_wide], axis=2
    )
    return turned.reshape(row_count, -1)


def row_factor(values):
    return lax.rsqrt(jnp.mean(values * values, axis=-1, keepdims=True) + EPSILON)


def norm_back(grad_unit, unit_rows, factor):
    return factor * (
        grad_unit - unit_rows * jnp.mean(grad_unit * unit_rows, axis=-1, keepdims=True)
    )


def root_mean(values):
    return jnp.sqrt(jnp.mean(values * values, axis=-1))


def dot(a, b):
    return jnp.dot(a, b, preferred_element_type=f32)


def dot_nt(a, b):
    return lax.dot_general(a, b, (((1,), (1,)), ((), ())), preferred_element_type=f32)


def dot_tn(a, b):
    return lax.dot_general(a, b, (((0,), (0,)), ((), ())), preferred_element_type=f32)


def per_device(
    tokens,
    out_grad,
    routes,
    gate_weights,
    prefix,
    query_weight,
    key_weight,
    value_weight,
    output_weight,
    norm_gains,
    expert_gate,
    expert_up,
    expert_down,
):
    rows, width = tokens.shape
    shards = lax.axis_size("shard")
    groups = lax.axis_size("dp")
    place = lax.axis_index("shard")
    group = lax.axis_index("dp")
    length = rows * shards
    local = width // shards
    heads = local // HEAD_DIM
    experts = expert_gate.shape[0]
    units = expert_gate.shape[2]
    scale = HEAD_DIM ** (-0.5)

    expert_ids = jnp.arange(experts, dtype=jnp.int32)
    weight_own = jnp.sum(
        jnp.where(routes[:, :, None] == expert_ids[None, None, :], gate_weights[:, :, None], 0.0),
        axis=1,
    )
    small = jnp.concatenate(
        [weight_own.reshape(-1), norm_gains[0].astype(f32), norm_gains[3].astype(f32)]
    )
    small_all = lax.all_gather(small, "shard", axis=0)
    combine = small_all[:, : rows * experts].reshape(length, experts)
    gain_in = small_all[:, rows * experts : rows * experts + local].reshape(width)
    gain_expert = small_all[:, rows * experts + local :].reshape(width)
    gain_query = norm_gains[1].astype(f32)
    gain_key = norm_gains[2].astype(f32)

    x_all_b = lax.all_gather(tokens, "shard", axis=0, tiled=True)
    slab = width // groups
    out_slab = lax.dynamic_slice_in_dim(output_weight, group * slab, slab, 0)
    out_slab = lax.all_gather(out_slab, "shard", axis=1, tiled=True)
    full_output = lax.all_gather(out_slab, "dp", axis=0, tiled=True)

    x_all = x_all_b.astype(f32)
    normed = (x_all * row_factor(x_all) * gain_in).astype(bf16)
    query_raw = dot(normed, query_weight)
    key_raw = dot(normed, key_weight)
    values = dot(normed, value_weight).astype(bf16)
    squares = jnp.stack([jnp.sum(query_raw * query_raw, -1), jnp.sum(key_raw * key_raw, -1)])
    squares = lax.psum(squares, "shard")
    factors = lax.rsqrt(squares / width + EPSILON)
    factor_query = factors[0][:, None]
    factor_key = factors[1][:, None]
    unit_query = query_raw * factor_query
    unit_key = key_raw * factor_key
    cosine, sine = rotary_tables(length)
    queries = rotate(unit_query * gain_query, cosine, sine).astype(bf16)
    keys = rotate(unit_key * gain_key, cosine, sine).astype(bf16)

    def split(v):
        return v.reshape(length, heads, HEAD_DIM).transpose(1, 0, 2)

    query_heads, key_heads, value_heads = split(queries), split(keys), split(values)
    positions = jnp.arange(length, dtype=jnp.int32)
    visible = (positions[None, :] <= positions[:, None]) | (positions[None, :] < prefix[0])
    scores = jnp.einsum("hqd,hkd->hqk", query_heads, key_heads, preferred_element_type=f32) * scale
    scores = jnp.where(visible[None], scores, MASKED)
    top = jnp.max(scores, axis=-1, keepdims=True)
    expd = jnp.exp(scores - top)
    total = jnp.sum(expd, axis=-1, keepdims=True)
    probs = expd / total
    mixed = jnp.einsum(
        "hqk,hkd->hqd", probs.astype(bf16), value_heads, preferred_element_type=f32
    )
    mixed_own = mixed.transpose(1, 0, 2).reshape(length, local).astype(bf16)
    mixed_all = lax.all_gather(mixed_own, "shard", axis=1, tiled=True)

    attended = dot(mixed_all, full_output)
    residual = x_all + attended
    factor_res = row_factor(residual)
    expert_in = (residual * factor_res * gain_expert).astype(bf16)

    g_all = lax.all_gather(out_grad, "shard", axis=0, tiled=True)
    gate_flat = expert_gate.transpose(1, 0, 2).reshape(width, experts * units)
    up_flat = expert_up.transpose(1, 0, 2).reshape(width, experts * units)
    down_flat = expert_down.reshape(experts * units, width)
    gate_part = dot(expert_in, gate_flat)
    up_part = dot(expert_in, up_flat)
    sig = jax.nn.sigmoid(gate_part)
    wide = jnp.repeat(combine, units, axis=1)
    hidden = (gate_part * sig * up_part * wide).astype(bf16)
    sum_part = dot(hidden, down_flat)
    expert_sum = lax.psum_scatter(
        sum_part.astype(bf16), "shard", scatter_dimension=0, tiled=True
    ).astype(f32)

    hidden_grad = dot_nt(g_all, down_flat) * wide
    up_grad = (hidden_grad * gate_part * sig).astype(bf16)
    gate_grad = (hidden_grad * up_part * sig * (1.0 + gate_part * (1.0 - sig))).astype(bf16)
    in_part = dot_nt(gate_grad, gate_flat) + dot_nt(up_grad, up_flat)
    in_grad = lax.psum_scatter(
        in_part.astype(bf16), "shard", scatter_dimension=0, tiled=True
    ).astype(f32)
    grad_down = dot_tn(hidden, g_all).reshape(experts, units, width)
    grad_gate = dot_tn(expert_in, gate_grad).reshape(width, experts, units).transpose(1, 0, 2)
    grad_up = dot_tn(expert_in, up_grad).reshape(width, experts, units).transpose(1, 0, 2)

    def own_rows(v):
        return lax.dynamic_slice_in_dim(v, place * rows, rows, 0)

    x_own = tokens.astype(f32)
    g_own = out_grad.astype(f32)
    attended_own = own_rows(attended)
    residual_own = x_own + attended_own
    output = residual_own + expert_sum
    root_means = jnp.stack([root_mean(attended_own), root_mean(expert_sum), root_mean(output)])
    factor_own = own_rows(factor_res)
    unit_res = residual_own * factor_own
    gain_grad_res = jnp.sum(in_grad * unit_res, axis=0)
    residual_grad = g_own + norm_back(in_grad * gain_expert, unit_res, factor_own)
    attended_grad = lax.all_gather(residual_grad.astype(bf16), "shard", axis=0, tiled=True)

    grad_output = dot_tn(
        mixed_all, lax.dynamic_slice_in_dim(attended_grad, place * local, local, 1)
    )
    mixed_grad = dot_nt(
        attended_grad, lax.dynamic_slice_in_dim(full_output, place * local, local, 0)
    ).astype(bf16)
    grad_heads = split(mixed_grad)
    delta = jnp.sum(grad_heads.astype(f32) * mixed, axis=-1, keepdims=True)
    prob_grad = jnp.einsum("hqd,hkd->hqk", grad_heads, value_heads, preferred_element_type=f32)
    score_grad = (probs * (prob_grad - delta)).astype(bf16)
    query_acc = jnp.einsum("hqk,hkd->hqd", score_grad, key_heads, preferred_element_type=f32)
    key_acc = jnp.einsum("hqk,hqd->hkd", score_grad, query_heads, preferred_element_type=f32)
    value_acc = jnp.einsum(
        "hqk,hqd->hkd", probs.astype(bf16), grad_heads, preferred_element_type=f32
    )

    def merge(v):
        return v.transpose(1, 0, 2).reshape(length, local)

    query_norm_grad = rotate(merge(query_acc) * scale, cosine, -sine)
    key_norm_grad = rotate(merge(key_acc) * scale, cosine, -sine)
    value_raw_grad = merge(value_acc).astype(bf16)
    gain_grad_query = jnp.sum(query_norm_grad * unit_query, axis=0)
    gain_grad_key = jnp.sum(key_norm_grad * unit_key, axis=0)
    query_norm_grad = query_norm_grad * gain_query
    key_norm_grad = key_norm_grad * gain_key
    inner = jnp.stack(
        [jnp.sum(query_norm_grad * unit_query, -1), jnp.sum(key_norm_grad * unit_key, -1)]
    )
    inner = lax.psum(inner, "shard") / width
    query_raw_grad = (factor_query * (query_norm_grad - unit_query * inner[0][:, None])).astype(
        bf16
    )
    key_raw_grad = (factor_key * (key_norm_grad - unit_key * inner[1][:, None])).astype(bf16)
    normed_part = (
        dot_nt(query_raw_grad, query_weight)
        + dot_nt(key_raw_grad, key_weight)
        + dot_nt(value_raw_grad, value_weight)
    )
    normed_grad = lax.psum_scatter(
        normed_part.astype(bf16), "shard", scatter_dimension=0, tiled=True
    ).astype(f32)
    grad_query = dot_tn(normed, query_raw_grad)
    grad_key = dot_tn(normed, key_raw_grad)
    grad_value = dot_tn(normed, value_raw_grad)

    factor_x = row_factor(x_own)
    unit_x = x_own * factor_x
    gain_grad_x = jnp.sum(normed_grad * unit_x, axis=0)
    grad_tokens = residual_grad + norm_back(normed_grad * gain_in, unit_x, factor_x)

    gain_rows = lax.psum_scatter(
        jnp.stack([gain_grad_x, gain_grad_res]), "shard", scatter_dimension=1, tiled=True
    )
    grad_gains = jnp.stack([gain_rows[0], gain_grad_query, gain_grad_key, gain_rows[1]])

    def over_groups(v):
        return lax.psum(v.astype(bf16), "dp").astype(f32)

    return (
        output.astype(bf16),
        grad_tokens,
        root_means,
        over_groups(grad_query),
        over_groups(grad_key),
        over_groups(grad_value),
        over_groups(grad_output),
        lax.psum(grad_gains, "dp"),
        over_groups(grad_gate),
        over_groups(grad_up),
        over_groups(grad_down),
    )


def solution(mesh):
    placed = (
        P(("dp", "shard"), None),
        P(("dp", "shard"), None),
        P(("dp", "shard"), None),
        P(("dp", "shard"), None),
        P("dp"),
        P(None, "shard"),
        P(None, "shard"),
        P(None, "shard"),
        P(None, "shard"),
        P(None, "shard"),
        P(None, None, "shard"),
        P(None, None, "shard"),
        P(None, "shard", None),
    )
    return jax.shard_map(
        per_device,
        mesh=mesh,
        in_specs=placed,
        out_specs=(
            P(("dp", "shard"), None),
            P(("dp", "shard"), None),
            P(None, ("dp", "shard")),
            P(None, "shard"),
            P(None, "shard"),
            P(None, "shard"),
            P(None, "shard"),
            P(None, "shard"),
            P(None, None, "shard"),
            P(None, None, "shard"),
            P(None, "shard", None),
        ),
        check_vma=False,
    )
```

time: 3750 us -> 1120 us (0.30)
  waiting for transfers between devices: 3290 us -> 734 us
  local copies, waits for them, and re-layouts: 101 us -> 53.9 us
    reduce_scatter x9 -> x3, waiting for transfers between devices: 1530 us -> 166 us  [the longest x1 80.3 us: per_device(): lax.psum_scatter(in_part.astype(bf16), 'shard', scatter_dimension=0, tile...]
    all_gather x9 -> x6, waiting for transfers between devices: 1470 us -> 295 us  [the longest x1 76.5 us: per_device(): lax.all_gather(residual_grad.astype(bf16), 'shard', axis=0, tiled=True)]
    dot_general x28 -> x26, matrix products: 207 us -> 175 us  [the longest x7 51.3 us: dot(): return jnp.dot(a, b, preferred_element_type=f32)]
  transfers between devices with their start and end apart: 20 -> 11, of which waited for: 20 -> 10; matrix products, arithmetic and copies ran while one was open for 6% -> 15% of each run, Pallas kernels for 0% -> 0%
where the time goes in v1:
time: 1120 us; the launch traced here: 1110 us
  waiting for transfers between devices  734 us (66%)
  matrix products  186 us (17%)
  other arithmetic  65.4 us (6%)
  local copies, waits for them, and re-layouts  53.9 us (5%)
  blocking collectives  51.1 us (5%)
  between operations  15.8 us (1%)
    psum x1, waiting for transfers between devices, over_groups(): return lax.psum(v.astype(bf16), 'dp').astype(f32)  258 us
    reduce_scatter x1, waiting for transfers between devices, per_device(): lax.psum_scatter(in_part.astype(bf16), 'shard', scatter_dimension=0, tile...  80.3 us
    all_gather x1, waiting for transfers between devices, per_device(): lax.all_gather(residual_grad.astype(bf16), 'shard', axis=0, tiled=True)  76.5 us
    all_gather x1, waiting for transfers between devices, per_device(): mixed_all = lax.all_gather(mixed_own, 'shard', axis=1, tiled=True)  70.1 us
    reduce_scatter x1, waiting for transfers between devices, per_device(): lax.psum_scatter(sum_part.astype(bf16), 'shard', scatter_dimension=0, til...  63.9 us
    all_gather x1, waiting for transfers between devices, per_device(): x_all_b = lax.all_gather(tokens, 'shard', axis=0, tiled=True)  59.5 us
    all_gather x1, waiting for transfers between devices, per_device(): full_output = lax.all_gather(out_slab, 'dp', axis=0, tiled=True)  56.8 us
    dot_general x7, matrix products, dot(): return jnp.dot(a, b, preferred_element_type=f32)  51.3 us
  transfers between devices with their start and end apart: 11, of which 10 were waited for; matrix products, arithmetic and copies ran while one was open for 15% of the time, Pallas kernels for 0%

profile of v1, /device:TPU:12, one launch (start us, length us, event | category | flops | bytes accessed | tf_op | source)
XLA Modules:
  0.0 1107.1 jit_solution(11407337733355831335)
XLA Ops:
  13.0 13.7 %all-gather = f32[8192]{0:T(1024)S(1)} all-gather(f32[2048]{0:T(1024)S(1)} %pad_maximum_fusion.5), channel_id=2, replica_groups=mesh['dp'=8,'shard'=4] {'shard'}, dimensions={0}, use_global_device_ids=true | all-gather | bytes 40960 | tf_op jit(solution)/shard_map/all_gather | solution.py:98
  29.8 59.5 %all-gather.8.cloned.1.call-done = bf16[1024,2048]{1,0:T(8,128)(2,1)} async-done(((bf16[256,2048]{1,0:T(8,128)(2,1)}), bf16[1024,2048]{1,0:T(8,128)(2,1)}) %all-gather.8.cloned.1.call-update) | async-done | bytes 4194320 | tf_op jit(solution)/shard_map/all_gather | solution.py:105
  100.6 11.9 %psum.70 = f32[2,1024]{1,0:T(2,128)S(1)} all-reduce(f32[2,1024]{1,0:T(2,128)S(1)} %pad_maximum_fusion.6), channel_id=1, replica_groups=mesh['dp'=8,'shard'=4] {'shard'}, use_global_device_ids=true, to_apply=%region_4.5 | all-reduce | flops 2048 | bytes 16384 | tf_op jit(solution)/shard_map/psum | solution.py:117
  120.6 6.3 convolution_convert_fusion.9
  126.9 11.3 %fusion.66 = (f32[4,1024]{1,0:T(4,128)S(1)}, f32[4,1024,1024]{1,2,0:T(8,128)}) fusion(pred[1024,1024]{0,1:T(8,128)(4,1)} %fusion.9, bf16[1024,4,128]{2,0,1:T(8,128)(2,1)} %copy.78, bf16[1024,4,128]{2,0,1:T(8,128)(2,1)} %copy.77), kind=kOutput, calls=%fused_computation.145 | convolution fusion | flops 1090520064 | bytes 19939328 | tf_op jit(solution)/shard_map/sub | solution.py:136
  138.2 7.1 fusion.8
  155.5 6.2 copy.82
  161.7 6.2 copy.83
  167.9 32.4 %all-gather.16.cloned.1.call-done = bf16[1024,2048]{1,0:T(8,128)(2,1)} async-done(((bf16[256,2048]{1,0:T(8,128)(2,1)}), bf16[1024,2048]{1,0:T(8,128)(2,1)}) %all-gather.16.cloned.1.call-update) | async-done | bytes 4194320 | tf_op jit(solution)/shard_map/all_gather | solution.py:150
  200.3 11.2 %convolution_multiply_fusion = f32[1024,1024]{1,0:T(8,128)} fusion(f32[1024,1024]{1,0:T(8,128)} %bitcast.174, bf16[1024,2048]{1,0:T(8,128)(2,1)} %all-gather.16.cloned.1.call-done, bf16[1024,2048]{1,0:T(8,128)(2,1)} %bitcast.224), kind=kOutput, calls=%fused_computation.48 | convolution fusion | flops 4296015872 | bytes 16777216 | tf_op jit(solution)/shard_map/dot_general | solution.py:56
  211.5 70.1 %all-gather.10.cloned.1.call-done = bf16[1024,2048]{0,1:T(8,128)(2,1)} async-done(((bf16[1024,512]{0,1:T(8,128)(2,1)}), bf16[1024,2048]{0,1:T(8,128)(2,1)}) %all-gather.10.cloned.1.call-update) | async-done | bytes 4194320 | tf_op jit(solution)/shard_map/all_gather | solution.py:143
  281.6 56.8 %all-gather.14.cloned.1.call-done = bf16[2048,2048]{1,0:T(8,128)(2,1)} async-done(((bf16[256,2048]{1,0:T(8,128)(2,1)}), bf16[2048,2048]{1,0:T(8,128)(2,1)}) %all-gather.14.cloned.1.call-update) | async-done | bytes 8388624 | tf_op jit(solution)/shard_map/all_gather | solution.py:109
  338.4 14.4 %multiply_reduce_fusion = (f32[1024]{0:T(1024)S(1)}, f32[1024,2048]{1,0:T(8,128)S(1)}) fusion(bf16[1024,2048]{1,0:T(8,128)(2,1)} %all-gather.8.cloned.1.call-done, bf16[1024,2048]{0,1:T(8,128)(2,1)} %all-gather.10.cloned.1.call-done, bf16[2048,2048]{1,0:T(8,128)(2,1)} %all-gather.14.cloned.1.call-done), kind=kOutput, calls=%fused_computation.14 | convolution fusion | flops 8598322176 | bytes 25169920 | tf_op jit(solution)/shard_map/dot_general | solution.py:52
  358.2 6.2 fusion.76
  364.4 10.4 multiply_convert_fusion.4
  382.3 7.1 fusion.77
  395.5 63.9 %reduce-scatter.7.cloned.1.call-done = bf16[256,2048]{1,0:T(8,128)(2,1)} async-done(((bf16[1024,2048]{1,0:T(8,128)(2,1)}), bf16[256,2048]{1,0:T(8,128)(2,1)}) %reduce-scatter.7.cloned.1.call-update) | async-done | bytes 1048592 | tf_op jit(solution)/shard_map/reduce_scatter | solution.py:160
  459.5 80.3 %reduce-scatter.9.cloned.1.call-done = bf16[256,2048]{1,0:T(8,128)(2,1)} async-done(((bf16[1024,2048]{1,0:T(8,128)(2,1)}), bf16[256,2048]{1,0:T(8,128)(2,1)}) %reduce-scatter.9.cloned.1.call-update) | async-done | bytes 1048592 | tf_op jit(solution)/shard_map/reduce_scatter | solution.py:168
  549.2 76.5 %all-gather.18.cloned.1.call-done = bf16[1024,2048]{1,0:T(8,128)(2,1)} async-done(((bf16[256,2048]{1,0:T(8,128)(2,1)}), bf16[1024,2048]{1,0:T(8,128)(2,1)}) %all-gather.18.cloned.1.call-update) | async-done | bytes 4194320 | tf_op jit(solution)/shard_map/all_gather | solution.py:188
  631.5 7.4 convolution_convert_fusion.8
  638.8 9.4 multiply_convert_fusion
  648.2 7.8 convolution_multiply_fusion.2
  663.7 11.8 %psum.71 = f32[2,1024]{1,0:T(2,128)S(1)} all-reduce(f32[2,1024]{1,0:T(2,128)S(1)} %pad_maximum_fusion.7), channel_id=1, replica_groups=mesh['dp'=8,'shard'=4] {'shard'}, use_global_device_ids=true, to_apply=%region_15.16 | all-reduce | flops 2048 | bytes 16384 | tf_op jit(solution)/shard_map/psum | solution.py:219
  687.8 8.0 add_convert_fusion
  696.1 9.4 convolution_convert_fusion.1
  711.7 9.4 convolution_convert_fusion.2
  721.1 6.4 copy.91
  727.6 9.6 convolution_convert_fusion
  750.5 21.4 %reduce-scatter.11.cloned.1.call-done = bf16[256,2048]{1,0:T(8,128)(2,1)} async-done(((bf16[1024,2048]{1,0:T(8,128)(2,1)}), bf16[256,2048]{1,0:T(8,128)(2,1)}) %reduce-scatter.11.cloned.1.call-update) | async-done | bytes 1048592 | tf_op jit(solution)/shard_map/reduce_scatter | solution.py:229
  788.1 13.1 %reduce-scatter.13.cloned.1.call-done = f32[512,2]{1,0:T(8,128)} async-done(((f32[2048,2]{1,0:T(8,128)}), f32[512,2]{1,0:T(8,128)}) %reduce-scatter.13.cloned.1.call-update) | async-done | bytes 4112
  802.7 13.7 %psum.76 = f32[4,512]{1,0:T(4,128)} all-reduce(f32[4,512]{1,0:T(4,128)S(1)} %pad_maximum_fusion.8), channel_id=1, replica_groups=mesh['dp'=8,'shard'=4] {'dp'}, use_global_device_ids=true, to_apply=%region_30.31 | all-reduce | flops 2048 | bytes 16384 | tf_op jit(solution)/shard_map/psum | solution.py:257
  816.4 257.8 %all-reduce.3.cloned.1.call-done = (bf16[2048,512]{1,0:T(8,128)(2,1)}, bf16[2048,512]{1,0:T(8,128)(2,1)}, bf16[2048,512]{1,0:T(8,128)(2,1)}, bf16[2048,512]{1,0:...) async-done(((bf16[2048,512]{1,0:T(8,128)(2,1)}, bf16[2048,512]{1,0:T(8,128)(2,1)}, ...) | async-done | bytes 20971536 | tf_op jit(solution)/shard_map/psum | solution.py:247
  (229 shorter events, 154.7 us)
Async XLA Ops:
  7.2 85.4 %copy-start = (bf16[2048,512]{1,0:T(8,128)(2,1)S(1)}, bf16[2048,512]{1,0:T(8,128)(2,1)}, u32[]{:S(2)}) copy-start(bf16[2048,512]{1,0:T(8,128)(2,1)} %param.19) | copy-start | bytes 6291460
  7.2 82.1 %all-gather.8.cloned.1.call-start = ((), (), s32[]{:S(2)}) async-start(), calls=%async_computation.4 | async-start | bytes 5242880 | tf_op jit(solution)/shard_map/all_gather | solution.py:105
  7.9 141.8 %all-gather.12.cloned.1.call-start = ((), (), s32[]{:S(2)}) async-start(), calls=%async_computation.6 | async-start | bytes 1310720 | tf_op jit(solution)/shard_map/all_gather | solution.py:108
  9.7 190.6 %all-gather.16.cloned.1.call-start = ((), (), s32[]{:S(2)}) async-start(), calls=%async_computation.9 | async-start | bytes 5242880 | tf_op jit(solution)/shard_map/all_gather | solution.py:150
  10.4 271.2 %all-gather.10.cloned.1.call-start = ((), (), s32[]{:S(2)}) async-start(), calls=%async_computation.5 | async-start | bytes 5242880 | tf_op jit(solution)/shard_map/all_gather | solution.py:143
  12.0 100.6 %copy-start.53 = (f32[1,512]{1,0:T(1,128)}, f32[1,512]{1,0:T(1,128)S(1)}, u32[]{:S(2)}) copy-start(f32[1,512]{1,0:T(1,128)S(1)} %get-tuple-element.62) | copy-start | bytes 6148
  12.0 102.6 %copy-start.51 = (f32[1,512]{1,0:T(1,128)}, f32[1,512]{1,0:T(1,128)S(1)}, u32[]{:S(2)}) copy-start(f32[1,512]{1,0:T(1,128)S(1)} %get-tuple-element.59) | copy-start | bytes 6148
  26.7 93.8 %copy-start.45 = (f32[1,4,4,128]{3,1,2,0:T(4,128)}, f32[1,4,4,128]{3,1,2,0:T(4,128)S(1)}, u32[]{:S(2)}) copy-start(f32[1,4,4,128]{3,1,2,0:T(4,128)S(1)} %copy.112) | copy-start | bytes 24580
  29.8 85.3 %copy-start.30 = (f32[1024,64]{0,1:T(8,128)}, f32[1024,64]{0,1:T(8,128)S(1)}, u32[]{:S(2)}) copy-start(f32[1024,64]{0,1:T(8,128)S(1)} %get-tuple-element.58) | copy-start | bytes 786436
  92.5 28.0 %copy-start.55 = (f32[1024]{0:T(1024)}, f32[1024]{0:T(1024)S(1)}, u32[]{:S(2)}) copy-start(f32[1024]{0:T(1024)S(1)} %add_rsqrt_fusion.2) | copy-start | bytes 12292
  117.0 9.9 copy-start.17
  138.2 7.1 copy-start.23
  149.6 188.8 %all-gather.14.cloned.1.call-start = ((), (), s32[]{:S(2)}) async-start(), calls=%async_computation.7 | async-start | bytes 9437184 | tf_op jit(solution)/shard_map/all_gather | solution.py:109
  150.2 309.3 %reduce-scatter.7.cloned.1.call-start = ((), (), s32[]{:S(2)}) async-start(), calls=%async_computation.8 | async-start | bytes 5242880 | tf_op jit(solution)/shard_map/reduce_scatter | solution.py:160
  338.4 14.5 %copy-start.12 = (bf16[1024,2048]{1,0:T(8,128)(2,1)S(1)}, bf16[1024,2048]{1,0:T(8,128)(2,1)}, u32[]{:S(2)}) copy-start(bf16[1024,2048]{1,0:T(8,128)(2,1)} %all-gather.8.cloned.1.call-done) | copy-start | bytes 12582916
  357.1 7.3 copy-start.29
  364.4 11.7 %copy-start.57 = (bf16[4,256,2048]{2,1,0:T(8,128)(2,1)S(1)}, bf16[4,256,2048]{2,1,0:T(8,128)(2,1)}, u32[]{:S(2)}) copy-start(bf16[4,256,2048]{2,1,0:T(8,128)(2,1)} %param.25) | copy-start | bytes 12582916
  382.2 157.6 %reduce-scatter.9.cloned.1.call-start = ((), (), s32[]{:S(2)}) async-start(), calls=%async_computation.10 | async-start | bytes 5242880 | tf_op jit(solution)/shard_map/reduce_scatter | solution.py:168
  382.2 7.1 copy-start.25
  395.4 144.4 %copy-start.10 = (bf16[256,2048]{1,0:T(8,128)(2,1)S(1)}, bf16[256,2048]{1,0:T(8,128)(2,1)}, u32[]{:S(2)}) copy-start(bf16[256,2048]{1,0:T(8,128)(2,1)} %param.13) | copy-start | bytes 3145732
  395.4 230.2 %all-gather.18.cloned.1.call-start = ((), (), s32[]{:S(2)}) async-start(), calls=%async_computation.11 | async-start | bytes 5242880 | tf_op jit(solution)/shard_map/all_gather | solution.py:188
  546.7 225.3 %reduce-scatter.11.cloned.1.call-start = ((), (), s32[]{:S(2)}) async-start(), calls=%async_computation.12 | async-start | bytes 5242880 | tf_op jit(solution)/shard_map/reduce_scatter | solution.py:229
  631.5 7.4 copy-start.43
  638.8 9.4 copy-start.28
  648.2 7.8 copy-start.18
  648.2 7.8 copy-start.19
  695.8 105.4 %reduce-scatter.13.cloned.1.call-start = ((), (), s32[]{:S(2)}) async-start(), calls=%async_computation.13 | async-start | bytes 1310720
  727.5 9.6 copy-start.13
  727.5 9.6 copy-start.42
  727.6 9.6 copy-start.46
  727.6 9.6 copy-start.56
  775.5 298.7 %all-reduce.3.cloned.1.call-start = ((), (), s32[]{:S(2)}) async-start(), calls=%async_computation.14 | async-start | bytes 41943040 | tf_op jit(solution)/shard_map/psum | solution.py:247
  (41 other events, 134.4 us)
Sparse Core Ops, SparseCore 0:
  9.6 79.6 all-gather.7
  91.4 29.3 all-gather.11
  122.4 77.8 all-gather.15
  202.3 79.2 all-gather.9
  283.3 55.0 all-gather.13
  382.3 77.1 reduce-scatter.6
  462.5 77.2 reduce-scatter.8
  546.8 78.8 all-gather.17
  696.0 75.9 reduce-scatter.10
  775.6 25.5 reduce-scatter.12
  807.5 266.6 all-reduce.2

commit v2 on v1

v2 whole, which is shorter than its diff:
```python
import functools

import jax
import jax.numpy as jnp
from jax import lax
from jax.experimental import pallas as pl
from jax.experimental.pallas import tpu as pltpu
from jax.sharding import PartitionSpec as P

HEAD_DIM = 128
EPSILON = 1e-05
ROPE_BASE = 10000.0
MASKED = -1e30
VMEM_LIMIT = 60 * 2**20

f32 = jnp.float32
bf16 = jnp.bfloat16


def rotary_tables(row_count):
    half_dim = HEAD_DIM // 2
    positions = jnp.arange(row_count, dtype=jnp.int32)
    inverse = ROPE_BASE ** (-jnp.arange(half_dim, dtype=f32) / half_dim)
    angles = positions.astype(f32)[:, None] * inverse[None, :]
    cosine, sine = jnp.cos(angles), jnp.sin(angles)
    return jnp.concatenate([cosine, cosine], 1), jnp.concatenate([-sine, sine], 1)


def row_factor(values):
    return lax.rsqrt(jnp.mean(values * values, axis=-1, keepdims=True) + EPSILON)


def norm_back(grad_unit, unit_rows, factor):
    return factor * (
        grad_unit - unit_rows * jnp.mean(grad_unit * unit_rows, axis=-1, keepdims=True)
    )


def root_mean(values):
    return jnp.sqrt(jnp.mean(values * values, axis=-1))


def dot(a, b):
    return jnp.dot(a, b, preferred_element_type=f32)


def dot_nt(a, b):
    return lax.dot_general(a, b, (((1,), (1,)), ((), ())), preferred_element_type=f32)


def dot_tn(a, b):
    return lax.dot_general(a, b, (((0,), (0,)), ((), ())), preferred_element_type=f32)


MESH = pl.DeviceIdType.MESH


def greet(peers):
    barrier = pltpu.get_barrier_semaphore()
    for peer in peers:
        pl.semaphore_signal(barrier, inc=1, device_id=peer, device_id_type=MESH)
    pl.semaphore_wait(barrier, len(peers))


def others(n):
    d, z = lax.axis_index("dp"), lax.axis_index("shard")
    return d, z, [(d, lax.rem(z + p, n)) for p in range(1, n)]


def gather_project_kernel(
    n, x_hbm, small_ref, wq_hbm, wk_hbm, wv_hbm,
    x_out, normed_out, q_out, k_out, v_out, small_out, sq_out,
    xs, nb, qb, kb, vb, wq, wk, wv, sq_all, small_all,
    load_sem, out_sem, up_sem, down_sem, recv_sem, small_send, small_recv, sq_send, sq_recv,
):
    T, D = xs.shape[1:]
    C = qb.shape[2]
    d, z, peers = others(n)
    own_load = pltpu.make_async_copy(x_hbm, xs.at[z], load_sem.at[0])
    own_load.start()
    loads = [
        pltpu.make_async_copy(src, dst, load_sem.at[i + 1])
        for i, (src, dst) in enumerate(((wq_hbm, wq), (wk_hbm, wk), (wv_hbm, wv)))
    ]
    for load in loads:
        load.start()
    greet(peers)

    def send_up(o):
        return pltpu.make_async_remote_copy(
            src_ref=xs.at[o], dst_ref=xs.at[o], send_sem=up_sem.at[o], recv_sem=recv_sem.at[o],
            device_id=(d, lax.rem(z + 1, n)), device_id_type=MESH,
        )

    def send_down(o):
        return pltpu.make_async_remote_copy(
            src_ref=xs.at[o], dst_ref=xs.at[o], send_sem=down_sem.at[o], recv_sem=recv_sem.at[o],
            device_id=(d, lax.rem(z + n - 1, n)), device_id_type=MESH,
        )

    own_load.wait()
    small_copies = []
    for p, peer in enumerate(peers):
        copy = pltpu.make_async_remote_copy(
            src_ref=small_ref, dst_ref=small_all.at[z], send_sem=small_send.at[p],
            recv_sem=small_recv.at[z], device_id=peer, device_id_type=MESH,
        )
        copy.start()
        small_copies.append(copy)

    @pl.when(z < n - 1)
    def _():
        send_up(z).start()

    @pl.when(z > 0)
    def _():
        send_down(z).start()

    small_all[z] = small_ref[...]
    for load in loads:
        load.wait()
    for p in range(1, n):
        o = lax.rem(z + n - p, n)
        pltpu.make_async_remote_copy(
            src_ref=small_ref, dst_ref=small_all.at[o], send_sem=small_send.at[p - 1],
            recv_sem=small_recv.at[o], device_id=(d, o), device_id_type=MESH,
        ).wait_recv()

    lanes = lax.broadcasted_iota(jnp.int32, (T, 128), 1)
    step_rows = 32

    def outs(o):
        return [
            pltpu.make_async_copy(src.at[o], dst.at[o], out_sem.at[i, o])
            for i, (src, dst) in enumerate(
                ((xs, x_out), (nb, normed_out), (qb, q_out), (kb, k_out), (vb, v_out))
            )
        ]

    def compute(o):
        gain = jnp.concatenate([small_all[s, 0:1, T:] for s in range(n)], axis=1)

        def norm_rows(i, carry):
            r = pl.ds(pl.multiple_of(i * step_rows, step_rows), step_rows)
            x = xs[o, r, :].astype(f32)
            factor = lax.rsqrt(jnp.sum(x * x, axis=1, keepdims=True) / D + EPSILON)
            nb[o, r, :] = (x * factor * gain).astype(bf16)
            return carry

        lax.fori_loop(0, T // step_rows, norm_rows, 0)
        q = jnp.dot(nb[o], wq[...], preferred_element_type=f32)
        qb[o] = q
        q_sum = jnp.sum(q * q, axis=1, keepdims=True)
        k = jnp.dot(nb[o], wk[...], preferred_element_type=f32)
        kb[o] = k
        k_sum = jnp.sum(k * k, axis=1, keepdims=True)
        vb[o] = jnp.dot(nb[o], wv[...], preferred_element_type=f32).astype(bf16)
        both = jnp.where(lanes == 0, q_sum, jnp.where(lanes == 1, k_sum, 0.0))
        sq_all[z, o] = both.T[0:8]
        for copy in outs(o):
            copy.start()

    def step(s, carry):
        below, above = z - s, z + s

        @pl.when((s > 0) & (below >= 0))
        def _():
            send_up(below).wait_recv()

            @pl.when(z < n - 1)
            def _():
                send_up(below).start()

        @pl.when((s > 0) & (above < n))
        def _():
            send_down(above).wait_recv()

            @pl.when(z > 0)
            def _():
                send_down(above).start()

        def side(j, inner):
            o = z - s + 2 * s * j

            @pl.when((o >= 0) & (o < n) & ((s > 0) | (j == 0)))
            def _():
                compute(o)

            return inner

        lax.fori_loop(0, 2, side, 0)
        return carry

    lax.fori_loop(0, n, step, 0)

    sq_copies = []
    for p, peer in enumerate(peers):
        copy = pltpu.make_async_remote_copy(
            src_ref=sq_all.at[z], dst_ref=sq_all.at[z], send_sem=sq_send.at[p],
            recv_sem=sq_recv.at[z], device_id=peer, device_id_type=MESH,
        )
        copy.start()
        sq_copies.append(copy)
    small_out[...] = small_all[...]

    def finish(o, carry):
        for copy in outs(o):
            copy.wait()

        @pl.when((z < n - 1) & (o <= z))
        def _():
            send_up(o).wait_send()

        @pl.when((z > 0) & (o >= z))
        def _():
            send_down(o).wait_send()

        return carry

    lax.fori_loop(0, n, finish, 0)
    for p in range(1, n):
        o = lax.rem(z + n - p, n)
        pltpu.make_async_remote_copy(
            src_ref=sq_all.at[o], dst_ref=sq_all.at[o], send_sem=sq_send.at[p - 1],
            recv_sem=sq_recv.at[o], device_id=(d, o), device_id_type=MESH,
        ).wait_recv()
    total = sq_all[0]
    for s in range(1, n):
        total = total + sq_all[s]
    sq_out[...] = total
    for copy in small_copies + sq_copies:
        copy.wait_send()


def gather_project(n, tokens, small, wq, wk, wv):
    T, D = tokens.shape
    C = wq.shape[1]
    hbm = pl.BlockSpec(memory_space=pl.ANY)
    vmem = pl.BlockSpec(memory_space=pltpu.VMEM)
    dma = pltpu.SemaphoreType.DMA
    return pl.pallas_call(
        functools.partial(gather_project_kernel, n),
        out_shape=[
            jax.ShapeDtypeStruct((n, T, D), bf16),
            jax.ShapeDtypeStruct((n, T, D), bf16),
            jax.ShapeDtypeStruct((n, T, C), f32),
            jax.ShapeDtypeStruct((n, T, C), f32),
            jax.ShapeDtypeStruct((n, T, C), bf16),
            jax.ShapeDtypeStruct((n,) + small.shape, f32),
            jax.ShapeDtypeStruct((n, 8, T), f32),
        ],
        in_specs=[hbm, vmem, hbm, hbm, hbm],
        out_specs=[hbm] * 5 + [vmem] * 2,
        scratch_shapes=[
            pltpu.VMEM((n, T, D), bf16),
            pltpu.VMEM((n, T, D), bf16),
            pltpu.VMEM((n, T, C), f32),
            pltpu.VMEM((n, T, C), f32),
            pltpu.VMEM((n, T, C), bf16),
            pltpu.VMEM((D, C), bf16),
            pltpu.VMEM((D, C), bf16),
            pltpu.VMEM((D, C), bf16),
            pltpu.VMEM((n, n, 8, T), f32),
            pltpu.VMEM((n,) + small.shape, f32),
            dma((4,)),
            dma((5, n)),
            dma((n,)),
            dma((n,)),
            dma((n,)),
            dma((n,)),
            dma((n,)),
            dma((n,)),
            dma((n,)),
        ],
        compiler_params=pltpu.CompilerParams(
            collective_id=0, has_side_effects=True, vmem_limit_bytes=VMEM_LIMIT
        ),
        name="gather_project",
    )(tokens, small, wq, wk, wv)


def rope(v, cosine, sine):
    return v * cosine + pltpu.roll(v, HEAD_DIM // 2, 1) * sine


def key_span(i, block, length):
    return min(length, max((i + 1) * block, length // 2))


def block_scores(q, k, i, block, limit):
    s = dot_nt(q, k) * (HEAD_DIM**-0.5)
    row = lax.broadcasted_iota(jnp.int32, s.shape, 0) + i * block
    col = lax.broadcasted_iota(jnp.int32, s.shape, 1)
    return jnp.where((col <= row) | (col < limit), s, MASKED)


def attention_kernel(prefix, q_raw, k_raw, v_ref, factors, cosine, sine, gains, q_out, k_out, mixed):
    length = q_raw.shape[0]
    block = 256
    limit = prefix[0]

    def turn(raw, out, column, gain):
        def part(i, carry):
            r = pl.ds(pl.multiple_of(i * block, block), block)
            v = raw[r, :] * factors[r, column : column + 1] * gain
            out[r, :] = rope(v, cosine[r, :], sine[r, :]).astype(bf16)
            return carry

        lax.fori_loop(0, length // block, part, 0)

    turn(q_raw, q_out, 0, gains[0:1, :])
    turn(k_raw, k_out, 1, gains[1:2, :])
    for i in range(length // block):
        span = key_span(i, block, length)
        r = pl.ds(i * block, block)
        s = block_scores(q_out[r, :], k_out[0:span, :], i, block, limit)
        e = jnp.exp(s - jnp.max(s, axis=1, keepdims=True))
        total = jnp.sum(e, axis=1, keepdims=True)
        mixed[r, :] = (dot(e.astype(bf16), v_ref[0:span, :]) / total).astype(bf16)


def attention(prefix, q_raw, k_raw, values, factors, cosine, sine, gains):
    length, local = q_raw.shape
    heads = local // HEAD_DIM
    head = pl.BlockSpec((length, HEAD_DIM), lambda h, p: (0, h))
    whole = lambda a: pl.BlockSpec(a.shape, lambda h, p: (0, 0))
    out = jax.ShapeDtypeStruct((length, local), bf16)
    return pl.pallas_call(
        attention_kernel,
        out_shape=[out] * 3,
        grid_spec=pltpu.PrefetchScalarGridSpec(
            num_scalar_prefetch=1,
            grid=(heads,),
            in_specs=[
                head, head, head, whole(factors), whole(cosine), whole(sine),
                pl.BlockSpec((2, HEAD_DIM), lambda h, p: (0, h)),
            ],
            out_specs=[head] * 3,
        ),
        compiler_params=pltpu.CompilerParams(vmem_limit_bytes=VMEM_LIMIT),
        name="attention",
    )(prefix, q_raw, k_raw, values, factors, cosine, sine, gains)


def attention_back_kernel(
    prefix, q_ref, k_ref, v_ref, g_ref, q_raw, k_raw, factors, cosine, sine, gains,
    dq_out, dk_out, dv_out, gain_out, inner_out, k_acc, v_acc, inner_acc,
):
    length = q_ref.shape[0]
    block = 256
    limit = prefix[0]
    scale = HEAD_DIM**-0.5
    h = pl.program_id(0)
    k_acc[...] = jnp.zeros_like(k_acc)
    v_acc[...] = jnp.zeros_like(v_acc)

    @pl.when(h == 0)
    def _():
        inner_acc[...] = jnp.zeros_like(inner_acc)

    for i in range(length // block):
        span = key_span(i, block, length)
        r = pl.ds(i * block, block)
        q, g = q_ref[r, :], g_ref[r, :]
        s = block_scores(q, k_ref[0:span, :], i, block, limit)
        e = jnp.exp(s - jnp.max(s, axis=1, keepdims=True))
        p = e * (1.0 / jnp.sum(e, axis=1, keepdims=True))
        pg = dot_nt(g, v_ref[0:span, :])
        t = p * pg
        ds = (t - p * jnp.sum(t, axis=1, keepdims=True)).astype(bf16)
        dq_out[r, :] = dot(ds, k_ref[0:span, :]) * scale
        k_acc[0:span, :] += dot_tn(ds, q) * scale
        v_acc[0:span, :] += dot_tn(p.astype(bf16), g)
    dv_out[...] = v_acc[...].astype(bf16)
    lanes = lax.broadcasted_iota(jnp.int32, (block, 128), 1)

    def back(i, carry):
        gq, gk = carry
        r = pl.ds(pl.multiple_of(i * block, block), block)
        c, s = cosine[r, :], sine[r, :]
        dq = rope(dq_out[r, :], c, -s)
        dk = rope(k_acc[r, :], c, -s)
        uq = q_raw[r, :] * factors[r, 0:1]
        uk = k_raw[r, :] * factors[r, 1:2]
        gq = gq + jnp.sum(dq * uq, axis=0, keepdims=True)
        gk = gk + jnp.sum(dk * uk, axis=0, keepdims=True)
        dq = dq * gains[0:1, :]
        dk = dk * gains[1:2, :]
        dq_out[r, :] = dq
        dk_out[r, :] = dk
        inner_q = jnp.sum(dq * uq, axis=1, keepdims=True)
        inner_k = jnp.sum(dk * uk, axis=1, keepdims=True)
        both = jnp.where(lanes == 0, inner_q, jnp.where(lanes == 1, inner_k, 0.0))
        inner_acc[i] += both.T[0:8]
        return gq, gk

    zero = jnp.zeros((1, HEAD_DIM), f32)
    gq, gk = lax.fori_loop(0, length // block, back, (zero, zero))
    gain_out[0:1, :] = gq
    gain_out[1:2, :] = gk

    @pl.when(h == pl.num_programs(0) - 1)
    def _():
        inner_out[...] = inner_acc[...]


def attention_back(prefix, q, k, v, g, q_raw, k_raw, factors, cosine, sine, gains):
    length, local = q.shape
    heads = local // HEAD_DIM
    head = pl.BlockSpec((length, HEAD_DIM), lambda h, p: (0, h))
    pair = pl.BlockSpec((2, HEAD_DIM), lambda h, p: (0, h))
    whole = lambda a: pl.BlockSpec(a.shape, lambda h, p: (0, 0))
    wide = jax.ShapeDtypeStruct((length, local), f32)
    inner = (length // 256, 8, 256)
    return pl.pallas_call(
        attention_back_kernel,
        out_shape=[
            wide, wide, jax.ShapeDtypeStruct((length, local), bf16),
            jax.ShapeDtypeStruct((2, local), f32), jax.ShapeDtypeStruct(inner, f32),
        ],
        grid_spec=pltpu.PrefetchScalarGridSpec(
            num_scalar_prefetch=1,
            grid=(heads,),
            in_specs=[head] * 6 + [whole(factors), whole(cosine), whole(sine), pair],
            out_specs=[head, head, head, pair, pl.BlockSpec(inner, lambda h, p: (0, 0, 0))],
            scratch_shapes=[
                pltpu.VMEM((length, HEAD_DIM), f32),
                pltpu.VMEM((length, HEAD_DIM), f32),
                pltpu.VMEM(inner, f32),
            ],
        ),
        compiler_params=pltpu.CompilerParams(vmem_limit_bytes=VMEM_LIMIT),
        name="attention_back",
    )(prefix, q, k, v, g, q_raw, k_raw, factors, cosine, sine, gains)


def per_device(
    tokens,
    out_grad,
    routes,
    gate_weights,
    prefix,
    query_weight,
    key_weight,
    value_weight,
    output_weight,
    norm_gains,
    expert_gate,
    expert_up,
    expert_down,
):
    rows, width = tokens.shape
    shards = lax.axis_size("shard")
    groups = lax.axis_size("dp")
    place = lax.axis_index("shard")
    group = lax.axis_index("dp")
    length = rows * shards
    local = width // shards
    experts = expert_gate.shape[0]
    units = expert_gate.shape[2]

    expert_ids = jnp.arange(experts, dtype=jnp.int32)
    weight_own = jnp.sum(
        jnp.where(routes[:, :, None] == expert_ids[None, None, :], gate_weights[:, :, None], 0.0),
        axis=1,
    )
    own_gains = norm_gains.astype(f32)
    small = jnp.concatenate(
        [
            jnp.pad(weight_own.T, ((0, 8 - experts), (0, 0))),
            jnp.pad(jnp.stack([own_gains[0], own_gains[3]]), ((0, 6), (0, 0))),
        ],
        axis=1,
    )
    x_all_b, normed, query_raw, key_raw, values, small_all, squares = gather_project(
        shards, tokens, small, query_weight, key_weight, value_weight
    )
    x_all_b = x_all_b.reshape(length, width)
    normed = normed.reshape(length, width)
    query_raw = query_raw.reshape(length, local)
    key_raw = key_raw.reshape(length, local)
    values = values.reshape(length, local)
    combine = small_all[:, :experts, :rows].transpose(0, 2, 1).reshape(length, experts)
    gain_in = small_all[:, 0, rows:].reshape(width)
    gain_expert = small_all[:, 1, rows:].reshape(width)
    head_gains = own_gains[1:3]
    slab = width // groups
    output_weight, out_grad_b, squares = lax.optimization_barrier(
        (output_weight, out_grad, squares)
    )
    out_slab = lax.dynamic_slice_in_dim(output_weight, group * slab, slab, 0)
    out_slab = lax.all_gather(out_slab, "shard", axis=1, tiled=True)
    full_output = lax.all_gather(out_slab, "dp", axis=0, tiled=True)

    x_all = x_all_b.astype(f32)
    factors = lax.rsqrt(squares[:, :2].transpose(0, 2, 1).reshape(length, 2) / width + EPSILON)
    cosine, sine = rotary_tables(length)
    queries, keys, mixed_own = attention(
        prefix, query_raw, key_raw, values, factors, cosine, sine, head_gains
    )
    mixed_all = lax.all_gather(mixed_own, "shard", axis=1, tiled=True)

    attended = dot(mixed_all, full_output)
    residual = x_all + attended
    factor_res = row_factor(residual)
    expert_in = (residual * factor_res * gain_expert).astype(bf16)

    g_all = lax.all_gather(out_grad_b, "shard", axis=0, tiled=True)
    gate_flat = expert_gate.transpose(1, 0, 2).reshape(width, experts * units)
    up_flat = expert_up.transpose(1, 0, 2).reshape(width, experts * units)
    down_flat = expert_down.reshape(experts * units, width)
    gate_part = dot(expert_in, gate_flat)
    up_part = dot(expert_in, up_flat)
    sig = jax.nn.sigmoid(gate_part)
    wide = jnp.repeat(combine, units, axis=1)
    hidden = (gate_part * sig * up_part * wide).astype(bf16)
    sum_part = dot(hidden, down_flat)
    expert_sum = lax.psum_scatter(
        sum_part.astype(bf16), "shard", scatter_dimension=0, tiled=True
    ).astype(f32)

    hidden_grad = dot_nt(g_all, down_flat) * wide
    up_grad = (hidden_grad * gate_part * sig).astype(bf16)
    gate_grad = (hidden_grad * up_part * sig * (1.0 + gate_part * (1.0 - sig))).astype(bf16)
    in_part = dot_nt(gate_grad, gate_flat) + dot_nt(up_grad, up_flat)
    in_grad = lax.psum_scatter(
        in_part.astype(bf16), "shard", scatter_dimension=0, tiled=True
    ).astype(f32)
    grad_down = dot_tn(hidden, g_all).reshape(experts, units, width)
    grad_gate = dot_tn(expert_in, gate_grad).reshape(width, experts, units).transpose(1, 0, 2)
    grad_up = dot_tn(expert_in, up_grad).reshape(width, experts, units).transpose(1, 0, 2)

    grad_gate, grad_up, grad_down = lax.psum(
        (grad_gate.astype(bf16), grad_up.astype(bf16), grad_down.astype(bf16)), "dp"
    )

    def own_rows(v):
        return lax.dynamic_slice_in_dim(v, place * rows, rows, 0)

    x_own = tokens.astype(f32)
    g_own = out_grad.astype(f32)
    attended_own = own_rows(attended)
    residual_own = x_own + attended_own
    output = residual_own + expert_sum
    root_means = jnp.stack([root_mean(attended_own), root_mean(expert_sum), root_mean(output)])
    factor_own = own_rows(factor_res)
    unit_res = residual_own * factor_own
    gain_grad_res = jnp.sum(in_grad * unit_res, axis=0)
    residual_grad = g_own + norm_back(in_grad * gain_expert, unit_res, factor_own)
    attended_grad = lax.all_gather(residual_grad.astype(bf16), "shard", axis=0, tiled=True)

    grad_output = dot_tn(
        mixed_all, lax.dynamic_slice_in_dim(attended_grad, place * local, local, 1)
    )
    mixed_grad = dot_nt(
        attended_grad, lax.dynamic_slice_in_dim(full_output, place * local, local, 0)
    ).astype(bf16)
    query_norm_grad, key_norm_grad, value_raw_grad, gain_grad_heads, inner = attention_back(
        prefix, queries, keys, values, mixed_grad, query_raw, key_raw, factors, cosine, sine,
        head_gains,
    )
    inner = lax.psum(inner[:, :2], "shard") / width
    inner = inner.transpose(0, 2, 1).reshape(length, 2)
    factor_query, factor_key = factors[:, 0:1], factors[:, 1:2]
    query_raw_grad = (
        factor_query * (query_norm_grad - query_raw * factor_query * inner[:, 0:1])
    ).astype(bf16)
    key_raw_grad = (factor_key * (key_norm_grad - key_raw * factor_key * inner[:, 1:2])).astype(
        bf16
    )
    normed_part = (
        dot_nt(query_raw_grad, query_weight)
        + dot_nt(key_raw_grad, key_weight)
        + dot_nt(value_raw_grad, value_weight)
    )
    normed_grad = lax.psum_scatter(
        normed_part.astype(bf16), "shard", scatter_dimension=0, tiled=True
    ).astype(f32)
    grad_query = dot_tn(normed, query_raw_grad)
    grad_key = dot_tn(normed, key_raw_grad)
    grad_value = dot_tn(normed, value_raw_grad)

    factor_x = row_factor(x_own)
    unit_x = x_own * factor_x
    gain_grad_x = jnp.sum(normed_grad * unit_x, axis=0)
    grad_tokens = residual_grad + norm_back(normed_grad * gain_in, unit_x, factor_x)

    gain_rows = lax.psum_scatter(
        jnp.stack([gain_grad_x, gain_grad_res]), "shard", scatter_dimension=1, tiled=True
    )
    grad_gains = jnp.stack([gain_rows[0], gain_grad_heads[0], gain_grad_heads[1], gain_rows[1]])

    (grad_query, grad_key, grad_value, grad_output), grad_gate, grad_up, grad_down = (
        lax.optimization_barrier(
            (
                tuple(v.astype(bf16) for v in (grad_query, grad_key, grad_value, grad_output)),
                grad_gate,
                grad_up,
                grad_down,
            )
        )
    )
    grad_query, grad_key, grad_value, grad_output = lax.psum(
        (grad_query, grad_key, grad_value, grad_output), "dp"
    )

    return (
        output.astype(bf16),
        grad_tokens,
        root_means,
        grad_query.astype(f32),
        grad_key.astype(f32),
        grad_value.astype(f32),
        grad_output.astype(f32),
        lax.psum(grad_gains, "dp"),
        grad_gate.astype(f32),
        grad_up.astype(f32),
        grad_down.astype(f32),
    )


def solution(mesh):
    placed = (
        P(("dp", "shard"), None),
        P(("dp", "shard"), None),
        P(("dp", "shard"), None),
        P(("dp", "shard"), None),
        P("dp"),
        P(None, "shard"),
        P(None, "shard"),
        P(None, "shard"),
        P(None, "shard"),
        P(None, "shard"),
        P(None, None, "shard"),
        P(None, None, "shard"),
        P(None, "shard", None),
    )
    return jax.shard_map(
        per_device,
        mesh=mesh,
        in_specs=placed,
        out_specs=(
            P(("dp", "shard"), None),
            P(("dp", "shard"), None),
            P(None, ("dp", "shard")),
            P(None, "shard"),
            P(None, "shard"),
            P(None, "shard"),
            P(None, "shard"),
            P(None, "shard"),
            P(None, None, "shard"),
            P(None, None, "shard"),
            P(None, "shard", None),
        ),
        check_vma=False,
    )
```

time: 1120 us -> 1090 us (0.973)
  Pallas kernels: 0 us -> 123 us
  matrix products: 186 us -> 130 us
  waiting for transfers between devices: 734 us -> 679 us
  blocking collectives: 51.1 us -> 25 us
    pallas_call x0 -> x3, Pallas kernels: none -> 123 us  [the longest x1 83.9 us: gather_project(): pl.pallas_call(functools.partial(gather_project_kernel, n), out_shape=[ja...]
    psum x1 -> x2, waiting for transfers between devices: 258 us -> 212 us  [the longest x1 115 us: per_device(): lax.psum((grad_gate.astype(bf16), grad_up.astype(bf16), grad_down.astype(...]
    reduce_scatter x1, waiting for transfers between devices: 21.4 us -> 66.9 us  [per_device(): lax.psum_scatter(normed_part.astype(bf16), 'shard', scatter_dimension=0,...]
    all_gather x1, waiting for transfers between devices: 76.5 us -> 38.6 us  [per_device(): lax.all_gather(residual_grad.astype(bf16), 'shard', axis=0, tiled=True)]
    all_gather x2 -> x1, waiting for transfers between devices: 91.8 us -> 59.9 us  [per_device(): g_all = lax.all_gather(out_grad_b, 'shard', axis=0, tiled=True)]
    dot_general x5 -> x0, matrix products: 29.2 us -> none  [the longest x1 9.38 us: per_device(): jnp.einsum('hqd,hkd->hqk', grad_heads, value_heads, preferred_element_typ...]
    reduce_scatter x1, waiting for transfers between devices: 63.9 us -> 80.1 us  [per_device(): lax.psum_scatter(sum_part.astype(bf16), 'shard', scatter_dimension=0, til...]
    all_gather x1 -> x0, blocking collectives: 13.7 us -> none  [per_device(): small_all = lax.all_gather(small, 'shard', axis=0)]
  transfers between devices with their start and end apart: 11 -> 11, of which waited for: 10 -> 11; matrix products, arithmetic and copies ran while one was open for 15% -> 15% of each run, Pallas kernels for 0% -> 4%
where the time goes in v2:
time: 1090 us; the launch traced here: 1070 us
  waiting for transfers between devices  679 us (62%)
  matrix products  130 us (12%)
  Pallas kernels  123 us (11%)
  other arithmetic  55.8 us (5%)
  local copies, waits for them, and re-layouts  45.4 us (4%)
  blocking collectives  25 us (2%)
  between operations  15.1 us (1%)
    psum x1, waiting for transfers between devices, per_device(): lax.psum((grad_gate.astype(bf16), grad_up.astype(bf16), grad_down.astype(...  115 us
    psum x1, waiting for transfers between devices, per_device(): lax.psum((grad_query, grad_key, grad_value, grad_output), 'dp')  96.7 us
    pallas_call x1, Pallas kernels, gather_project(): pl.pallas_call(functools.partial(gather_project_kernel, n), out_shape=[ja...  83.9 us
    reduce_scatter x1, waiting for transfers between devices, per_device(): lax.psum_scatter(sum_part.astype(bf16), 'shard', scatter_dimension=0, til...  80.1 us
    all_gather x1, waiting for transfers between devices, per_device(): mixed_all = lax.all_gather(mixed_own, 'shard', axis=1, tiled=True)  70.3 us
    reduce_scatter x1, waiting for transfers between devices, per_device(): lax.psum_scatter(in_part.astype(bf16), 'shard', scatter_dimension=0, tile...  68.3 us
    reduce_scatter x1, waiting for transfers between devices, per_device(): lax.psum_scatter(normed_part.astype(bf16), 'shard', scatter_dimension=0,...  66.9 us
    all_gather x1, waiting for transfers between devices, per_device(): g_all = lax.all_gather(out_grad_b, 'shard', axis=0, tiled=True)  59.9 us
  transfers between devices with their start and end apart: 11, of which 11 were waited for; matrix products, arithmetic and copies ran while one was open for 15% of the time, Pallas kernels for 4%

profile of v2, /device:TPU:12, one launch (start us, length us, event | category | flops | bytes accessed | tf_op | source)
XLA Modules:
  0.0 1074.6 jit_solution(10353727494127442976)
XLA Ops:
  9.4 83.9 %gather_project.1 = (bf16[4,256,2048]{2,1,0:T(8,128)(2,1)}, bf16[4,256,2048]{2,1,0:T(8,128)(2,1)}, f32[4,256,512]{2,1,0:T(8,128)}, f32[4,256,512]{2,1,0:T(8,128)...) custom-call(bf16[256,2048]{1,0:T(8,128)(2,1)} %x_hbm.1, ...), custom_call_target="tpu_custom_call" | custom-call | tf_op jit(solution)/shard_map/gather_project/pallas_call | solution.py:241
  101.9 15.6 %attention.1 = (bf16[1024,512]{1,0:T(8,128)(2,1)}, bf16[1024,512]{1,0:T(8,128)(2,1)}, bf16[1024,512]{1,0:T(8,128)(2,1)}) custom-call(s32[1]{0:T(128)S(6)} %copy.63.prefix, f32[1024,512]{1,0:T(8,128)} %bitcast.79, f32[1024,512]{1,0:T(8,128)} %bitcast.81, bf16[1024,512]{1,0:T(8,128)(2,1)} %bitcast.90, f32[1024,2]{1,0:T(8,128)} %bitcast.86, ...), custom_call_target="tpu_custom_call" | custom-call | tf_op jit(solution)/shard_map/attention/pallas_call | solution.py:328
  128.6 6.3 copy.46
  134.9 6.2 copy.47
  142.6 59.9 %all-gather.12.cloned.1.call-done = bf16[1024,2048]{1,0:T(8,128)(2,1)} async-done(((bf16[256,2048]{1,0:T(8,128)(2,1)}), bf16[1024,2048]{1,0:T(8,128)(2,1)}) %all-gather.12.cloned.1.call-update) | async-done | bytes 4194320 | tf_op jit(solution)/shard_map/all_gather | solution.py:508
  202.5 11.2 %convolution_multiply_fusion = f32[1024,1024]{1,0:T(8,128)} fusion(f32[1024,1024]{1,0:T(8,128)} %bitcast.96, bf16[1024,2048]{1,0:T(8,128)(2,1)} %all-gather.12.cloned.1.call-done, bf16[1024,2048]{1,0:T(8,128)(2,1)} %bitcast.118), kind=kOutput, calls=%fused_computation.31 | convolution fusion | flops 4296015872 | bytes 16777216 | tf_op jit(solution)/shard_map/dot_general | solution.py:48
  213.7 70.3 %all-gather.6.cloned.1.call-done = bf16[1024,2048]{1,0:T(8,128)(2,1)} async-done(((bf16[1024,512]{1,0:T(8,128)(2,1)}), bf16[1024,2048]{1,0:T(8,128)(2,1)}) %all-gather.6.cloned.1.call-update) | async-done | bytes 4194320 | tf_op jit(solution)/shard_map/all_gather | solution.py:501
  284.0 56.8 %all-gather.10.cloned.1.call-done = bf16[2048,2048]{1,0:T(8,128)(2,1)} async-done(((bf16[256,2048]{1,0:T(8,128)(2,1)}), bf16[2048,2048]{1,0:T(8,128)(2,1)}) %all-gather.10.cloned.1.call-update) | async-done | bytes 8388624 | tf_op jit(solution)/shard_map/all_gather | solution.py:493
  340.8 13.5 %multiply_reduce_fusion = (f32[1024]{0:T(1024)S(1)}, f32[1024,2048]{1,0:T(8,128)S(1)}) fusion(bf16[4,256,2048]{2,1,0:T(8,128)(2,1)} %get-tuple-element.43, bf16[1024,2048]{1,0:T(8,128)(2,1)} %all-gather.6.cloned.1.call-done, bf16[2048,2048]{1,0:T(8,128)(2,1)} %all-gather.10.cloned.1.call-done), kind=kOutput, calls=%fused_computation.4 | convolution fusion | flops 8598322176 | bytes 25169920 | tf_op jit(solution)/shard_map/dot_general | solution.py:44
  359.6 6.3 fusion.31
  365.9 9.8 multiply_convert_fusion.3
  375.7 7.6 fusion.32
  383.3 6.0 add_convert_fusion.1
  389.4 8.3 convolution_convert_fusion.3
  398.3 68.3 %reduce-scatter.9.cloned.1.call-done = bf16[256,2048]{1,0:T(8,128)(2,1)} async-done(((bf16[1024,2048]{1,0:T(8,128)(2,1)}), bf16[256,2048]{1,0:T(8,128)(2,1)}) %reduce-scatter.9.cloned.1.call-update) | async-done | bytes 1048592 | tf_op jit(solution)/shard_map/reduce_scatter | solution.py:526
  466.6 80.1 %reduce-scatter.7.cloned.1.call-done = bf16[256,2048]{1,0:T(8,128)(2,1)} async-done(((bf16[1024,2048]{1,0:T(8,128)(2,1)}), bf16[256,2048]{1,0:T(8,128)(2,1)}) %reduce-scatter.7.cloned.1.call-update) | async-done | bytes 1048592 | tf_op jit(solution)/shard_map/reduce_scatter | solution.py:518
  554.3 9.4 convolution_convert_fusion.2
  563.8 6.4 copy.49
  570.1 8.4 convolution_convert_fusion.1
  578.5 6.3 copy.50
  584.9 8.3 convolution_convert_fusion
  594.7 38.6 %all-gather.14.cloned.1.call-done = bf16[1024,2048]{1,0:T(8,128)(2,1)} async-done(((bf16[256,2048]{1,0:T(8,128)(2,1)}), bf16[1024,2048]{1,0:T(8,128)(2,1)}) %all-gather.14.cloned.1.call-update) | async-done | bytes 4194320 | tf_op jit(solution)/shard_map/all_gather | solution.py:550
  633.3 6.2 fusion.18.g_ref
  639.5 23.6 %attention_back.1 = (f32[1024,512]{1,0:T(8,128)}, f32[1024,512]{1,0:T(8,128)}, bf16[1024,512]{1,0:T(8,128)(2,1)}, f32[2,512]{1,0:T(2,128)}, f32[4,8,256]{2,1,0:T(8,128)}) custom-call(s32[1]{0:T(128)S(6)} %copy.63.prefix, bf16[1024,512]{1,0:T(8,128)(2,1)} %get-tuple-element.46.q_ref, bf16[1024,512]{1,0:T(8,128)(2,1)} %get-tuple-element.47.k_ref, ...), custom_call_target="tpu_custom_call" | custom-call | tf_op jit(solution)/shard_map/attention_back/pallas_call | solution.py:415
  663.8 11.4 %psum.63 = f32[4,2,256]{2,1,0:T(2,128)S(1)} all-reduce(f32[4,2,256]{2,1,0:T(2,128)S(1)} %slice.52), channel_id=1, replica_groups=mesh['dp'=8,'shard'=4] {'shard'}, use_global_device_ids=true, to_apply=%region_6.7 | all-reduce | flops 2048 | bytes 16384 | tf_op jit(solution)/shard_map/psum | solution.py:562
  696.8 114.9 %all-reduce.9.cloned.1.call-done = (bf16[4,2048,256]{2,1,0:T(8,128)(2,1)}, bf16[4,2048,256]{2,1,0:T(8,128)(2,1)}, bf16[4,256,2048]{2,1,0:T(8,128)(2,1)}) async-done(((bf16[4,2048,256]{2,1,0:T(8,128)(2,1)}, bf16[4,2048,256]{2,1,0:T(8,128)(2,1)}, bf16[4,256,2048]{2,1,0:T(8,128)(2,1)}), (bf16[4,2048,256]{2,1,0:T(8,128)(2,1)}, bf16[4,2048,256]{2,1,0:T(8,128)(2,1)}, ...) | async-done | bytes 12582928 | tf_op jit(solution)/shard_map/psum | solution.py:533
  822.8 8.3 add_convert_fusion
  831.8 6.6 convert_element_type.171
  847.7 96.7 %all-reduce.7.cloned.1.call-done = (bf16[2048,512]{1,0:T(8,128)(2,1)}, bf16[2048,512]{1,0:T(8,128)(2,1)}, bf16[2048,512]{1,0:T(8,128)(2,1)}, bf16[2048,512]{1,0:T(8,128)(2,1)}) async-done(((bf16[2048,512]{1,0:T(8,128)(2,1)}, bf16[2048,512]{1,0:T(8,128)(2,1)}, bf16[2048,512]{1,0:T(8,128)(2,1)}, bf16[2048,512]{1,0:T(8,128)(2,1)}), (bf16[2048,512]{1,0:T(8,128)(2,1)}, bf16[2048,512]{1,0:T(8,128)(2,1)}, ...) | async-done | bytes 8388624 | tf_op jit(solution)/shard_map/psum | solution.py:603
  956.7 66.9 %reduce-scatter.11.cloned.1.call-done = bf16[256,2048]{1,0:T(8,128)(2,1)} async-done(((bf16[1024,2048]{1,0:T(8,128)(2,1)}), bf16[256,2048]{1,0:T(8,128)(2,1)}) %reduce-scatter.11.cloned.1.call-update) | async-done | bytes 1048592 | tf_op jit(solution)/shard_map/reduce_scatter | solution.py:576
  1032.9 19.9 %reduce-scatter.13.cloned.1.call-done = f32[512,2]{1,0:T(8,128)} async-done(((f32[2048,2]{1,0:T(8,128)}), f32[512,2]{1,0:T(8,128)}) %reduce-scatter.13.cloned.1.call-update) | async-done | bytes 4112
  1054.2 13.6 %psum.71 = f32[4,512]{1,0:T(4,128)} all-reduce(f32[4,512]{1,0:T(4,128)S(1)} %pad_maximum_fusion.3), channel_id=1, replica_groups=mesh['dp'=8,'shard'=4] {'dp'}, use_global_device_ids=true, to_apply=%region_22.23 | all-reduce | flops 2048 | bytes 16384 | tf_op jit(solution)/shard_map/psum | solution.py:615
  (147 shorter events, 103.9 us)
Async XLA Ops:
  7.2 86.2 %copy-start = (bf16[2048,512]{1,0:T(8,128)(2,1)S(1)}, bf16[2048,512]{1,0:T(8,128)(2,1)}, u32[]{:S(2)}) copy-start(bf16[2048,512]{1,0:T(8,128)(2,1)} %param.21) | copy-start | bytes 6291460
  7.2 115.9 %all-gather.8.cloned.1.call-start = ((), (), s32[]{:S(2)}) async-start(), calls=%async_computation.5 | async-start | bytes 1310720 | tf_op jit(solution)/shard_map/all_gather | solution.py:492
  9.4 85.5 %copy-start.27 = (bf16[4,512]{1,0:T(4,128)(2,1)S(1)}, bf16[4,512]{1,0:T(4,128)(2,1)}, u32[]{:S(2)}) copy-start(bf16[4,512]{1,0:T(4,128)(2,1)} %param.22) | copy-start | bytes 12292
  94.2 108.4 %all-gather.12.cloned.1.call-start = ((), (), s32[]{:S(2)}) async-start(), calls=%async_computation.8 | async-start | bytes 5242880 | tf_op jit(solution)/shard_map/all_gather | solution.py:508
  94.9 189.1 %all-gather.6.cloned.1.call-start = ((), (), s32[]{:S(2)}) async-start(), calls=%async_computation.4 | async-start | bytes 5242880 | tf_op jit(solution)/shard_map/all_gather | solution.py:501
  117.6 223.2 %all-gather.10.cloned.1.call-start = ((), (), s32[]{:S(2)}) async-start(), calls=%async_computation.6 | async-start | bytes 9437184 | tf_op jit(solution)/shard_map/all_gather | solution.py:493
  123.1 343.5 %reduce-scatter.9.cloned.1.call-start = ((), (), s32[]{:S(2)}) async-start(), calls=%async_computation.9 | async-start | bytes 5242880 | tf_op jit(solution)/shard_map/reduce_scatter | solution.py:526
  340.8 13.5 %copy-start.14 = (bf16[4,256,2048]{2,1,0:T(8,128)(2,1)S(1)}, bf16[4,256,2048]{2,1,0:T(8,128)(2,1)}, u32[]{:S(2)}) copy-start(bf16[4,256,2048]{2,1,0:T(8,128)(2,1)} %get-tuple-element.43) | copy-start | bytes 12582916
  358.5 7.4 copy-start.15
  359.6 6.3 copy-start.11
  359.6 6.3 copy-start.13
  375.7 7.6 copy-start.33
  375.7 13.8 %copy-start.31 = (bf16[1024,1024]{1,0:T(8,128)(2,1)}, bf16[1024,1024]{1,0:T(8,128)(2,1)S(1)}, u32[]{:S(2)}) copy-start(bf16[1024,1024]{1,0:T(8,128)(2,1)S(1)} %get-tuple-element.78) | copy-start | bytes 6291460
  389.4 157.4 %reduce-scatter.7.cloned.1.call-start = ((), (), s32[]{:S(2)}) async-start(), calls=%async_computation.7 | async-start | bytes 5242880 | tf_op jit(solution)/shard_map/reduce_scatter | solution.py:518
  397.7 149.1 %copy-start.4 = (bf16[256,2048]{1,0:T(8,128)(2,1)S(1)}, bf16[256,2048]{1,0:T(8,128)(2,1)}, u32[]{:S(2)}) copy-start(bf16[256,2048]{1,0:T(8,128)(2,1)} %x_hbm.1) | copy-start | bytes 3145732
  397.7 235.5 %all-gather.14.cloned.1.call-start = ((), (), s32[]{:S(2)}) async-start(), calls=%async_computation.10 | async-start | bytes 5242880 | tf_op jit(solution)/shard_map/all_gather | solution.py:550
  550.6 13.2 %copy-start.3 = (f32[256,2048]{1,0:T(8,128)}, f32[256,2048]{1,0:T(8,128)S(1)}, u32[]{:S(2)}) copy-start(f32[256,2048]{1,0:T(8,128)S(1)} %get-tuple-element.76) | copy-start | bytes 6291460
  554.3 257.4 %all-reduce.9.cloned.1.call-start = ((), (), s32[]{:S(2)}) async-start(), calls=%async_computation.14 | async-start | bytes 25165824 | tf_op jit(solution)/shard_map/psum | solution.py:533
  563.8 6.4 copy-start.34
  578.5 6.4 copy-start.32
  593.2 351.2 %all-reduce.7.cloned.1.call-start = ((), (), s32[]{:S(2)}) async-start(), calls=%async_computation.13 | async-start | bytes 16777216 | tf_op jit(solution)/shard_map/psum | solution.py:603
  639.5 35.9 %copy-start.2 = (f32[4,256,512]{2,1,0:T(8,128)S(1)}, f32[4,256,512]{2,1,0:T(8,128)}, u32[]{:S(2)}) copy-start(f32[4,256,512]{2,1,0:T(8,128)} %get-tuple-element.36) | copy-start | bytes 6291460
  679.6 5.9 copy-start.25
  679.6 9.6 copy-start.23
  679.6 5.9 copy-start.29
  811.7 211.9 %reduce-scatter.11.cloned.1.call-start = ((), (), s32[]{:S(2)}) async-start(), calls=%async_computation.11 | async-start | bytes 5242880 | tf_op jit(solution)/shard_map/reduce_scatter | solution.py:576
  817.0 5.8 copy-start.8
  831.1 221.7 %reduce-scatter.13.cloned.1.call-start = ((), (), s32[]{:S(2)}) async-start(), calls=%async_computation.12 | async-start | bytes 1310720
  831.8 6.6 copy-start.10
  954.1 69.5 %copy-start.26 = (f32[4,1,512]{2,1,0:T(1,128)S(1)}, f32[4,1,512]{2,1,0:T(1,128)}, u32[]{:S(2)}) copy-start(f32[4,1,512]{2,1,0:T(1,128)} %get-tuple-element.86) | copy-start | bytes 24580
  1027.1 27.1 %copy-start.28 = (f32[2,512]{1,0:T(2,128)S(1)}, f32[2,512]{1,0:T(2,128)}, u32[]{:S(2)}) copy-start(f32[2,512]{1,0:T(2,128)} %get-tuple-element.57) | copy-start | bytes 12292
  1027.1 40.8 %copy-start.1 = (bf16[2048,512]{1,0:T(8,128)(2,1)S(1)}, bf16[2048,512]{1,0:T(8,128)(2,1)}, u32[]{:S(2)}) copy-start(bf16[2048,512]{1,0:T(8,128)(2,1)} %param.21) | copy-start | bytes 6291460
  (14 other events, 51.9 us)
Sparse Core Ops, SparseCore 0:
  94.3 28.7 all-gather.7
  124.6 77.8 all-gather.11
  204.7 79.2 all-gather.5
  285.7 55.0 all-gather.9
  389.5 77.0 reduce-scatter.8
  469.5 77.2 reduce-scatter.6
  554.4 78.8 all-gather.13
  637.8 173.8 all-reduce.8
  816.6 127.6 all-reduce.6
  946.5 77.0 reduce-scatter.10
  1027.2 25.5 reduce-scatter.12

commit v3 on v2

--- a/solution.py
+++ b/solution.py
@@ -275,6 +275,7 @@
         compiler_params=pltpu.CompilerParams(
             collective_id=0, has_side_effects=True, vmem_limit_bytes=VMEM_LIMIT
         ),
+        cost_estimate=pl.CostEstimate(flops=80 * 10**9, bytes_accessed=32 * 2**20, transcendentals=0),
         name="gather_project",
     )(tokens, small, wq, wk, wv)
 
@@ -338,6 +339,7 @@
             out_specs=[head] * 3,
         ),
         compiler_params=pltpu.CompilerParams(vmem_limit_bytes=VMEM_LIMIT),
+        cost_estimate=pl.CostEstimate(flops=14 * 10**9, bytes_accessed=16 * 2**20, transcendentals=0),
         name="attention",
     )(prefix, q_raw, k_raw, values, factors, cosine, sine, gains)
 
@@ -430,8 +432,615 @@
             ],
         ),
         compiler_params=pltpu.CompilerParams(vmem_limit_bytes=VMEM_LIMIT),
+        cost_estimate=pl.CostEstimate(flops=2 * 10**9, bytes_accessed=2**20, transcendentals=0),
         name="attention_back",
     )(prefix, q, k, v, g, q_raw, k_raw, factors, cosine, sine, gains)
+
+
+def scatter_norm_kernel(n, steps, gather, plain, *refs):
+    part, refs = refs[0], refs[1:]
+    if not plain:
+        base, addend, gain = refs[:3]
+        refs = refs[3:]
+    if gather:
+        out, all_out, gain_out = refs[:3]
+        refs = refs[3:]
+        alls, ag_up, ag_down, ag_recv, all_sem = refs[:5]
+        refs = refs[5:]
+    elif plain:
+        out, refs = refs[0], refs[1:]
+    else:
+        out, gain_out = refs[:2]
+        refs = refs[2:]
+    from_below, from_above, gain_acc, up_send, up_recv, down_send, down_recv = refs
+    R, D = part.shape[2:]
+    d, z, peers = others(n)
+    upper, lower = (d, lax.rem(z + 1, n)), (d, lax.rem(z + n - 1, n))
+    greet(peers)
+    gain_acc[...] = jnp.zeros_like(gain_acc)
+
+    def move_up(src, o, k):
+        return pltpu.make_async_remote_copy(
+            src_ref=src.at[o, k], dst_ref=from_below.at[o, k], send_sem=up_send.at[o, k],
+            recv_sem=up_recv.at[o, k], device_id=upper, device_id_type=MESH,
+        )
+
+    def move_down(src, o, k):
+        return pltpu.make_async_remote_copy(
+            src_ref=src.at[o, k], dst_ref=from_above.at[o, k], send_sem=down_send.at[o, k],
+            recv_sem=down_recv.at[o, k], device_id=lower, device_id_type=MESH,
+        )
+
+    def all_up(o, k):
+        return pltpu.make_async_remote_copy(
+            src_ref=alls.at[o, k], dst_ref=alls.at[o, k], send_sem=ag_up.at[o, k],
+            recv_sem=ag_recv.at[o, k], device_id=upper, device_id_type=MESH,
+        )
+
+    def all_down(o, k):
+        return pltpu.make_async_remote_copy(
+            src_ref=alls.at[o, k], dst_ref=alls.at[o, k], send_sem=ag_down.at[o, k],
+            recv_sem=ag_recv.at[o, k], device_id=lower, device_id_type=MESH,
+        )
+
+    def pass_up(k):
+        def far(i, carry):
+            o = z + n - 1 - i
+
+            @pl.when(o < n)
+            def _():
+                @pl.when(z == 0)
+                def _():
+                    move_up(part, o, k).start()
+
+                @pl.when(z > 0)
+                def _():
+                    move_up(part, o, k).wait_recv()
+                    both = from_below[o, k].astype(f32) + part[o, k].astype(f32)
+                    from_below[o, k] = both.astype(bf16)
+                    move_up(from_below, o, k).start()
+
+            return carry
+
+        lax.fori_loop(0, n - 1, far, 0)
+
+    def pass_down(k):
+        def far(i, carry):
+            o = z - n + 1 + i
+
+            @pl.when(o >= 0)
+            def _():
+                @pl.when(z == n - 1)
+                def _():
+                    move_down(part, o, k).start()
+
+                @pl.when(z < n - 1)
+                def _():
+                    move_down(part, o, k).wait_recv()
+                    both = from_above[o, k].astype(f32) + part[o, k].astype(f32)
+                    from_above[o, k] = both.astype(bf16)
+                    move_down(from_above, o, k).start()
+
+            return carry
+
+        lax.fori_loop(0, n - 1, far, 0)
+
+    def own(k):
+        @pl.when(z > 0)
+        def _():
+            move_up(part, z, k).wait_recv()
+
+        @pl.when(z == 0)
+        def _():
+            from_below[z, k] = jnp.zeros((R, D), bf16)
+
+        @pl.when(z < n - 1)
+        def _():
+            move_down(part, z, k).wait_recv()
+
+        @pl.when(z == n - 1)
+        def _():
+            from_above[z, k] = jnp.zeros((R, D), bf16)
+
+        total = (
+            part[z, k].astype(f32) + from_below[z, k].astype(f32) + from_above[z, k].astype(f32)
+        )
+        if plain:
+            out[k] = total
+            return
+        rows = base[k].astype(f32)
+        factor = lax.rsqrt(jnp.sum(rows * rows, axis=1, keepdims=True) / D + EPSILON)
+        unit = rows * factor
+        along = total * unit
+        gain_acc[...] += jnp.sum(along.reshape(R // 8, 8, D), axis=0)
+        weighted = along * gain[...]
+        mean = jnp.sum(weighted, axis=1, keepdims=True) / D
+        result = addend[k].astype(f32) + factor * (total * gain[...] - unit * mean)
+        out[k] = result
+        if gather:
+            alls[z, k] = result.astype(bf16)
+
+            @pl.when(z < n - 1)
+            def _():
+                all_up(z, k).start()
+
+            @pl.when(z > 0)
+            def _():
+                all_down(z, k).start()
+
+    def forward(own_k):
+        def hop(s, carry):
+            below, above, k = z - s, z + s, own_k - s
+            live = (k >= 0) & (k < steps)
+
+            @pl.when(live & (below >= 0))
+            def _():
+                all_up(below, k).wait_recv()
+
+                @pl.when(z < n - 1)
+                def _():
+                    all_up(below, k).start()
+
+            @pl.when(live & (above < n))
+            def _():
+                all_down(above, k).wait_recv()
+
+                @pl.when(z > 0)
+                def _():
+                    all_down(above, k).start()
+
+            return carry
+
+        lax.fori_loop(1, n, hop, 0)
+
+    def turn(t, carry):
+        up_k, down_k, own_k = t - z, t - (n - 1 - z), t - (n - 1)
+
+        @pl.when((up_k >= 0) & (up_k < steps))
+        def _():
+            pass_up(up_k)
+
+        @pl.when((down_k >= 0) & (down_k < steps))
+        def _():
+            pass_down(down_k)
+
+        @pl.when((own_k >= 0) & (own_k < steps))
+        def _():
+            own(own_k)
+
+        if gather:
+            forward(own_k)
+
+        return carry
+
+    lax.fori_loop(0, steps + (2 * n - 2 if gather else n - 1), turn, 0)
+    if not plain:
+        gain_out[...] = gain_acc[...]
+
+    def drain(i, carry):
+        o, k = i // steps, i % steps
+
+        @pl.when(o > z)
+        def _():
+            move_up(part, o, k).wait_send()
+
+        @pl.when(o < z)
+        def _():
+            move_down(part, o, k).wait_send()
+
+        if gather:
+
+            @pl.when((z < n - 1) & (o <= z))
+            def _():
+                all_up(o, k).wait_send()
+
+            @pl.when((z > 0) & (o >= z))
+            def _():
+                all_down(o, k).wait_send()
+
+        return carry
+
+    lax.fori_loop(0, n * steps, drain, 0)
+    if gather:
+        copies = [pltpu.make_async_copy(alls.at[o], all_out.at[o], all_sem.at[o]) for o in range(n)]
+        for copy in copies:
+            copy.start()
+        for copy in copies:
+            copy.wait()
+
+
+def scatter_norm(n, steps, gather, part, base, addend, gain, collective_id, plain=False):
+    T, D = part.shape[0] // n, part.shape[1]
+    R = T // steps
+    hbm = pl.BlockSpec(memory_space=pl.ANY)
+    vmem = pl.BlockSpec(memory_space=pltpu.VMEM)
+    dma = pltpu.SemaphoreType.DMA
+    slots = pltpu.VMEM((n, steps, R, D), bf16)
+    rows = jax.ShapeDtypeStruct((steps, R, D), f32)
+    gains = jax.ShapeDtypeStruct((8, D), f32)
+    sems = dma((n, steps))
+    results = pl.pallas_call(
+        functools.partial(scatter_norm_kernel, n, steps, gather, plain),
+        out_shape=[rows]
+        + ([jax.ShapeDtypeStruct((n, steps, R, D), bf16)] if gather else [])
+        + ([] if plain else [gains]),
+        in_specs=[vmem] * (1 if plain else 4),
+        out_specs=[vmem] + ([hbm] if gather else []) + ([] if plain else [vmem]),
+        scratch_shapes=([slots, sems, sems, sems, dma((n,))] if gather else [])
+        + [slots, slots, pltpu.VMEM((8, D), f32), sems, sems, sems, sems],
+        compiler_params=pltpu.CompilerParams(
+            collective_id=collective_id, has_side_effects=True, vmem_limit_bytes=VMEM_LIMIT
+        ),
+        cost_estimate=pl.CostEstimate(
+            flops=10**9, bytes_accessed=2**20, transcendentals=0
+        ),
+        name="scatter_norm_gather" if gather else "scatter_norm",
+    )(
+        part.reshape(n, steps, R, D),
+        *(
+            ()
+            if plain
+            else (base.reshape(steps, R, D), addend.reshape(steps, R, D), gain)
+        ),
+    )
+    if plain:
+        return results[0].reshape(T, D)
+    if gather:
+        out, alls, gains = results
+        return out.reshape(T, D), alls.reshape(n * T, D), gains
+    out, gains = results
+    return out.reshape(T, D), gains
+
+
+def gather_mix_kernel(
+    n, mixed_hbm, weight_hbm, x_ref, gain, mixed_out, in_out, own_out,
+    ms, acc, weight, load_sem, up_sem, down_sem, recv_sem, out_sem,
+):
+    L, C = ms.shape[1:]
+    D = weight.shape[1]
+    T = own_out.shape[0]
+    d, z, peers = others(n)
+    own_load = pltpu.make_async_copy(mixed_hbm, ms.at[z], load_sem.at[0])
+    own_load.start()
+    weight_load = pltpu.make_async_copy(weight_hbm, weight, load_sem.at[1])
+    weight_load.start()
+    greet(peers)
+
+    def send_up(o):
+        return pltpu.make_async_remote_copy(
+            src_ref=ms.at[o], dst_ref=ms.at[o], send_sem=up_sem.at[o], recv_sem=recv_sem.at[o],
+            device_id=(d, lax.rem(z + 1, n)), device_id_type=MESH,
+        )
+
+    def send_down(o):
+        return pltpu.make_async_remote_copy(
+            src_ref=ms.at[o], dst_ref=ms.at[o], send_sem=down_sem.at[o], recv_sem=recv_sem.at[o],
+            device_id=(d, lax.rem(z + n - 1, n)), device_id_type=MESH,
+        )
+
+    own_load.wait()
+
+    @pl.when(z < n - 1)
+    def _():
+        send_up(z).start()
+
+    @pl.when(z > 0)
+    def _():
+        send_down(z).start()
+
+    weight_load.wait()
+    block = 256
+
+    def add(o, first):
+        w = weight[pl.ds(pl.multiple_of(o * C, C), C), :]
+
+        def rows(i, carry):
+            r = pl.ds(pl.multiple_of(i * block, block), block)
+            new = jnp.dot(ms[o, r, :], w, preferred_element_type=f32)
+            acc[r, :] = new if first else acc[r, :] + new
+            return carry
+
+        lax.fori_loop(0, L // block, rows, 0)
+
+    def save(o):
+        return pltpu.make_async_copy(ms.at[o], mixed_out.at[o], out_sem.at[o])
+
+    add(z, True)
+    save(z).start()
+
+    def step(s, carry):
+        below, above = z - s, z + s
+
+        @pl.when(below >= 0)
+        def _():
+            send_up(below).wait_recv()
+
+            @pl.when(z < n - 1)
+            def _():
+                send_up(below).start()
+
+        @pl.when(above < n)
+        def _():
+            send_down(above).wait_recv()
+
+            @pl.when(z > 0)
+            def _():
+                send_down(above).start()
+
+        def side(j, inner):
+            o = z - s + 2 * s * j
+
+            @pl.when((o >= 0) & (o < n))
+            def _():
+                add(o, False)
+                save(o).start()
+
+            return inner
+
+        lax.fori_loop(0, 2, side, 0)
+        return carry
+
+    lax.fori_loop(1, n, step, 0)
+    own_rows = pl.ds(pl.multiple_of(z * T, T), T)
+    own_out[...] = acc[own_rows, :]
+    part = 32
+
+    def norm_rows(i, carry):
+        r = pl.ds(pl.multiple_of(i * part, part), part)
+        v = acc[r, :] + x_ref[r, :].astype(f32)
+        factor = lax.rsqrt(jnp.sum(v * v, axis=1, keepdims=True) / D + EPSILON)
+        in_out[r, :] = (v * factor * gain[...]).astype(bf16)
+        return carry
+
+    lax.fori_loop(0, L // part, norm_rows, 0)
+
+    def finish(o, carry):
+        save(o).wait()
+
+        @pl.when((z < n - 1) & (o <= z))
+        def _():
+            send_up(o).wait_send()
+
+        @pl.when((z > 0) & (o >= z))
+        def _():
+            send_down(o).wait_send()
+
+        return carry
+
+    lax.fori_loop(0, n, finish, 0)
+
+
+def gather_mix(n, mixed, weight, x_all, gain, rows):
+    L, C = mixed.shape
+    D = weight.shape[1]
+    hbm = pl.BlockSpec(memory_space=pl.ANY)
+    vmem = pl.BlockSpec(memory_space=pltpu.VMEM)
+    dma = pltpu.SemaphoreType.DMA
+    return pl.pallas_call(
+        functools.partial(gather_mix_kernel, n),
+        out_shape=[
+            jax.ShapeDtypeStruct((n, L, C), bf16),
+            jax.ShapeDtypeStruct((L, D), bf16),
+            jax.ShapeDtypeStruct((rows, D), f32),
+        ],
+        in_specs=[hbm, hbm, vmem, vmem],
+        out_specs=[hbm, vmem, vmem],
+        scratch_shapes=[
+            pltpu.VMEM((n, L, C), bf16),
+            pltpu.VMEM((L, D), f32),
+            pltpu.VMEM((D, D), bf16),
+            dma((2,)),
+            dma((n,)),
+            dma((n,)),
+            dma((n,)),
+            dma((n,)),
+        ],
+        compiler_params=pltpu.CompilerParams(
+            collective_id=1, has_side_effects=True, vmem_limit_bytes=VMEM_LIMIT
+        ),
+        cost_estimate=pl.CostEstimate(flops=100 * 10**9, bytes_accessed=32 * 2**20, transcendentals=0),
+        name="gather_mix",
+    )(mixed, weight, x_all, gain)
+
+
+def experts_kernel(
+    x_ref, g_ref, combine, gate_w, up_w, down_w,
+    sum_out, in_out, hidden_out, gate_out, up_out, sum_acc, in_acc,
+):
+    e = pl.program_id(1)
+    last = pl.num_programs(1) - 1
+    x, g = x_ref[...], g_ref[...]
+    gate_m, up_m, down_m = gate_w[0], up_w[0], down_w[0]
+    lane = lax.broadcasted_iota(jnp.int32, combine.shape, 1)
+    weight = jnp.sum(jnp.where(lane == e, combine[...], 0.0), axis=1, keepdims=True)
+    gate_part = dot(x, gate_m)
+    up_part = dot(x, up_m)
+    hidden_grad = dot_nt(g, down_m) * weight
+    sig = jax.nn.sigmoid(gate_part)
+    silu = gate_part * sig
+    hidden = (silu * up_part * weight).astype(bf16)
+    hidden_out[...] = hidden
+    up_grad = (hidden_grad * silu).astype(bf16)
+    up_out[...] = up_grad
+    gate_grad = (hidden_grad * up_part * sig * (1.0 + gate_part * (1.0 - sig))).astype(bf16)
+    gate_out[...] = gate_grad
+    made = dot(hidden, down_m)
+    back = dot_nt(gate_grad, gate_m) + dot_nt(up_grad, up_m)
+
+    @pl.when(e == 0)
+    def _():
+        sum_acc[...] = made
+        in_acc[...] = back
+
+    @pl.when((e > 0) & (e < last))
+    def _():
+        sum_acc[...] += made
+        in_acc[...] += back
+
+    @pl.when((e > 0) & (e == last))
+    def _():
+        sum_out[...] = (sum_acc[...] + made).astype(bf16)
+        in_out[...] = (in_acc[...] + back).astype(bf16)
+
+    @pl.when((e == 0) & (e == last))
+    def _():
+        sum_out[...] = made.astype(bf16)
+        in_out[...] = back.astype(bf16)
+
+
+def experts_pass(x, g, combine, gate_w, up_w, down_w):
+    L, D = x.shape
+    E, _, F = gate_w.shape
+    block = min(512, L)
+    rows = pl.BlockSpec((block, D), lambda i, e: (i, 0))
+    units = pl.BlockSpec((block, F), lambda i, e: (i, e))
+    column = pl.BlockSpec((1, D, F), lambda i, e: (e, 0, 0))
+    wide = jax.ShapeDtypeStruct((L, D), bf16)
+    narrow = jax.ShapeDtypeStruct((L, E * F), bf16)
+    return pl.pallas_call(
+        experts_kernel,
+        out_shape=[wide, wide, narrow, narrow, narrow],
+        grid=(L // block, E),
+        in_specs=[
+            rows, rows, pl.BlockSpec((block, combine.shape[1]), lambda i, e: (i, 0)),
+            column, column, pl.BlockSpec((1, F, D), lambda i, e: (e, 0, 0)),
+        ],
+        out_specs=[rows, rows, units, units, units],
+        scratch_shapes=[pltpu.VMEM((block, D), f32), pltpu.VMEM((block, D), f32)],
+        compiler_params=pltpu.CompilerParams(vmem_limit_bytes=VMEM_LIMIT),
+        cost_estimate=pl.CostEstimate(
+            flops=12 * L * D * E * F, bytes_accessed=40 * 2**20, transcendentals=L * E * F
+        ),
+        name="experts_pass",
+    )(x, g, combine, gate_w, up_w, down_w)
+
+
+def expert_grads_kernel(x_ref, g_ref, hidden, gate_grad, up_grad, gate_out, up_out, down_out, xt):
+    @pl.when(pl.program_id(0) == 0)
+    def _():
+        xt[...] = x_ref[...].T
+
+    gate_out[0] = dot(xt[...], gate_grad[...]).astype(bf16)
+    up_out[0] = dot(xt[...], up_grad[...]).astype(bf16)
+    down_out[0] = dot_tn(hidden[...], g_ref[...]).astype(bf16)
+
+
+def expert_grads(x, g, hidden, gate_grad, up_grad, experts):
+    L, D = x.shape
+    F = hidden.shape[1] // experts
+    whole = pl.BlockSpec((L, D), lambda e: (0, 0))
+    units = pl.BlockSpec((L, F), lambda e: (0, e))
+    column = pl.BlockSpec((1, D, F), lambda e: (e, 0, 0))
+    grad = jax.ShapeDtypeStruct((experts, D, F), bf16)
+    return pl.pallas_call(
+        expert_grads_kernel,
+        out_shape=[grad, grad, jax.ShapeDtypeStruct((experts, F, D), bf16)],
+        grid=(experts,),
+        in_specs=[whole, whole, units, units, units],
+        out_specs=[column, column, pl.BlockSpec((1, F, D), lambda e: (e, 0, 0))],
+        scratch_shapes=[pltpu.VMEM((D, L), bf16)],
+        compiler_params=pltpu.CompilerParams(vmem_limit_bytes=VMEM_LIMIT),
+        cost_estimate=pl.CostEstimate(
+            flops=6 * L * D * experts * F, bytes_accessed=26 * 2**20, transcendentals=0
+        ),
+        name="expert_grads",
+    )(x, g, hidden, gate_grad, up_grad)
+
+
+def gather_line_kernel(n, v_hbm, out, slots, load_sem, up_sem, down_sem, recv_sem, out_sem):
+    d, z, peers = others(n)
+    own_load = pltpu.make_async_copy(v_hbm, slots.at[z], load_sem.at[0])
+    own_load.start()
+    greet(peers)
+
+    def send_up(o):
+        return pltpu.make_async_remote_copy(
+            src_ref=slots.at[o], dst_ref=slots.at[o], send_sem=up_sem.at[o],
+            recv_sem=recv_sem.at[o], device_id=(d, lax.rem(z + 1, n)), device_id_type=MESH,
+        )
+
+    def send_down(o):
+        return pltpu.make_async_remote_copy(
+            src_ref=slots.at[o], dst_ref=slots.at[o], send_sem=down_sem.at[o],
+            recv_sem=recv_sem.at[o], device_id=(d, lax.rem(z + n - 1, n)), device_id_type=MESH,
+        )
+
+    own_load.wait()
+
+    @pl.when(z < n - 1)
+    def _():
+        send_up(z).start()
+
+    @pl.when(z > 0)
+    def _():
+        send_down(z).start()
+
+    def save(o):
+        return pltpu.make_async_copy(slots.at[o], out.at[o], out_sem.at[o])
+
+    save(z).start()
+
+    def step(s, carry):
+        below, above = z - s, z + s
+
+        @pl.when(below >= 0)
+        def _():
+            send_up(below).wait_recv()
+
+            @pl.when(z < n - 1)
+            def _():
+                send_up(below).start()
+
+            save(below).start()
+
+        @pl.when(above < n)
+        def _():
+            send_down(above).wait_recv()
+
+            @pl.when(z > 0)
+            def _():
+                send_down(above).start()
+
+            save(above).start()
+
+        return carry
+
+    lax.fori_loop(1, n, step, 0)
+
+    def finish(o, carry):
+        save(o).wait()
+
+        @pl.when((z < n - 1) & (o <= z))
+        def _():
+            send_up(o).wait_send()
+
+        @pl.when((z > 0) & (o >= z))
+        def _():
+            send_down(o).wait_send()
+
+        return carry
+
+    lax.fori_loop(0, n, finish, 0)
+
+
+def gather_line(n, v, collective_id):
+    hbm = pl.BlockSpec(memory_space=pl.ANY)
+    dma = pltpu.SemaphoreType.DMA
+    return pl.pallas_call(
+        functools.partial(gather_line_kernel, n),
+        out_shape=jax.ShapeDtypeStruct((n,) + v.shape, v.dtype),
+        in_specs=[hbm],
+        out_specs=hbm,
+        scratch_shapes=[
+            pltpu.VMEM((n,) + v.shape, v.dtype), dma((1,)), dma((n,)), dma((n,)), dma((n,)),
+            dma((n,)),
+        ],
+        compiler_params=pltpu.CompilerParams(
+            collective_id=collective_id, has_side_effects=True, vmem_limit_bytes=VMEM_LIMIT
+        ),
+        cost_estimate=pl.CostEstimate(flops=20 * 10**9, bytes_accessed=2 * 2**20, transcendentals=0),
+        name="gather_line",
+    )(v)
 
 
 def per_device(
@@ -485,79 +1094,49 @@
     gain_expert = small_all[:, 1, rows:].reshape(width)
     head_gains = own_gains[1:3]
     slab = width // groups
-    output_weight, out_grad_b, squares = lax.optimization_barrier(
-        (output_weight, out_grad, squares)
-    )
+    out_grad_b, squares = lax.optimization_barrier((out_grad, squares))
     out_slab = lax.dynamic_slice_in_dim(output_weight, group * slab, slab, 0)
-    out_slab = lax.all_gather(out_slab, "shard", axis=1, tiled=True)
+    out_slab = gather_line(shards, out_slab, 4).transpose(1, 0, 2).reshape(slab, width)
     full_output = lax.all_gather(out_slab, "dp", axis=0, tiled=True)
 
-    x_all = x_all_b.astype(f32)
     factors = lax.rsqrt(squares[:, :2].transpose(0, 2, 1).reshape(length, 2) / width + EPSILON)
     cosine, sine = rotary_tables(length)
     queries, keys, mixed_own = attention(
         prefix, query_raw, key_raw, values, factors, cosine, sine, head_gains
     )
-    mixed_all = lax.all_gather(mixed_own, "shard", axis=1, tiled=True)
-
-    attended = dot(mixed_all, full_output)
-    residual = x_all + attended
-    factor_res = row_factor(residual)
-    expert_in = (residual * factor_res * gain_expert).astype(bf16)
+    mixed_all, expert_in, attended_own = gather_mix(
+        shards, mixed_own, full_output, x_all_b, gain_expert[None, :], rows
+    )
 
     g_all = lax.all_gather(out_grad_b, "shard", axis=0, tiled=True)
-    gate_flat = expert_gate.transpose(1, 0, 2).reshape(width, experts * units)
-    up_flat = expert_up.transpose(1, 0, 2).reshape(width, experts * units)
-    down_flat = expert_down.reshape(experts * units, width)
-    gate_part = dot(expert_in, gate_flat)
-    up_part = dot(expert_in, up_flat)
-    sig = jax.nn.sigmoid(gate_part)
-    wide = jnp.repeat(combine, units, axis=1)
-    hidden = (gate_part * sig * up_part * wide).astype(bf16)
-    sum_part = dot(hidden, down_flat)
-    expert_sum = lax.psum_scatter(
-        sum_part.astype(bf16), "shard", scatter_dimension=0, tiled=True
-    ).astype(f32)
-
-    hidden_grad = dot_nt(g_all, down_flat) * wide
-    up_grad = (hidden_grad * gate_part * sig).astype(bf16)
-    gate_grad = (hidden_grad * up_part * sig * (1.0 + gate_part * (1.0 - sig))).astype(bf16)
-    in_part = dot_nt(gate_grad, gate_flat) + dot_nt(up_grad, up_flat)
-    in_grad = lax.psum_scatter(
-        in_part.astype(bf16), "shard", scatter_dimension=0, tiled=True
-    ).astype(f32)
-    grad_down = dot_tn(hidden, g_all).reshape(experts, units, width)
-    grad_gate = dot_tn(expert_in, gate_grad).reshape(width, experts, units).transpose(1, 0, 2)
-    grad_up = dot_tn(expert_in, up_grad).reshape(width, experts, units).transpose(1, 0, 2)
-
-    grad_gate, grad_up, grad_down = lax.psum(
-        (grad_gate.astype(bf16), grad_up.astype(bf16), grad_down.astype(bf16)), "dp"
-    )
-
-    def own_rows(v):
-        return lax.dynamic_slice_in_dim(v, place * rows, rows, 0)
+    sum_part, in_part, hidden, gate_grad, up_grad = experts_pass(
+        expert_in, g_all, combine, expert_gate, expert_up, expert_down
+    )
+    grad_gate, grad_up, grad_down = expert_grads(
+        expert_in, g_all, hidden, gate_grad, up_grad, experts
+    )
+    in_part, grad_gate, grad_up, grad_down = lax.optimization_barrier(
+        (in_part, grad_gate, grad_up, grad_down)
+    )
+    grad_gate, grad_up, grad_down = lax.psum((grad_gate, grad_up, grad_down), "dp")
 
     x_own = tokens.astype(f32)
-    g_own = out_grad.astype(f32)
-    attended_own = own_rows(attended)
     residual_own = x_own + attended_own
-    output = residual_own + expert_sum
-    root_means = jnp.stack([root_mean(attended_own), root_mean(expert_sum), root_mean(output)])
-    factor_own = own_rows(factor_res)
-    unit_res = residual_own * factor_own
-    gain_grad_res = jnp.sum(in_grad * unit_res, axis=0)
-    residual_grad = g_own + norm_back(in_grad * gain_expert, unit_res, factor_own)
-    attended_grad = lax.all_gather(residual_grad.astype(bf16), "shard", axis=0, tiled=True)
-
-    grad_output = dot_tn(
-        mixed_all, lax.dynamic_slice_in_dim(attended_grad, place * local, local, 1)
-    )
+    residual_grad, attended_grad, gain_grad_res = scatter_norm(
+        shards, 16, True, in_part, residual_own, out_grad, gain_expert[None, :], 2
+    )
+
+    own_columns = lax.dynamic_slice_in_dim(attended_grad, place * local, local, 1)
+    grad_output = jnp.concatenate([dot_tn(mixed_all[s], own_columns) for s in range(shards)], 0)
     mixed_grad = dot_nt(
         attended_grad, lax.dynamic_slice_in_dim(full_output, place * local, local, 0)
     ).astype(bf16)
     query_norm_grad, key_norm_grad, value_raw_grad, gain_grad_heads, inner = attention_back(
         prefix, queries, keys, values, mixed_grad, query_raw, key_raw, factors, cosine, sine,
         head_gains,
+    )
+    inner, grad_gate, grad_up, grad_down = lax.optimization_barrier(
+        (inner, grad_gate, grad_up, grad_down)
     )
     inner = lax.psum(inner[:, :2], "shard") / width
     inner = inner.transpose(0, 2, 1).reshape(length, 2)
@@ -573,36 +1152,32 @@
         + dot_nt(key_raw_grad, key_weight)
         + dot_nt(value_raw_grad, value_weight)
     )
-    normed_grad = lax.psum_scatter(
-        normed_part.astype(bf16), "shard", scatter_dimension=0, tiled=True
-    ).astype(f32)
     grad_query = dot_tn(normed, query_raw_grad)
     grad_key = dot_tn(normed, key_raw_grad)
     grad_value = dot_tn(normed, value_raw_grad)
 
-    factor_x = row_factor(x_own)
-    unit_x = x_own * factor_x
-    gain_grad_x = jnp.sum(normed_grad * unit_x, axis=0)
-    grad_tokens = residual_grad + norm_back(normed_grad * gain_in, unit_x, factor_x)
-
-    gain_rows = lax.psum_scatter(
-        jnp.stack([gain_grad_x, gain_grad_res]), "shard", scatter_dimension=1, tiled=True
-    )
-    grad_gains = jnp.stack([gain_rows[0], gain_grad_heads[0], gain_grad_heads[1], gain_rows[1]])
-
-    (grad_query, grad_key, grad_value, grad_output), grad_gate, grad_up, grad_down = (
-        lax.optimization_barrier(
-            (
-                tuple(v.astype(bf16) for v in (grad_query, grad_key, grad_value, grad_output)),
-                grad_gate,
-                grad_up,
-                grad_down,
-            )
-        )
-    )
-    grad_query, grad_key, grad_value, grad_output = lax.psum(
-        (grad_query, grad_key, grad_value, grad_output), "dp"
-    )
+    attention_grads, normed_part = lax.optimization_barrier(
+        (
+            tuple(v.astype(bf16) for v in (grad_query, grad_key, grad_value, grad_output)),
+            normed_part.astype(bf16),
+        )
+    )
+    grad_query, grad_key, grad_value, grad_output = lax.psum(attention_grads, "dp")
+    grad_tokens, gain_grad_x = scatter_norm(
+        shards, 8, False, normed_part, tokens, residual_grad, gain_in[None, :], 3
+    )
+    sum_part, grad_tokens = lax.optimization_barrier((sum_part, grad_tokens))
+    expert_sum = scatter_norm(shards, 8, False, sum_part, None, None, None, 5, plain=True)
+    output = residual_own + expert_sum
+    root_means = jnp.stack([root_mean(attended_own), root_mean(expert_sum), root_mean(output)])
+    placed = lax.dynamic_update_slice(
+        jnp.zeros((2, width), f32), gain_grad_heads, (jnp.int32(0), place * local)
+    )
+    gain_rows = lax.psum(
+        jnp.concatenate([gain_grad_x.sum(0)[None], placed, gain_grad_res.sum(0)[None]], 0),
+        ("dp", "shard"),
+    )
+    grad_gains = lax.dynamic_slice_in_dim(gain_rows, place * local, local, 1)
 
     return (
         output.astype(bf16),
@@ -612,7 +1187,7 @@
         grad_key.astype(f32),
         grad_value.astype(f32),
         grad_output.astype(f32),
-        lax.psum(grad_gains, "dp"),
+        grad_gains,
         grad_gate.astype(f32),
         grad_up.astype(f32),
         grad_down.astype(f32),

time: 1090 us -> 805 us (0.74)
  waiting for transfers between devices: 679 us -> 8.54 us
  Pallas kernels: 123 us -> 605 us
  matrix products: 130 us -> 45.5 us
  local copies, waits for them, and re-layouts: 45.4 us -> 16.7 us
  blocking collectives: 25 us -> 50.9 us
    pallas_call x0 -> x7, Pallas kernels: none -> 484 us  [the longest x3 280 us: scatter_norm(): pl.pallas_call(functools.partial(scatter_norm_kernel, n, steps, gather, p...]
    reduce_scatter x3 -> x0, waiting for transfers between devices: 215 us -> none  [the longest x1 80.1 us: per_device(): lax.psum_scatter(sum_part.astype(bf16), 'shard', scatter_dimension=0, til...]
    psum x2, waiting for transfers between devices: 212 us -> 8.45 us  [the longest x1 8.45 us: per_device(): lax.psum((grad_gate, grad_up, grad_down), 'dp')]
    all_gather x3 -> x0, waiting for transfers between devices: 114 us -> none  [the longest x1 70.3 us: per_device(): mixed_all = lax.all_gather(mixed_own, 'shard', axis=1, tiled=True)]
    all_gather x1, waiting for transfers between devices: 59.9 us -> 0.02 us  [per_device(): g_all = lax.all_gather(out_grad_b, 'shard', axis=0, tiled=True)]
    all_gather x1, waiting for transfers between devices: 56.8 us -> 0.01 us  [per_device(): full_output = lax.all_gather(out_slab, 'dp', axis=0, tiled=True)]
    dot_general x4 -> x0, matrix products: 37.8 us -> none  [dot(): return jnp.dot(a, b, preferred_element_type=f32)]
    psum x1, blocking collectives: 13.6 us -> 41.9 us  [per_device(): lax.psum(jnp.concatenate([gain_grad_x.sum(0)[None], placed, gain_grad_res...]
  transfers between devices with their start and end apart: 11 -> 4, of which waited for: 11 -> 1; matrix products, arithmetic and copies ran while one was open for 15% -> 7% of each run, Pallas kernels for 4% -> 66%
where the time goes in v3:
time: 805 us; the launch traced here: 789 us
  Pallas kernels  605 us (75%)
  blocking collectives  50.9 us (6%)
  other arithmetic  47.1 us (6%)
  matrix products  45.5 us (6%)
  local copies, waits for them, and re-layouts  16.7 us (2%)
  between operations  15 us (2%)
  waiting for transfers between devices  8.54 us (1%)
    pallas_call x3, Pallas kernels, scatter_norm(): pl.pallas_call(functools.partial(scatter_norm_kernel, n, steps, gather, p...  280 us
    pallas_call x1, Pallas kernels, gather_mix(): pl.pallas_call(functools.partial(gather_mix_kernel, n), out_shape=[jax.Sh...  123 us
    pallas_call x1, Pallas kernels, gather_project(): pl.pallas_call(functools.partial(gather_project_kernel, n), out_shape=[ja...  81.6 us
    psum x1, blocking collectives, per_device(): lax.psum(jnp.concatenate([gain_grad_x.sum(0)[None], placed, gain_grad_res...  41.9 us
    pallas_call x1, Pallas kernels, experts_pass(): pl.pallas_call(experts_kernel, out_shape=[wide, wide, narrow, narrow, nar...  40 us
    dot_general x4, matrix products, dot_nt(): lax.dot_general(a, b, (((1,), (1,)), ((), ())), preferred_element_type=f32)  28.4 us
    pallas_call x1, Pallas kernels, attention_back(): pl.pallas_call(attention_back_kernel, out_shape=[wide, wide, jax.ShapeDty...  23.7 us
    pallas_call x1, Pallas kernels, gather_line(): pl.pallas_call(functools.partial(gather_line_kernel, n), out_shape=jax.Sh...  20.8 us
  transfers between devices with their start and end apart: 4, of which 1 were waited for; matrix products, arithmetic and copies ran while one was open for 7% of the time, Pallas kernels for 66%

profile of v3, /device:TPU:12, one launch (start us, length us, event | category | flops | bytes accessed | tf_op | source)
XLA Modules:
  0.0 789.3 jit_solution(2402036829285105158)
XLA Ops:
  9.5 20.8 %gather_line.1 = bf16[4,256,512]{2,1,0:T(8,128)(2,1)} custom-call(bf16[256,512]{1,0:T(8,128)(2,1)} %constant_dynamic-slice_fusion.1.v_hbm), custom_call_target="tpu_custom_call" | custom-call | flops 20000000000 | bytes 2097152 | tf_op jit(solution)/shard_map/gather_line/pallas_call | solution.py:1029
  30.3 2.3 copy.37
  33.4 81.6 %gather_project.1 = (bf16[4,256,2048]{2,1,0:T(8,128)(2,1)}, bf16[4,256,2048]{2,1,0:T(8,128)(2,1)}, f32[4,256,512]{2,1,0:T(8,128)}, f32[4,256,512]{2,1,0:T(8,128)...) custom-call(bf16[256,2048]{1,0:T(8,128)(2,1)} %x_hbm.1, ...), custom_call_target="tpu_custom_call" | custom-call | flops 80000000000 | bytes 33554432 | tf_op jit(solution)/shard_map/gather_project/pallas_call | solution.py:241
  125.4 15.7 %attention.1 = (bf16[1024,512]{1,0:T(8,128)(2,1)}, bf16[1024,512]{1,0:T(8,128)(2,1)}, bf16[1024,512]{1,0:T(8,128)(2,1)}) custom-call(s32[1]{0:T(128)S(6)} %copy.47.prefix, f32[1024,512]{1,0:T(8,128)} %bitcast.73, f32[1024,512]{1,0:T(8,128)} %bitcast.75, bf16[1024,512]{1,0:T(8,128)(2,1)} %bitcast.84, f32[1024,2]{1,0:T(8,128)} %bitcast.70, ...), custom_call_target="tpu_custom_call" | custom-call | flops 14000000000 | bytes 16777216 | tf_op jit(solution)/shard_map/attention/pallas_call | solution.py:329
  141.2 123.4 %gather_mix.1 = (bf16[4,1024,512]{2,1,0:T(8,128)(2,1)}, bf16[1024,2048]{1,0:T(8,128)(2,1)}, f32[256,2048]{1,0:T(8,128)}) custom-call(bf16[1024,512]{1,0:T(8,128)(2,1)} %get-tuple-element.64.mixed_hbm, bf16[2048,2048]{1,0:T(8,128)(2,1)} %all-gather.3.cloned.1.call-done.weight_hbm, bf16[1024,2048]{1,0:T(8,128)(2,1)} %bitcast.107, f32[1,2048]{1,0:T(1,128)} %bitcast.92), custom_call_target="tpu_custom_call" | custom-call | flops 99999997952 | bytes 33554432 | tf_op jit(solution)/shard_map/gather_mix/pallas_call | solution.py:819
  264.6 40.0 %experts_pass.1 = (bf16[1024,2048]{1,0:T(8,128)(2,1)}, bf16[1024,2048]{1,0:T(8,128)(2,1)}, bf16[1024,1024]{1,0:T(8,128)(2,1)}, bf16[1024,1024]{1,0:T(8,128)(2,1)}, bf16[1024,1024]{1,0:T(8,128)(2,1)}) custom-call(bf16[1024,2048]{1,0:T(8,128)(2,1)} %get-tuple-element.68.x_ref, bf16[1024,2048]{1,0:T(8,128)(2,1)} %all-gather.5.cloned.1.call-done.g_ref, ...), custom_call_target="tpu_custom_call" | custom-call | flops 25769803776 | bytes 41943040 | tf_op jit(solution)/shard_map/experts_pass/pallas_call | solution.py:900
  304.6 20.5 %expert_grads.1 = (bf16[4,2048,256]{2,1,0:T(8,128)(2,1)}, bf16[4,2048,256]{2,1,0:T(8,128)(2,1)}, bf16[4,256,2048]{2,1,0:T(8,128)(2,1)}) custom-call(bf16[1024,2048]{1,0:T(8,128)(2,1)} %get-tuple-element.68.x_ref, bf16[1024,2048]{1,0:T(8,128)(2,1)} %all-gather.5.cloned.1.call-done.g_ref, bf16[1024,1024]{1,0:T(8,128)(2,1)} %get-tuple-element.75.hidden, ...), custom_call_target="tpu_custom_call" | custom-call | flops 12884901888 | bytes 27262976 | tf_op jit(solution)/shard_map/expert_grads/pallas_call | solution.py:935
  326.7 3.2 multiply_reduce_fusion.2
  329.9 124.2 %scatter_norm_gather.1 = (f32[16,16,2048]{2,1,0:T(8,128)}, bf16[4,16,16,2048]{3,2,1,0:T(8,128)(2,1)}, f32[8,2048]{1,0:T(8,128)}) custom-call(bf16[4,16,16,2048]{3,2,1,0:T(8,128)(2,1)} %bitcast.78, f32[16,16,2048]{2,1,0:T(8,128)} %bitcast.68, bf16[16,16,2048]{2,1,0:T(8,128)(2,1)} %bitcast.80, f32[1,2048]{1,0:T(1,128)} %bitcast.93), custom_call_target="tpu_custom_call" | custom-call | flops 1000000000 | bytes 1048576 | tf_op jit(solution)/shard_map/scatter_norm_gather/pallas_call | solution.py:662
  454.1 6.7 fusion.2.g_ref
  460.8 23.7 %attention_back.1 = (f32[1024,512]{1,0:T(8,128)}, f32[1024,512]{1,0:T(8,128)}, bf16[1024,512]{1,0:T(8,128)(2,1)}, f32[2,512]{1,0:T(2,128)}, f32[4,8,256]{2,1,0:T(8,128)}) custom-call(s32[1]{0:T(128)S(6)} %copy.47.prefix, bf16[1024,512]{1,0:T(8,128)(2,1)} %get-tuple-element.72.q_ref, bf16[1024,512]{1,0:T(8,128)(2,1)} %get-tuple-element.73.k_ref, ...), custom_call_target="tpu_custom_call" | custom-call | flops 2000000000 | bytes 1048576 | tf_op jit(solution)/shard_map/attention_back/pallas_call | solution.py:417
  484.4 2.5 convolution_convert_fusion.6
  494.0 3.7 convolution_convert_fusion
  497.7 8.4 %all-reduce.9.cloned.1.call-done = (bf16[4,2048,256]{2,1,0:T(8,128)(2,1)}, bf16[4,2048,256]{2,1,0:T(8,128)(2,1)}, bf16[4,256,2048]{2,1,0:T(8,128)(2,1)}) async-done(((bf16[4,2048,256]{2,1,0:T(8,128)(2,1)}, bf16[4,2048,256]{2,1,0:T(8,128)(2,1)}, bf16[4,256,2048]{2,1,0:T(8,128)(2,1)}), (bf16[4,2048,256]{2,1,0:T(8,128)(2,1)}, bf16[4,2048,256]{2,1,0:T(8,128)(2,1)}, ...) | async-done | bytes 12582928 | tf_op jit(solution)/shard_map/psum | solution.py:1121
  506.9 9.0 %psum.66 = f32[4,2,256]{2,1,0:T(2,128)S(1)} all-reduce(f32[4,2,256]{2,1,0:T(2,128)S(1)} %slice.55), channel_id=1, replica_groups=mesh['dp'=8,'shard'=4] {'shard'}, use_global_device_ids=true, to_apply=%region_4.5 | all-reduce | flops 2048 | bytes 16384 | tf_op jit(solution)/shard_map/psum | solution.py:1141
  516.0 3.6 multiply_convert_fusion
  519.6 5.8 fusion.28
  525.3 3.7 convolution_convert_fusion.1
  529.0 5.8 fusion.27
  534.8 3.7 convolution_convert_fusion.2
  538.5 10.2 %add_convert_fusion = bf16[1024,2048]{1,0:T(8,128)(2,1)} fusion(f32[1024,2048]{1,0:T(8,128)} %fusion.27, f32[1024,2048]{1,0:T(8,128)} %fusion.28, bf16[1024,512]{1,0:T(8,128)(2,1)S(1)} %copy-done.13, bf16[2048,512]{1,0:T(8,128)(2,1)S(1)} %copy-done.8), kind=kOutput, calls=%fused_computation | convolution fusion | flops 2153775104 | bytes 24117248 | tf_op jit(solution)/shard_map/dot_general | solution.py:48
  549.6 80.6 %scatter_norm.2 = (f32[8,32,2048]{2,1,0:T(8,128)}, f32[8,2048]{1,0:T(8,128)}) custom-call(bf16[4,8,32,2048]{3,2,1,0:T(8,128)(2,1)} %bitcast.69, bf16[8,32,2048]{2,1,0:T(8,128)(2,1)} %bitcast.81, f32[8,32,2048]{2,1,0:T(8,128)} %bitcast.83, f32[1,2048]{1,0:T(1,128)} %bitcast.91), custom_call_target="tpu_custom_call" | custom-call | flops 1000000000 | bytes 1048576 | tf_op jit(solution)/shard_map/scatter_norm/pallas_call | solution.py:662
  631.0 74.9 %scatter_norm.3 = f32[8,32,2048]{2,1,0:T(8,128)} custom-call(bf16[4,8,32,2048]{3,2,1,0:T(8,128)(2,1)} %bitcast.77), custom_call_target="tpu_custom_call" | custom-call | flops 1000000000 | bytes 1048576 | tf_op jit(solution)/shard_map/scatter_norm/pallas_call | solution.py:662
  707.9 6.5 convert_element_type.84
  714.4 4.1 convert_element_type.85
  718.5 4.4 convert_element_type.86
  723.0 41.9 %psum.71 = f32[4,2048]{1,0:T(4,128)S(1)} all-reduce(f32[4,2048]{1,0:T(4,128)S(1)} %pad_maximum_fusion.3), channel_id=1, replica_groups=mesh['dp'=8,'shard'=4] {'dp','shard'}, use_global_device_ids=true, to_apply=%region_14.15 | all-reduce | flops 8192 | bytes 65536 | tf_op jit(solution)/shard_map/psum | solution.py:1176
  764.9 2.8 multiply_reduce_fusion
  768.9 4.3 convert_element_type.80
  773.3 2.6 convert_element_type.81
  775.9 2.6 convert_element_type.82
  778.5 2.7 convert_element_type.83
  (98 shorter events, 28.3 us)
Async XLA Ops:
  7.2 1.6 copy-start
  7.2 134.0 %all-gather.3.cloned.1.call-start = ((), (), s32[]{:S(2)}) async-start(), calls=%async_computation | async-start | bytes 9437184 | tf_op jit(solution)/shard_map/all_gather | solution.py:1100
  9.5 23.2 %copy-start.15 = (bf16[4,512]{1,0:T(4,128)(2,1)S(1)}, bf16[4,512]{1,0:T(4,128)(2,1)}, u32[]{:S(2)}) copy-start(bf16[4,512]{1,0:T(4,128)(2,1)} %param.22) | copy-start | bytes 12292
  9.5 23.3 %copy-start.17 = (f32[256,2]{0,1:T(2,128)S(1)}, f32[256,2]{0,1:T(2,128)}, u32[]{:S(2)}) copy-start(f32[256,2]{0,1:T(2,128)} %param.16) | copy-start | bytes 6148
  9.5 23.3 %copy-start.18 = (s32[256,2]{0,1:T(2,128)S(1)}, s32[256,2]{0,1:T(2,128)}, u32[]{:S(2)}) copy-start(s32[256,2]{0,1:T(2,128)} %param.15) | copy-start | bytes 6148
  32.7 231.9 %all-gather.5.cloned.1.call-start = ((), (), s32[]{:S(2)}) async-start(), calls=%async_computation.1 | async-start | bytes 5242880 | tf_op jit(solution)/shard_map/all_gather | solution.py:1111
  115.1 391.1 %all-reduce.9.cloned.1.call-start = ((), (), s32[]{:S(2)}) async-start(), calls=%async_computation.3 | async-start | bytes 25165824 | tf_op jit(solution)/shard_map/psum | solution.py:1121
  325.1 1.0 copy-start.3
  325.1 1.5 copy-start.7
  325.2 443.8 %all-reduce.7.cloned.1.call-start = ((), (), s32[]{:S(2)}) async-start(), calls=%async_computation.2 | async-start | bytes 16777216 | tf_op jit(solution)/shard_map/psum | solution.py:1165
  484.4 3.0 copy-start.19
  487.4 2.6 copy-start.24
  490.7 2.2 copy-start.13
  490.7 3.3 copy-start.22
  494.0 21.9 %copy-start.4 = (f32[4,256,512]{2,1,0:T(8,128)S(1)}, f32[4,256,512]{2,1,0:T(8,128)}, u32[]{:S(2)}) copy-start(f32[4,256,512]{2,1,0:T(8,128)} %get-tuple-element.59) | copy-start | bytes 6291460
  516.0 3.6 copy-start.20
  519.6 5.8 copy-start.23
  525.3 3.7 copy-start.21
  534.8 3.7 copy-start.8
  548.7 0.8 copy-start.14
  548.7 0.9 copy-start.16
  707.9 6.5 copy-start.6
  714.4 4.1 copy-start.5
  718.5 46.4 %copy-start.2 = (f32[8,32,2048]{2,1,0:T(8,128)S(1)}, f32[8,32,2048]{2,1,0:T(8,128)}, u32[]{:S(2)}) copy-start(f32[8,32,2048]{2,1,0:T(8,128)} %scatter_norm.3) | copy-start | bytes 6291460
  768.9 4.4 copy-start.11
  773.3 2.6 copy-start.10
  775.9 2.6 copy-start.9
  778.5 2.7 copy-start.12
  778.5 4.1 copy-start.1
Sparse Core Ops, SparseCore 0:
  32.8 56.3 all-gather.2
  115.2 102.5 all-gather.4
  325.3 180.8 all-reduce.8
  548.8 127.7 all-reduce.6

commit v4 on v3

--- a/solution.py
+++ b/solution.py
@@ -345,118 +345,167 @@
 
 
 def attention_back_kernel(
-    prefix, q_ref, k_ref, v_ref, g_ref, q_raw, k_raw, factors, cosine, sine, gains,
-    dq_out, dk_out, dv_out, gain_out, inner_out, k_acc, v_acc, inner_acc,
+    n, steps, width, limit_ref, q_ref, k_ref, v_ref, g_ref, q_raw, k_raw, factors, cosine, sine,
+    gains, sum_hbm, q_grad, k_grad, v_grad, gain_out, own_sum,
+    dq_acc, dk_acc, k_acc, v_acc, inner_all, inner_send, inner_recv, part, *line,
 ):
-    length = q_ref.shape[0]
+    length, local = q_ref.shape
+    heads = local // HEAD_DIM
     block = 256
-    limit = prefix[0]
+    blocks = length // block
     scale = HEAD_DIM**-0.5
-    h = pl.program_id(0)
-    k_acc[...] = jnp.zeros_like(k_acc)
-    v_acc[...] = jnp.zeros_like(v_acc)
-
-    @pl.when(h == 0)
-    def _():
-        inner_acc[...] = jnp.zeros_like(inner_acc)
-
-    for i in range(length // block):
-        span = key_span(i, block, length)
-        r = pl.ds(i * block, block)
-        q, g = q_ref[r, :], g_ref[r, :]
-        s = block_scores(q, k_ref[0:span, :], i, block, limit)
-        e = jnp.exp(s - jnp.max(s, axis=1, keepdims=True))
-        p = e * (1.0 / jnp.sum(e, axis=1, keepdims=True))
-        pg = dot_nt(g, v_ref[0:span, :])
-        t = p * pg
-        ds = (t - p * jnp.sum(t, axis=1, keepdims=True)).astype(bf16)
-        dq_out[r, :] = dot(ds, k_ref[0:span, :]) * scale
-        k_acc[0:span, :] += dot_tn(ds, q) * scale
-        v_acc[0:span, :] += dot_tn(p.astype(bf16), g)
-    dv_out[...] = v_acc[...].astype(bf16)
+    load_sem = line[-1]
+    turn, drain = line_sum(n, steps, part, own_sum, *line[:-1])
+    load = pltpu.make_async_copy(sum_hbm.at[:, 1], part, load_sem.at[0])
+    load.start()
+    d, z, peers = others(n)
+    greet(peers)
+    load.wait()
+    slots = -(-(steps + n - 1) // heads)
+    limit = limit_ref[0:1, 0:1]
     lanes = lax.broadcasted_iota(jnp.int32, (block, 128), 1)
 
-    def back(i, carry):
-        gq, gk = carry
+    def clear(i, carry):
+        inner_all[z, i] = jnp.zeros((8, block), f32)
+        return carry
+
+    lax.fori_loop(0, blocks, clear, 0)
+
+    def head(h, carry):
+        c = pl.ds(pl.multiple_of(h * HEAD_DIM, HEAD_DIM), HEAD_DIM)
+        k_acc[...] = jnp.zeros_like(k_acc)
+        v_acc[...] = jnp.zeros_like(v_acc)
+        for i in range(blocks):
+            for j in range(i * slots // blocks, (i + 1) * slots // blocks):
+                turn(h * slots + j)
+            span = key_span(i, block, length)
+            r = pl.ds(i * block, block)
+            q, g, k, v = q_ref[r, c], g_ref[r, c], k_ref[0:span, c], v_ref[0:span, c]
+            s = block_scores(q, k, i, block, limit)
+            e = jnp.exp(s - jnp.max(s, axis=1, keepdims=True))
+            p = e * (1.0 / jnp.sum(e, axis=1, keepdims=True))
+            t = p * dot_nt(g, v)
+            ds = (t - p * jnp.sum(t, axis=1, keepdims=True)).astype(bf16)
+            dq_acc[r, c] = dot(ds, k) * scale
+            k_acc[0:span, :] += dot_tn(ds, q) * scale
+            v_acc[0:span, :] += dot_tn(p.astype(bf16), g)
+        v_grad[:, c] = v_acc[...].astype(bf16)
+        gain_q, gain_k = gains[0:1, c], gains[1:2, c]
+
+        def back(i, carry):
+            gq, gk = carry
+            r = pl.ds(pl.multiple_of(i * block, block), block)
+            cos, sin = cosine[r, :], sine[r, :]
+            dq = rope(dq_acc[r, c], cos, -sin)
+            dk = rope(k_acc[r, :], cos, -sin)
+            uq = q_raw[r, c] * factors[r, 0:1]
+            uk = k_raw[r, c] * factors[r, 1:2]
+            gq = gq + jnp.sum(dq * uq, axis=0, keepdims=True)
+            gk = gk + jnp.sum(dk * uk, axis=0, keepdims=True)
+            dq = dq * gain_q
+            dk = dk * gain_k
+            dq_acc[r, c] = dq
+            dk_acc[r, c] = dk
+            inner_q = jnp.sum(dq * uq, axis=1, keepdims=True)
+            inner_k = jnp.sum(dk * uk, axis=1, keepdims=True)
+            both = jnp.where(lanes == 0, inner_q, jnp.where(lanes == 1, inner_k, 0.0))
+            inner_all[z, i] += both.T[0:8]
+            return gq, gk
+
+        zero = jnp.zeros((1, HEAD_DIM), f32)
+        gq, gk = lax.fori_loop(0, blocks, back, (zero, zero))
+        gain_out[0:1, c] = gq
+        gain_out[1:2, c] = gk
+        return carry
+
+    lax.fori_loop(0, heads, head, 0)
+
+    copies = []
+    for p, peer in enumerate(peers):
+        copy = pltpu.make_async_remote_copy(
+            src_ref=inner_all.at[z], dst_ref=inner_all.at[z], send_sem=inner_send.at[p],
+            recv_sem=inner_recv.at[z], device_id=peer, device_id_type=MESH,
+        )
+        copy.start()
+        copies.append(copy)
+    drain()
+    for p in range(1, n):
+        o = lax.rem(z + n - p, n)
+        pltpu.make_async_remote_copy(
+            src_ref=inner_all.at[o], dst_ref=inner_all.at[o], send_sem=inner_send.at[p - 1],
+            recv_sem=inner_recv.at[o], device_id=(d, o), device_id_type=MESH,
+        ).wait_recv()
+
+    def raw(i, carry):
         r = pl.ds(pl.multiple_of(i * block, block), block)
-        c, s = cosine[r, :], sine[r, :]
-        dq = rope(dq_out[r, :], c, -s)
-        dk = rope(k_acc[r, :], c, -s)
-        uq = q_raw[r, :] * factors[r, 0:1]
-        uk = k_raw[r, :] * factors[r, 1:2]
-        gq = gq + jnp.sum(dq * uq, axis=0, keepdims=True)
-        gk = gk + jnp.sum(dk * uk, axis=0, keepdims=True)
-        dq = dq * gains[0:1, :]
-        dk = dk * gains[1:2, :]
-        dq_out[r, :] = dq
-        dk_out[r, :] = dk
-        inner_q = jnp.sum(dq * uq, axis=1, keepdims=True)
-        inner_k = jnp.sum(dk * uk, axis=1, keepdims=True)
-        both = jnp.where(lanes == 0, inner_q, jnp.where(lanes == 1, inner_k, 0.0))
-        inner_acc[i] += both.T[0:8]
-        return gq, gk
-
-    zero = jnp.zeros((1, HEAD_DIM), f32)
-    gq, gk = lax.fori_loop(0, length // block, back, (zero, zero))
-    gain_out[0:1, :] = gq
-    gain_out[1:2, :] = gk
-
-    @pl.when(h == pl.num_programs(0) - 1)
-    def _():
-        inner_out[...] = inner_acc[...]
-
-
-def attention_back(prefix, q, k, v, g, q_raw, k_raw, factors, cosine, sine, gains):
+        total = inner_all[0, i]
+        for s in range(1, n):
+            total = total + inner_all[s, i]
+        total = jnp.concatenate([total, jnp.zeros((120, block), f32)], axis=0).T
+        fq, fk = factors[r, 0:1], factors[r, 1:2]
+        mean_q, mean_k = total[:, 0:1] / width, total[:, 1:2] / width
+        q_grad[r, :] = (fq * (dq_acc[r, :] - q_raw[r, :] * (fq * mean_q))).astype(bf16)
+        k_grad[r, :] = (fk * (dk_acc[r, :] - k_raw[r, :] * (fk * mean_k))).astype(bf16)
+        return carry
+
+    lax.fori_loop(0, blocks, raw, 0)
+    for copy in copies:
+        copy.wait_send()
+
+
+def attention_back(
+    n, width, limit, q, k, v, g, q_raw, k_raw, factors, cosine, sine, gains, sum_halves
+):
     length, local = q.shape
-    heads = local // HEAD_DIM
-    head = pl.BlockSpec((length, HEAD_DIM), lambda h, p: (0, h))
-    pair = pl.BlockSpec((2, HEAD_DIM), lambda h, p: (0, h))
-    whole = lambda a: pl.BlockSpec(a.shape, lambda h, p: (0, 0))
-    wide = jax.ShapeDtypeStruct((length, local), f32)
-    inner = (length // 256, 8, 256)
+    _, _, steps, R, D = sum_halves.shape
+    vmem = pl.BlockSpec(memory_space=pltpu.VMEM)
+    dma = pltpu.SemaphoreType.DMA
+    grad = jax.ShapeDtypeStruct((length, local), bf16)
     return pl.pallas_call(
-        attention_back_kernel,
+        functools.partial(attention_back_kernel, n, steps, width),
         out_shape=[
-            wide, wide, jax.ShapeDtypeStruct((length, local), bf16),
-            jax.ShapeDtypeStruct((2, local), f32), jax.ShapeDtypeStruct(inner, f32),
+            grad, grad, grad, jax.ShapeDtypeStruct((2, local), f32),
+            jax.ShapeDtypeStruct((steps, R, D), f32),
         ],
-        grid_spec=pltpu.PrefetchScalarGridSpec(
-            num_scalar_prefetch=1,
-            grid=(heads,),
-            in_specs=[head] * 6 + [whole(factors), whole(cosine), whole(sine), pair],
-            out_specs=[head, head, head, pair, pl.BlockSpec(inner, lambda h, p: (0, 0, 0))],
-            scratch_shapes=[
-                pltpu.VMEM((length, HEAD_DIM), f32),
-                pltpu.VMEM((length, HEAD_DIM), f32),
-                pltpu.VMEM(inner, f32),
-            ],
+        in_specs=[vmem] * 11 + [pl.BlockSpec(memory_space=pl.ANY)],
+        out_specs=[vmem] * 5,
+        scratch_shapes=[
+            pltpu.VMEM((length, local), f32),
+            pltpu.VMEM((length, local), f32),
+            pltpu.VMEM((length, HEAD_DIM), f32),
+            pltpu.VMEM((length, HEAD_DIM), f32),
+            pltpu.VMEM((n, length // 256, 8, 256), f32),
+            dma((n,)),
+            dma((n,)),
+        ]
+        + line_scratch(n, steps, R, D),
+        compiler_params=pltpu.CompilerParams(
+            collective_id=6, has_side_effects=True, vmem_limit_bytes=VMEM_LIMIT
         ),
-        compiler_params=pltpu.CompilerParams(vmem_limit_bytes=VMEM_LIMIT),
-        cost_estimate=pl.CostEstimate(flops=2 * 10**9, bytes_accessed=2**20, transcendentals=0),
+        cost_estimate=pl.CostEstimate(
+            flops=2 * 10**9, bytes_accessed=2**20, transcendentals=0
+        ),
         name="attention_back",
-    )(prefix, q, k, v, g, q_raw, k_raw, factors, cosine, sine, gains)
-
-
-def scatter_norm_kernel(n, steps, gather, plain, *refs):
-    part, refs = refs[0], refs[1:]
-    if not plain:
-        base, addend, gain = refs[:3]
-        refs = refs[3:]
+    )(limit, q, k, v, g, q_raw, k_raw, factors, cosine, sine, gains, sum_halves)
+
+
+def scatter_norm_kernel(n, groups, steps, gather, *refs):
+    part, base, addend, gain = refs[:4]
+    refs = refs[4:]
     if gather:
         out, all_out, gain_out = refs[:3]
-        refs = refs[3:]
-        alls, ag_up, ag_down, ag_recv, all_sem = refs[:5]
-        refs = refs[5:]
-    elif plain:
-        out, refs = refs[0], refs[1:]
+        alls, ag_up, ag_down, ag_recv, all_sem = refs[3:8]
+        refs = refs[8:]
     else:
-        out, gain_out = refs[:2]
-        refs = refs[2:]
+        expert_gains, head_gains, out, gain_out = refs[:4]
+        pieces, landed, sums, piece_send, piece_recv, sum_send, sum_recv = refs[4:11]
+        refs = refs[11:]
     from_below, from_above, gain_acc, up_send, up_recv, down_send, down_recv = refs
     R, D = part.shape[2:]
     d, z, peers = others(n)
     upper, lower = (d, lax.rem(z + 1, n)), (d, lax.rem(z + n - 1, n))
-    greet(peers)
+    alike = [] if gather else [(lax.rem(d + p, groups), z) for p in range(1, groups)]
+    greet(peers + alike)
     gain_acc[...] = jnp.zeros_like(gain_acc)
 
     def move_up(src, o, k):
@@ -545,9 +594,6 @@
         total = (
             part[z, k].astype(f32) + from_below[z, k].astype(f32) + from_above[z, k].astype(f32)
         )
-        if plain:
-            out[k] = total
-            return
         rows = base[k].astype(f32)
         factor = lax.rsqrt(jnp.sum(rows * rows, axis=1, keepdims=True) / D + EPSILON)
         unit = rows * factor
@@ -614,8 +660,61 @@
         return carry
 
     lax.fori_loop(0, steps + (2 * n - 2 if gather else n - 1), turn, 0)
-    if not plain:
+    if gather:
         gain_out[...] = gain_acc[...]
+    else:
+        C = D // n
+        for s in range(n):
+            c = slice(s * C, (s + 1) * C)
+            pieces[s, 0:1] = jnp.sum(gain_acc[:, c], axis=0, keepdims=True)
+            pieces[s, 1:2] = jnp.sum(expert_gains[:, c], axis=0, keepdims=True)
+            pieces[s, 2:8] = jnp.zeros((6, C), f32)
+
+        def piece(p):
+            o = lax.rem(z + p, n)
+            return pltpu.make_async_remote_copy(
+                src_ref=pieces.at[o], dst_ref=landed.at[z], send_sem=piece_send.at[p - 1],
+                recv_sem=piece_recv.at[z], device_id=(d, o), device_id_type=MESH,
+            )
+
+        for p in range(1, n):
+            piece(p).start()
+        landed[z] = pieces[z]
+        for p in range(1, n):
+            o = lax.rem(z + n - p, n)
+            pltpu.make_async_remote_copy(
+                src_ref=pieces.at[o], dst_ref=landed.at[o], send_sem=piece_send.at[p - 1],
+                recv_sem=piece_recv.at[o], device_id=(d, o), device_id_type=MESH,
+            ).wait_recv()
+        two = landed[0]
+        for s in range(1, n):
+            two = two + landed[s]
+        sums[d, 0:1] = two[0:1]
+        sums[d, 1:3] = head_gains[...]
+        sums[d, 3:4] = two[1:2]
+        sums[d, 4:8] = jnp.zeros((4, C), f32)
+        for p in range(1, groups):
+            pltpu.make_async_remote_copy(
+                src_ref=sums.at[d], dst_ref=sums.at[d], send_sem=sum_send.at[p - 1],
+                recv_sem=sum_recv.at[d], device_id=alike[p - 1], device_id_type=MESH,
+            ).start()
+        for p in range(1, groups):
+            o = lax.rem(d + groups - p, groups)
+            pltpu.make_async_remote_copy(
+                src_ref=sums.at[o], dst_ref=sums.at[o], send_sem=sum_send.at[p - 1],
+                recv_sem=sum_recv.at[o], device_id=(o, z), device_id_type=MESH,
+            ).wait_recv()
+        total = sums[0]
+        for s in range(1, groups):
+            total = total + sums[s]
+        gain_out[...] = total
+        for p in range(1, n):
+            piece(p).wait_send()
+        for p in range(1, groups):
+            pltpu.make_async_remote_copy(
+                src_ref=sums.at[d], dst_ref=sums.at[d], send_sem=sum_send.at[p - 1],
+                recv_sem=sum_recv.at[d], device_id=alike[p - 1], device_id_type=MESH,
+            ).wait_send()
 
     def drain(i, carry):
         o, k = i // steps, i % steps
@@ -649,27 +748,35 @@
             copy.wait()
 
 
-def scatter_norm(n, steps, gather, part, base, addend, gain, collective_id, plain=False):
-    T, D = part.shape[0] // n, part.shape[1]
+def scatter_norm(n, groups, steps, part, base, addend, gain, other_gains=None):
+    gather = other_gains is None
+    T, D = base.shape
     R = T // steps
+    C = D // n
     hbm = pl.BlockSpec(memory_space=pl.ANY)
     vmem = pl.BlockSpec(memory_space=pltpu.VMEM)
     dma = pltpu.SemaphoreType.DMA
     slots = pltpu.VMEM((n, steps, R, D), bf16)
     rows = jax.ShapeDtypeStruct((steps, R, D), f32)
-    gains = jax.ShapeDtypeStruct((8, D), f32)
     sems = dma((n, steps))
-    results = pl.pallas_call(
-        functools.partial(scatter_norm_kernel, n, steps, gather, plain),
-        out_shape=[rows]
-        + ([jax.ShapeDtypeStruct((n, steps, R, D), bf16)] if gather else [])
-        + ([] if plain else [gains]),
-        in_specs=[vmem] * (1 if plain else 4),
-        out_specs=[vmem] + ([hbm] if gather else []) + ([] if plain else [vmem]),
-        scratch_shapes=([slots, sems, sems, sems, dma((n,))] if gather else [])
-        + [slots, slots, pltpu.VMEM((8, D), f32), sems, sems, sems, sems],
+    if gather:
+        own = [slots, sems, sems, sems, dma((n,))]
+        outs = [rows, jax.ShapeDtypeStruct((n, steps, R, D), bf16)]
+        outs += [jax.ShapeDtypeStruct((8, D), f32)]
+    else:
+        own = [
+            pltpu.VMEM((n, 8, C), f32), pltpu.VMEM((n, 8, C), f32),
+            pltpu.VMEM((groups, 8, C), f32), dma((n,)), dma((n,)), dma((groups,)), dma((groups,)),
+        ]
+        outs = [rows, jax.ShapeDtypeStruct((8, C), f32)]
+    return pl.pallas_call(
+        functools.partial(scatter_norm_kernel, n, groups, steps, gather),
+        out_shape=outs,
+        in_specs=[vmem] * (4 if gather else 6),
+        out_specs=[vmem, hbm, vmem] if gather else [vmem, vmem],
+        scratch_shapes=own + [slots, slots, pltpu.VMEM((8, D), f32), sems, sems, sems, sems],
         compiler_params=pltpu.CompilerParams(
-            collective_id=collective_id, has_side_effects=True, vmem_limit_bytes=VMEM_LIMIT
+            collective_id=2 if gather else 3, has_side_effects=True, vmem_limit_bytes=VMEM_LIMIT
         ),
         cost_estimate=pl.CostEstimate(
             flops=10**9, bytes_accessed=2**20, transcendentals=0
@@ -677,19 +784,11 @@
         name="scatter_norm_gather" if gather else "scatter_norm",
     )(
         part.reshape(n, steps, R, D),
-        *(
-            ()
-            if plain
-            else (base.reshape(steps, R, D), addend.reshape(steps, R, D), gain)
-        ),
-    )
-    if plain:
-        return results[0].reshape(T, D)
-    if gather:
-        out, alls, gains = results
-        return out.reshape(T, D), alls.reshape(n * T, D), gains
-    out, gains = results
-    return out.reshape(T, D), gains
+        base.reshape(steps, R, D),
+        addend.reshape(steps, R, D),
+        gain,
+        *(() if gather else other_gains),
+    )
 
 
 def gather_mix_kernel(
@@ -915,6 +1014,109 @@
     )(x, g, combine, gate_w, up_w, down_w)
 
 
+def line_sum(n, steps, part, out, from_below, from_above, up_send, up_recv, down_send, down_recv):
+    d, z = lax.axis_index("dp"), lax.axis_index("shard")
+    upper, lower = (d, lax.rem(z + 1, n)), (d, lax.rem(z + n - 1, n))
+
+    def move_up(src, o, k):
+        return pltpu.make_async_remote_copy(
+            src_ref=src.at[o, k], dst_ref=from_below.at[o, k], send_sem=up_send.at[o, k],
+            recv_sem=up_recv.at[o, k], device_id=upper, device_id_type=MESH,
+        )
+
+    def move_down(src, o, k):
+        return pltpu.make_async_remote_copy(
+            src_ref=src.at[o, k], dst_ref=from_above.at[o, k], send_sem=down_send.at[o, k],
+            recv_sem=down_recv.at[o, k], device_id=lower, device_id_type=MESH,
+        )
+
+    def passing(move, landed, first, owner):
+        def run(k):
+            def far(i, carry):
+                o = owner(i)
+
+                @pl.when((o >= 0) & (o < n))
+                def _():
+                    @pl.when(z == first)
+                    def _():
+                        move(part, o, k).start()
+
+                    @pl.when(z != first)
+                    def _():
+                        move(part, o, k).wait_recv()
+                        both = landed[o, k].astype(f32) + part[o, k].astype(f32)
+                        landed[o, k] = both.astype(bf16)
+                        move(landed, o, k).start()
+
+                return carry
+
+            lax.fori_loop(0, n - 1, far, 0)
+
+        return run
+
+    pass_up = passing(move_up, from_below, 0, lambda i: z + n - 1 - i)
+    pass_down = passing(move_down, from_above, n - 1, lambda i: z - n + 1 + i)
+
+    def own(k):
+        @pl.when(z > 0)
+        def _():
+            move_up(part, z, k).wait_recv()
+
+        @pl.when(z == 0)
+        def _():
+            from_below[z, k] = jnp.zeros(part.shape[2:], bf16)
+
+        @pl.when(z < n - 1)
+        def _():
+            move_down(part, z, k).wait_recv()
+
+        @pl.when(z == n - 1)
+        def _():
+            from_above[z, k] = jnp.zeros(part.shape[2:], bf16)
+
+        out[k] = (
+            part[z, k].astype(f32) + from_below[z, k].astype(f32) + from_above[z, k].astype(f32)
+        )
+
+    def turn(t):
+        up_k, down_k, own_k = t - z, t - (n - 1 - z), t - (n - 1)
+
+        @pl.when((up_k >= 0) & (up_k < steps))
+        def _():
+            pass_up(up_k)
+
+        @pl.when((down_k >= 0) & (down_k < steps))
+        def _():
+            pass_down(down_k)
+
+        @pl.when((own_k >= 0) & (own_k < steps))
+        def _():
+            own(own_k)
+
+    def drain():
+        def one(i, carry):
+            o, k = i // steps, i % steps
+
+            @pl.when(o > z)
+            def _():
+                move_up(part, o, k).wait_send()
+
+            @pl.when(o < z)
+            def _():
+                move_down(part, o, k).wait_send()
+
+            return carry
+
+        lax.fori_loop(0, n * steps, one, 0)
+
+    return turn, drain
+
+
+def line_scratch(n, steps, R, D):
+    dma = pltpu.SemaphoreType.DMA
+    return [pltpu.VMEM((n, steps, R, D), bf16)] * 3 + [dma((n, steps))] * 4 + [dma((1,))]
+
+
 def expert_grads_kernel(x_ref, g_ref, hidden, gate_grad, up_grad, gate_out, up_out, down_out, xt):
     @pl.when(pl.program_id(0) == 0)
     def _():
@@ -945,6 +1147,40 @@
         ),
         name="expert_grads",
     )(x, g, hidden, gate_grad, up_grad)
+
+
+def line_sum_kernel(n, half, sum_hbm, own_sum, part, *line):
+    steps = part.shape[1]
+    load_sem = line[-1]
+    load = pltpu.make_async_copy(sum_hbm.at[:, half], part, load_sem.at[0])
+    load.start()
+    _, _, peers = others(n)
+    greet(peers)
+    load.wait()
+    turn, drain = line_sum(n, steps, part, own_sum, *line[:-1])
+
+    def one(t, carry):
+        turn(t)
+        return carry
+
+    lax.fori_loop(0, steps + n - 1, one, 0)
+    drain()
+
+
+def line_sum_alone(n, half, sum_halves):
+    _, _, steps, R, D = sum_halves.shape
+    return pl.pallas_call(
+        functools.partial(line_sum_kernel, n, half),
+        out_shape=jax.ShapeDtypeStruct((steps, R, D), f32),
+        in_specs=[pl.BlockSpec(memory_space=pl.ANY)],
+        out_specs=pl.BlockSpec(memory_space=pltpu.VMEM),
+        scratch_shapes=line_scratch(n, steps, R, D),
+        compiler_params=pltpu.CompilerParams(
+            collective_id=5, has_side_effects=True, vmem_limit_bytes=VMEM_LIMIT
+        ),
+        cost_estimate=pl.CostEstimate(flops=10**9, bytes_accessed=2**20, transcendentals=0),
+        name="line_sum",
+    )(sum_halves)
 
 
 def gather_line_kernel(n, v_hbm, out, slots, load_sem, up_sem, down_sem, recv_sem, out_sem):
@@ -1112,6 +1348,7 @@
     sum_part, in_part, hidden, gate_grad, up_grad = experts_pass(
         expert_in, g_all, combine, expert_gate, expert_up, expert_down
     )
+    sum_halves = sum_part.reshape(shards, 2, 8, rows // 16, width)
     grad_gate, grad_up, grad_down = expert_grads(
         expert_in, g_all, hidden, gate_grad, up_grad, experts
     )
@@ -1123,29 +1360,23 @@
     x_own = tokens.astype(f32)
     residual_own = x_own + attended_own
     residual_grad, attended_grad, gain_grad_res = scatter_norm(
-        shards, 16, True, in_part, residual_own, out_grad, gain_expert[None, :], 2
-    )
+        shards, groups, 16, in_part, residual_own, out_grad, gain_expert[None, :]
+    )
+    residual_grad = residual_grad.reshape(rows, width)
+    attended_grad = attended_grad.reshape(length, width)
 
     own_columns = lax.dynamic_slice_in_dim(attended_grad, place * local, local, 1)
     grad_output = jnp.concatenate([dot_tn(mixed_all[s], own_columns) for s in range(shards)], 0)
     mixed_grad = dot_nt(
         attended_grad, lax.dynamic_slice_in_dim(full_output, place * local, local, 0)
     ).astype(bf16)
-    query_norm_grad, key_norm_grad, value_raw_grad, gain_grad_heads, inner = attention_back(
-        prefix, queries, keys, values, mixed_grad, query_raw, key_raw, factors, cosine, sine,
-        head_gains,
-    )
-    inner, grad_gate, grad_up, grad_down = lax.optimization_barrier(
-        (inner, grad_gate, grad_up, grad_down)
-    )
-    inner = lax.psum(inner[:, :2], "shard") / width
-    inner = inner.transpose(0, 2, 1).reshape(length, 2)
-    factor_query, factor_key = factors[:, 0:1], factors[:, 1:2]
-    query_raw_grad = (
-        factor_query * (query_norm_grad - query_raw * factor_query * inner[:, 0:1])
-    ).astype(bf16)
-    key_raw_grad = (factor_key * (key_norm_grad - key_raw * factor_key * inner[:, 1:2])).astype(
-        bf16
+    limit = jnp.broadcast_to(prefix.reshape(1, 1), (8, 128))
+    query_raw_grad, key_raw_grad, value_raw_grad, gain_grad_heads, sum_second = attention_back(
+        shards, width, limit, queries, keys, values, mixed_grad, query_raw, key_raw, factors,
+        cosine, sine, head_gains, sum_halves,
+    )
+    query_raw_grad, key_raw_grad, grad_gate, grad_up, grad_down = lax.optimization_barrier(
+        (query_raw_grad, key_raw_grad, grad_gate, grad_up, grad_down)
     )
     normed_part = (
         dot_nt(query_raw_grad, query_weight)
@@ -1163,22 +1394,19 @@
         )
     )
     grad_query, grad_key, grad_value, grad_output = lax.psum(attention_grads, "dp")
-    grad_tokens, gain_grad_x = scatter_norm(
-        shards, 8, False, normed_part, tokens, residual_grad, gain_in[None, :], 3
-    )
-    sum_part, grad_tokens = lax.optimization_barrier((sum_part, grad_tokens))
-    expert_sum = scatter_norm(shards, 8, False, sum_part, None, None, None, 5, plain=True)
+    grad_tokens, grad_gains = scatter_norm(
+        shards, groups, 8, normed_part, tokens, residual_grad, gain_in[None, :],
+        (gain_grad_res, gain_grad_heads),
+    )
+    grad_tokens = grad_tokens.reshape(rows, width)
+    grad_gains = grad_gains[:4]
+    sum_halves, grad_tokens = lax.optimization_barrier((sum_halves, grad_tokens))
+    sum_first = line_sum_alone(shards, 0, sum_halves)
+    expert_sum = jnp.concatenate(
+        [sum_first.reshape(rows // 2, width), sum_second.reshape(rows // 2, width)], 0
+    )
     output = residual_own + expert_sum
     root_means = jnp.stack([root_mean(attended_own), root_mean(expert_sum), root_mean(output)])
-    placed = lax.dynamic_update_slice(
-        jnp.zeros((2, width), f32), gain_grad_heads, (jnp.int32(0), place * local)
-    )
-    gain_rows = lax.psum(
-        jnp.concatenate([gain_grad_x.sum(0)[None], placed, gain_grad_res.sum(0)[None]], 0),
-        ("dp", "shard"),
-    )
-    grad_gains = lax.dynamic_slice_in_dim(gain_rows, place * local, local, 1)
-
     return (
         output.astype(bf16),
         grad_tokens,

time: 805 us -> 756 us (0.939)
  blocking collectives: 50.9 us -> 0 us
  Pallas kernels: 605 us -> 623 us
  waiting for transfers between devices: 8.54 us -> 0.09 us
    psum x2 -> x0, blocking collectives: 50.9 us -> none  [the longest x1 41.9 us: per_device(): lax.psum(jnp.concatenate([gain_grad_x.sum(0)[None], placed, gain_grad_res...]
    pallas_call x4, Pallas kernels: 303 us -> 320 us  [the longest x2 214 us: scatter_norm(): pl.pallas_call(functools.partial(scatter_norm_kernel, n, groups, steps, g...]
    psum x1, waiting for transfers between devices: 8.45 us -> 0.01 us  [per_device(): lax.psum((grad_gate, grad_up, grad_down), 'dp')]
  transfers between devices with their start and end apart: 4 -> 4, of which waited for: 1 -> 0; matrix products, arithmetic and copies ran while one was open for 7% -> 7% of each run, Pallas kernels for 66% -> 73%
where the time goes in v4:
time: 756 us; the launch traced here: 741 us
  Pallas kernels  623 us (82%)
  matrix products  47.1 us (6%)
  other arithmetic  40.4 us (5%)
  local copies, waits for them, and re-layouts  15.8 us (2%)
  between operations  14.9 us (2%)
    pallas_call x2, Pallas kernels, scatter_norm(): pl.pallas_call(functools.partial(scatter_norm_kernel, n, groups, steps, g...  214 us
    pallas_call x1, Pallas kernels, gather_mix(): pl.pallas_call(functools.partial(gather_mix_kernel, n), out_shape=[jax.Sh...  124 us
    pallas_call x1, Pallas kernels, gather_project(): pl.pallas_call(functools.partial(gather_project_kernel, n), out_shape=[ja...  81.6 us
    pallas_call x1, Pallas kernels, attention_back(): pl.pallas_call(functools.partial(attention_back_kernel, n, steps, width),...  62.5 us
    pallas_call x1, Pallas kernels, line_sum_alone(): pl.pallas_call(functools.partial(line_sum_kernel, n, half), out_shape=jax...  44.1 us
    pallas_call x1, Pallas kernels, experts_pass(): pl.pallas_call(experts_kernel, out_shape=[wide, wide, narrow, narrow, nar...  40.1 us
    dot_general x4, matrix products, dot_nt(): lax.dot_general(a, b, (((1,), (1,)), ((), ())), preferred_element_type=f32)  29.8 us
    pallas_call x1, Pallas kernels, gather_line(): pl.pallas_call(functools.partial(gather_line_kernel, n), out_shape=jax.Sh...  20.8 us
  transfers between devices with their start and end apart: 4, of which 0 were waited for; matrix products, arithmetic and copies ran while one was open for 7% of the time, Pallas kernels for 73%

profile of v4, /device:TPU:12, one launch (start us, length us, event | category | flops | bytes accessed | tf_op | source)
XLA Modules:
  0.0 741.2 jit_solution(17521937006735088214)
XLA Ops:
  7.2 1.5 copy-done
  9.5 20.8 %gather_line.1 = bf16[4,256,512]{2,1,0:T(8,128)(2,1)} custom-call(bf16[256,512]{1,0:T(8,128)(2,1)} %constant_dynamic-slice_fusion.v_hbm), custom_call_target="tpu_custom_call" | custom-call | flops 20000000000 | bytes 2097152 | tf_op jit(solution)/shard_map/gather_line/pallas_call | solution.py:1265
  30.3 2.3 copy.32
  33.4 81.6 %gather_project.1 = (bf16[4,256,2048]{2,1,0:T(8,128)(2,1)}, bf16[4,256,2048]{2,1,0:T(8,128)(2,1)}, f32[4,256,512]{2,1,0:T(8,128)}, f32[4,256,512]{2,1,0:T(8,128)...) custom-call(bf16[256,2048]{1,0:T(8,128)(2,1)} %x_hbm.1, ...), custom_call_target="tpu_custom_call" | custom-call | flops 80000000000 | bytes 33554432 | tf_op jit(solution)/shard_map/gather_project/pallas_call | solution.py:241
  115.7 1.5 fusion.25
  121.5 1.9 fusion.19
  124.8 15.7 %attention.1 = (bf16[1024,512]{1,0:T(8,128)(2,1)}, bf16[1024,512]{1,0:T(8,128)(2,1)}, bf16[1024,512]{1,0:T(8,128)(2,1)}) custom-call(s32[1]{0:T(128)} %copy.41.prefix, f32[1024,512]{1,0:T(8,128)} %bitcast.70, f32[1024,512]{1,0:T(8,128)} %bitcast.72, bf16[1024,512]{1,0:T(8,128)(2,1)} %bitcast.75, f32[1024,2]{1,0:T(8,128)} %bitcast.67, ...), custom_call_target="tpu_custom_call" | custom-call | flops 14000000000 | bytes 16777216 | tf_op jit(solution)/shard_map/attention/pallas_call | solution.py:329
  140.5 123.9 %gather_mix.1 = (bf16[4,1024,512]{2,1,0:T(8,128)(2,1)}, bf16[1024,2048]{1,0:T(8,128)(2,1)}, f32[256,2048]{1,0:T(8,128)}) custom-call(bf16[1024,512]{1,0:T(8,128)(2,1)} %get-tuple-element.65.mixed_hbm, bf16[2048,2048]{1,0:T(8,128)(2,1)} %all-gather.3.cloned.1.call-done.weight_hbm, bf16[1024,2048]{1,0:T(8,128)(2,1)} %bitcast.95, f32[1,2048]{1,0:T(1,128)} %bitcast.81), custom_call_target="tpu_custom_call" | custom-call | flops 99999997952 | bytes 33554432 | tf_op jit(solution)/shard_map/gather_mix/pallas_call | solution.py:918
  264.5 40.1 %experts_pass.1 = (bf16[1024,2048]{1,0:T(8,128)(2,1)}, bf16[1024,2048]{1,0:T(8,128)(2,1)}, bf16[1024,1024]{1,0:T(8,128)(2,1)}, bf16[1024,1024]{1,0:T(8,128)(2,1)}, bf16[1024,1024]{1,0:T(8,128)(2,1)}) custom-call(bf16[1024,2048]{1,0:T(8,128)(2,1)} %get-tuple-element.69.x_ref, bf16[1024,2048]{1,0:T(8,128)(2,1)} %all-gather.5.cloned.1.call-done.g_ref, ...), custom_call_target="tpu_custom_call" | custom-call | flops 25769803776 | bytes 41943040 | tf_op jit(solution)/shard_map/experts_pass/pallas_call | solution.py:999
  304.6 20.5 %expert_grads.1 = (bf16[4,2048,256]{2,1,0:T(8,128)(2,1)}, bf16[4,2048,256]{2,1,0:T(8,128)(2,1)}, bf16[4,256,2048]{2,1,0:T(8,128)(2,1)}) custom-call(bf16[1024,2048]{1,0:T(8,128)(2,1)} %get-tuple-element.69.x_ref, bf16[1024,2048]{1,0:T(8,128)(2,1)} %all-gather.5.cloned.1.call-done.g_ref, bf16[1024,1024]{1,0:T(8,128)(2,1)} %get-tuple-element.76.hidden, ...), custom_call_target="tpu_custom_call" | custom-call | flops 12884901888 | bytes 27262976 | tf_op jit(solution)/shard_map/expert_grads/pallas_call | solution.py:1137
  326.3 3.2 multiply_reduce_fusion.2
  329.5 124.3 %scatter_norm_gather.1 = (f32[16,16,2048]{2,1,0:T(8,128)}, bf16[4,16,16,2048]{3,2,1,0:T(8,128)(2,1)}, f32[8,2048]{1,0:T(8,128)}) custom-call(bf16[4,16,16,2048]{3,2,1,0:T(8,128)(2,1)} %bitcast.63, f32[16,16,2048]{2,1,0:T(8,128)} %bitcast.58, bf16[16,16,2048]{2,1,0:T(8,128)(2,1)} %bitcast.65, f32[1,2048]{1,0:T(1,128)} %bitcast.82), custom_call_target="tpu_custom_call" | custom-call | flops 1000000000 | bytes 1048576 | tf_op jit(solution)/shard_map/scatter_norm_gather/pallas_call | solution.py:772
  453.8 6.7 fusion.3.g_ref
  461.1 62.5 %attention_back.1 = (bf16[1024,512]{1,0:T(8,128)(2,1)}, bf16[1024,512]{1,0:T(8,128)(2,1)}, bf16[1024,512]{1,0:T(8,128)(2,1)}, f32[2,512]{1,0:T(2,128)}, f32[8,16,2048]{2,1,0:T(8,128)}) custom-call(s32[8,128]{1,0:T(8,128)} %broadcast_in_dim.27.limit_ref, bf16[1024,512]{1,0:T(8,128)(2,1)} %get-tuple-element.73.q_ref, ...), custom_call_target="tpu_custom_call" | custom-call | flops 2000000000 | bytes 1048576 | tf_op jit(solution)/shard_map/attention_back/pallas_call | solution.py:464
  523.6 2.4 convolution_convert_fusion.6
  526.4 2.1 convolution_convert_fusion.5
  532.9 3.7 convolution_convert_fusion
  536.6 7.1 fusion.28
  543.8 3.7 convolution_convert_fusion.1
  547.5 5.8 fusion.27
  553.3 3.9 convolution_convert_fusion.2
  557.2 10.2 %add_convert_fusion = bf16[1024,2048]{1,0:T(8,128)(2,1)} fusion(f32[1024,2048]{1,0:T(8,128)} %fusion.27, f32[1024,2048]{1,0:T(8,128)} %fusion.28, bf16[1024,512]{1,0:T(8,128)(2,1)S(1)} %copy-done.12, bf16[2048,512]{1,0:T(8,128)(2,1)S(1)} %copy-done.6), kind=kOutput, calls=%fused_computation | convolution fusion | flops 2153775104 | bytes 24117248 | tf_op jit(solution)/shard_map/dot_general | solution.py:48
  567.4 89.3 %scatter_norm.1 = (f32[8,32,2048]{2,1,0:T(8,128)}, f32[8,512]{1,0:T(8,128)}) custom-call(bf16[4,8,32,2048]{3,2,1,0:T(8,128)(2,1)} %bitcast.61, bf16[8,32,2048]{2,1,0:T(8,128)(2,1)} %bitcast.66, f32[8,32,2048]{2,1,0:T(8,128)} %bitcast.74, f32[1,2048]{1,0:T(1,128)} %bitcast.80, f32[8,2048]{1,0:T(8,128)} %get-tuple-element.95.refs_4_, ...), custom_call_target="tpu_custom_call" | custom-call | flops 1000000000 | bytes 1048576 | tf_op jit(solution)/shard_map/scatter_norm/pallas_call | solution.py:772
  658.0 6.9 convert_element_type.76
  664.9 4.3 convert_element_type.77
  669.2 4.4 convert_element_type.78
  673.6 44.1 %line_sum.1 = f32[8,16,2048]{2,1,0:T(8,128)} custom-call(bf16[4,2,8,16,2048]{4,3,2,1,0:T(8,128)(2,1)} %bitcast.60), custom_call_target="tpu_custom_call" | custom-call | flops 1000000000 | bytes 1048576 | tf_op jit(solution)/shard_map/line_sum/pallas_call | solution.py:1172
  717.7 2.5 multiply_reduce_fusion.1
  720.8 4.3 convert_element_type.72
  725.2 2.6 convert_element_type.73
  727.8 2.6 convert_element_type.74
  730.4 2.7 convert_element_type.75
  (82 shorter events, 17.0 us)
Async XLA Ops:
  7.2 1.6 copy-start
  7.2 133.3 %all-gather.3.cloned.1.call-start = ((), (), s32[]{:S(2)}) async-start(), calls=%async_computation | async-start | bytes 9437184 | tf_op jit(solution)/shard_map/all_gather | solution.py:1336
  9.5 23.2 %copy-start.13 = (bf16[4,512]{1,0:T(4,128)(2,1)S(1)}, bf16[4,512]{1,0:T(4,128)(2,1)}, u32[]{:S(2)}) copy-start(bf16[4,512]{1,0:T(4,128)(2,1)} %param.22) | copy-start | bytes 12292
  9.5 23.3 %copy-start.14 = (f32[256,2]{0,1:T(2,128)S(1)}, f32[256,2]{0,1:T(2,128)}, u32[]{:S(2)}) copy-start(f32[256,2]{0,1:T(2,128)} %param.16) | copy-start | bytes 6148
  9.5 23.3 %copy-start.15 = (s32[256,2]{0,1:T(2,128)S(1)}, s32[256,2]{0,1:T(2,128)}, u32[]{:S(2)}) copy-start(s32[256,2]{0,1:T(2,128)} %param.15) | copy-start | bytes 6148
  32.7 231.8 %all-gather.5.cloned.1.call-start = ((), (), s32[]{:S(2)}) async-start(), calls=%async_computation.1 | async-start | bytes 5242880 | tf_op jit(solution)/shard_map/all_gather | solution.py:1347
  115.1 421.6 %all-reduce.9.cloned.1.call-start = ((), (), s32[]{:S(2)}) async-start(), calls=%async_computation.3 | async-start | bytes 25165824 | tf_op jit(solution)/shard_map/psum | solution.py:1358
  325.1 1.2 copy-start.5
  325.1 395.7 %all-reduce.7.cloned.1.call-start = ((), (), s32[]{:S(2)}) async-start(), calls=%async_computation.2 | async-start | bytes 16777216 | tf_op jit(solution)/shard_map/psum | solution.py:1396
  523.6 2.8 copy-start.16
  526.4 2.5 copy-start.23
  529.7 2.2 copy-start.12
  529.7 3.3 copy-start.21
  532.9 3.7 copy-start.17
  536.6 7.2 copy-start.20
  536.6 7.2 copy-start.22
  543.8 3.7 copy-start.18
  543.8 3.7 copy-start.19
  553.3 3.9 copy-start.6
  658.0 6.9 copy-start.4
  664.9 4.3 copy-start.3
  673.6 44.1 %copy-start.2 = (f32[256,2048]{1,0:T(8,128)S(1)}, f32[256,2048]{1,0:T(8,128)}, u32[]{:S(2)}) copy-start(f32[256,2048]{1,0:T(8,128)} %get-tuple-element.120) | copy-start | bytes 6291460
  673.6 44.1 %copy-start.11 = (f32[8,16,2048]{2,1,0:T(8,128)S(1)}, f32[8,16,2048]{2,1,0:T(8,128)}, u32[]{:S(2)}) copy-start(f32[8,16,2048]{2,1,0:T(8,128)} %get-tuple-element.99) | copy-start | bytes 3145732
  720.8 4.4 copy-start.9
  725.2 2.6 copy-start.8
  727.8 2.6 copy-start.7
  730.4 2.7 copy-start.10
  730.4 4.1 copy-start.1
Sparse Core Ops, SparseCore 0:
  32.8 56.3 all-gather.2
  115.2 103.1 all-gather.4
  325.2 180.7 all-reduce.8
  567.5 129.1 all-reduce.6

commit v5 on v4

--- a/solution.py
+++ b/solution.py
@@ -346,22 +346,42 @@
 
 def attention_back_kernel(
     n, steps, width, limit_ref, q_ref, k_ref, v_ref, g_ref, q_raw, k_raw, factors, cosine, sine,
-    gains, sum_hbm, q_grad, k_grad, v_grad, gain_out, own_sum,
-    dq_acc, dk_acc, k_acc, v_acc, inner_all, inner_send, inner_recv, part, *line,
+    gains, wq, wk, wv, normed_hbm, sum_hbm, gq_out, gk_out, gv_out, normed_out, gain_out, own_sum,
+    dq_acc, dk_acc, k_acc, v_acc, q_grad, k_grad, v_grad, columns, turned, staged,
+    inner_all, inner_send, inner_recv, column_sem, staged_sem, part, *line,
 ):
     length, local = q_ref.shape
+    strips = width // local
     heads = local // HEAD_DIM
     block = 256
     blocks = length // block
     scale = HEAD_DIM**-0.5
     load_sem = line[-1]
     turn, drain = line_sum(n, steps, part, own_sum, *line[:-1])
-    load = pltpu.make_async_copy(sum_hbm.at[:, 1], part, load_sem.at[0])
+    load = pltpu.make_async_copy(sum_hbm, part, load_sem.at[0])
     load.start()
     d, z, peers = others(n)
     greet(peers)
+
+    def strip(b):
+        c = pl.ds(pl.multiple_of(b * local, local), local)
+        return pltpu.make_async_copy(
+            normed_hbm.at[:, c], columns.at[lax.rem(b, 2)], column_sem.at[lax.rem(b, 2)]
+        )
+
+    strip(0).start()
     load.wait()
-    slots = -(-(steps + n - 1) // heads)
+    turns = steps + n - 1
+    in_heads, in_parts = 8 * turns // 19, 4 * turns // 19
+    slots = -(-in_heads // heads)
+    in_strips = turns - heads * slots - in_parts - 2
+
+    def take(first, count, i, of):
+        def one(t, carry):
+            turn(first + t)
+            return carry
+
+        lax.fori_loop(i * count // of, (i + 1) * count // of, one, 0)
     limit = limit_ref[0:1, 0:1]
     lanes = lax.broadcasted_iota(jnp.int32, (block, 128), 1)
 
@@ -428,7 +448,7 @@
         )
         copy.start()
         copies.append(copy)
-    drain()
+    turn(heads * slots)
     for p in range(1, n):
         o = lax.rem(z + n - p, n)
         pltpu.make_async_remote_copy(
@@ -449,34 +469,91 @@
         return carry
 
     lax.fori_loop(0, blocks, raw, 0)
+    turn(heads * slots + 1)
+
+    def save(i):
+        r = pl.ds(pl.multiple_of(i * block, block), block)
+        return pltpu.make_async_copy(
+            staged.at[lax.rem(i, 2)], normed_out.at[r, :], staged_sem.at[lax.rem(i, 2)]
+        )
+
+    def rows_back(i, carry):
+        r = pl.ds(pl.multiple_of(i * block, block), block)
+
+        @pl.when(i >= 2)
+        def _():
+            save(i - 2).wait()
+
+        staged[lax.rem(i, 2)] = (
+            dot_nt(q_grad[r, :], wq[...])
+            + dot_nt(k_grad[r, :], wk[...])
+            + dot_nt(v_grad[r, :], wv[...])
+        ).astype(bf16)
+        save(i).start()
+        take(heads * slots + 2, in_parts, i, blocks)
+        return carry
+
+    lax.fori_loop(0, blocks, rows_back, 0)
+
+    def strip_grads(b, carry):
+        strip(b).wait()
+
+        @pl.when(b + 1 < strips)
+        def _():
+            strip(b + 1).start()
+
+        turned[...] = columns[lax.rem(b, 2)].T
+        c = pl.ds(pl.multiple_of(b * local, local), local)
+        gq_out[c, :] = dot(turned[...], q_grad[...]).astype(bf16)
+        gk_out[c, :] = dot(turned[...], k_grad[...]).astype(bf16)
+        gv_out[c, :] = dot(turned[...], v_grad[...]).astype(bf16)
+        take(heads * slots + 2 + in_parts, in_strips, b, strips)
+        return carry
+
+    lax.fori_loop(0, strips, strip_grads, 0)
+    drain()
+    for i in range(max(blocks - 2, 0), blocks):
+        save(i).wait()
     for copy in copies:
         copy.wait_send()
 
 
 def attention_back(
-    n, width, limit, q, k, v, g, q_raw, k_raw, factors, cosine, sine, gains, sum_halves
+    n, width, limit, q, k, v, g, q_raw, k_raw, factors, cosine, sine, gains, wq, wk, wv, normed,
+    sum_parts,
 ):
     length, local = q.shape
-    _, _, steps, R, D = sum_halves.shape
+    _, steps, R, D = sum_parts.shape
+    hbm = pl.BlockSpec(memory_space=pl.ANY)
     vmem = pl.BlockSpec(memory_space=pltpu.VMEM)
     dma = pltpu.SemaphoreType.DMA
-    grad = jax.ShapeDtypeStruct((length, local), bf16)
+    weight = jax.ShapeDtypeStruct((D, local), bf16)
+    raw = pltpu.VMEM((length, local), bf16)
     return pl.pallas_call(
         functools.partial(attention_back_kernel, n, steps, width),
         out_shape=[
-            grad, grad, grad, jax.ShapeDtypeStruct((2, local), f32),
+            weight, weight, weight, jax.ShapeDtypeStruct((length, D), bf16),
+            jax.ShapeDtypeStruct((2, local), f32),
             jax.ShapeDtypeStruct((steps, R, D), f32),
         ],
-        in_specs=[vmem] * 11 + [pl.BlockSpec(memory_space=pl.ANY)],
-        out_specs=[vmem] * 5,
+        in_specs=[vmem] * 14 + [hbm, hbm],
+        out_specs=[vmem, vmem, vmem, hbm, vmem, vmem],
         scratch_shapes=[
             pltpu.VMEM((length, local), f32),
             pltpu.VMEM((length, local), f32),
             pltpu.VMEM((length, HEAD_DIM), f32),
             pltpu.VMEM((length, HEAD_DIM), f32),
+            raw,
+            raw,
+            raw,
+            pltpu.VMEM((2, length, local), bf16),
+            pltpu.VMEM((local, length), bf16),
+            pltpu.VMEM((2, 256, D), bf16),
             pltpu.VMEM((n, length // 256, 8, 256), f32),
             dma((n,)),
             dma((n,)),
+            dma((2,)),
+            dma((2,)),
         ]
         + line_scratch(n, steps, R, D),
         compiler_params=pltpu.CompilerParams(
@@ -486,7 +563,9 @@
             flops=2 * 10**9, bytes_accessed=2**20, transcendentals=0
         ),
         name="attention_back",
-    )(limit, q, k, v, g, q_raw, k_raw, factors, cosine, sine, gains, sum_halves)
+    )(
+        limit, q, k, v, g, q_raw, k_raw, factors, cosine, sine, gains, wq, wk, wv, normed, sum_parts
+    )
 
 
 def scatter_norm_kernel(n, groups, steps, gather, *refs):
@@ -1014,23 +1093,24 @@
     )(x, g, combine, gate_w, up_w, down_w)
 
 
-def line_sum(n, steps, part, out, from_below, from_above, up_send, up_recv, down_send, down_recv):
+def line_sum(n, steps, part, out, landed, up_send, up_recv, down_send, down_recv):
     d, z = lax.axis_index("dp"), lax.axis_index("shard")
     upper, lower = (d, lax.rem(z + 1, n)), (d, lax.rem(z + n - 1, n))
 
     def move_up(src, o, k):
         return pltpu.make_async_remote_copy(
-            src_ref=src.at[o, k], dst_ref=from_below.at[o, k], send_sem=up_send.at[o, k],
+            src_ref=src.at[o, k], dst_ref=landed.at[o, k], send_sem=up_send.at[o, k],
             recv_sem=up_recv.at[o, k], device_id=upper, device_id_type=MESH,
         )
 
     def move_down(src, o, k):
+        slot = jnp.where(o == z - 1, n, o)
         return pltpu.make_async_remote_copy(
-            src_ref=src.at[o, k], dst_ref=from_above.at[o, k], send_sem=down_send.at[o, k],
+            src_ref=src.at[o, k], dst_ref=landed.at[slot, k], send_sem=down_send.at[o, k],
             recv_sem=down_recv.at[o, k], device_id=lower, device_id_type=MESH,
         )
 
-    def passing(move, landed, first, owner):
+    def passing(move, first, owner):
         def run(k):
             def far(i, carry):
                 o = owner(i)
@@ -1054,8 +1134,8 @@
 
         return run
 
-    pass_up = passing(move_up, from_below, 0, lambda i: z + n - 1 - i)
-    pass_down = passing(move_down, from_above, n - 1, lambda i: z - n + 1 + i)
+    pass_up = passing(move_up, 0, lambda i: z + n - 1 - i)
+    pass_down = passing(move_down, n - 1, lambda i: z - n + 1 + i)
 
     def own(k):
         @pl.when(z > 0)
@@ -1064,7 +1144,7 @@
 
         @pl.when(z == 0)
         def _():
-            from_below[z, k] = jnp.zeros(part.shape[2:], bf16)
+            landed[z, k] = jnp.zeros(part.shape[2:], bf16)
 
         @pl.when(z < n - 1)
         def _():
@@ -1072,11 +1152,9 @@
 
         @pl.when(z == n - 1)
         def _():
-            from_above[z, k] = jnp.zeros(part.shape[2:], bf16)
-
-        out[k] = (
-            part[z, k].astype(f32) + from_below[z, k].astype(f32) + from_above[z, k].astype(f32)
-        )
+            landed[n, k] = jnp.zeros(part.shape[2:], bf16)
+
+        out[k] = part[z, k].astype(f32) + landed[z, k].astype(f32) + landed[n, k].astype(f32)
 
     def turn(t):
         up_k, down_k, own_k = t - z, t - (n - 1 - z), t - (n - 1)
@@ -1114,7 +1192,8 @@
 
 def line_scratch(n, steps, R, D):
     dma = pltpu.SemaphoreType.DMA
-    return [pltpu.VMEM((n, steps, R, D), bf16)] * 3 + [dma((n, steps))] * 4 + [dma((1,))]
+    slots = [pltpu.VMEM((n, steps, R, D), bf16), pltpu.VMEM((n + 1, steps, R, D), bf16)]
+    return slots + [dma((n, steps))] * 4 + [dma((1,))]
 
 
 def expert_grads_kernel(x_ref, g_ref, hidden, gate_grad, up_grad, gate_out, up_out, down_out, xt):
@@ -1149,38 +1228,30 @@
     )(x, g, hidden, gate_grad, up_grad)
 
 
-def line_sum_kernel(n, half, sum_hbm, own_sum, part, *line):
-    steps = part.shape[1]
-    load_sem = line[-1]
-    load = pltpu.make_async_copy(sum_hbm.at[:, half], part, load_sem.at[0])
-    load.start()
-    _, _, peers = others(n)
-    greet(peers)
-    load.wait()
-    turn, drain = line_sum(n, steps, part, own_sum, *line[:-1])
-
-    def one(t, carry):
-        turn(t)
-        return carry
-
-    lax.fori_loop(0, steps + n - 1, one, 0)
-    drain()
-
-
-def line_sum_alone(n, half, sum_halves):
-    _, _, steps, R, D = sum_halves.shape
-    return pl.pallas_call(
-        functools.partial(line_sum_kernel, n, half),
-        out_shape=jax.ShapeDtypeStruct((steps, R, D), f32),
-        in_specs=[pl.BlockSpec(memory_space=pl.ANY)],
-        out_specs=pl.BlockSpec(memory_space=pltpu.VMEM),
-        scratch_shapes=line_scratch(n, steps, R, D),
-        compiler_params=pltpu.CompilerParams(
-            collective_id=5, has_side_effects=True, vmem_limit_bytes=VMEM_LIMIT
+def widen_kernel(count, *refs):
+    for src, dst in zip(refs[:count], refs[count:]):
+        dst[...] = src[...].astype(f32)
+
+
+def widen(*arrays):
+    flat = [v.reshape(-1, v.shape[-1]) for v in arrays]
+    steps = 8
+    specs = [
+        pl.BlockSpec((v.shape[0] // steps, v.shape[1]), lambda i: (i, 0)) for v in flat
+    ]
+    out = pl.pallas_call(
+        functools.partial(widen_kernel, len(flat)),
+        out_shape=[jax.ShapeDtypeStruct(v.shape, f32) for v in flat],
+        grid=(steps,),
+        in_specs=specs,
+        out_specs=specs,
+        compiler_params=pltpu.CompilerParams(vmem_limit_bytes=VMEM_LIMIT),
+        cost_estimate=pl.CostEstimate(
+            flops=0, bytes_accessed=sum(6 * v.size for v in flat), transcendentals=0
         ),
-        cost_estimate=pl.CostEstimate(flops=10**9, bytes_accessed=2**20, transcendentals=0),
-        name="line_sum",
-    )(sum_halves)
+        name="widen",
+    )(*flat)
+    return tuple(v.reshape(w.shape) for v, w in zip(out, arrays))
 
 
 def gather_line_kernel(n, v_hbm, out, slots, load_sem, up_sem, down_sem, recv_sem, out_sem):
@@ -1348,7 +1419,7 @@
     sum_part, in_part, hidden, gate_grad, up_grad = experts_pass(
         expert_in, g_all, combine, expert_gate, expert_up, expert_down
     )
-    sum_halves = sum_part.reshape(shards, 2, 8, rows // 16, width)
+    sum_parts = sum_part.reshape(shards, 16, rows // 16, width)
     grad_gate, grad_up, grad_down = expert_grads(
         expert_in, g_all, hidden, gate_grad, up_grad, experts
     )
@@ -1366,31 +1437,25 @@
     attended_grad = attended_grad.reshape(length, width)
 
     own_columns = lax.dynamic_slice_in_dim(attended_grad, place * local, local, 1)
-    grad_output = jnp.concatenate([dot_tn(mixed_all[s], own_columns) for s in range(shards)], 0)
+    grad_output = lax.dot_general(
+        mixed_all, own_columns, (((1,), (0,)), ((), ())), preferred_element_type=f32
+    ).reshape(width, local)
     mixed_grad = dot_nt(
         attended_grad, lax.dynamic_slice_in_dim(full_output, place * local, local, 0)
     ).astype(bf16)
     limit = jnp.broadcast_to(prefix.reshape(1, 1), (8, 128))
-    query_raw_grad, key_raw_grad, value_raw_grad, gain_grad_heads, sum_second = attention_back(
+    grad_query, grad_key, grad_value, normed_part, gain_grad_heads, expert_sum = attention_back(
         shards, width, limit, queries, keys, values, mixed_grad, query_raw, key_raw, factors,
-        cosine, sine, head_gains, sum_halves,
-    )
-    query_raw_grad, key_raw_grad, grad_gate, grad_up, grad_down = lax.optimization_barrier(
-        (query_raw_grad, key_raw_grad, grad_gate, grad_up, grad_down)
-    )
-    normed_part = (
-        dot_nt(query_raw_grad, query_weight)
-        + dot_nt(key_raw_grad, key_weight)
-        + dot_nt(value_raw_grad, value_weight)
-    )
-    grad_query = dot_tn(normed, query_raw_grad)
-    grad_key = dot_tn(normed, key_raw_grad)
-    grad_value = dot_tn(normed, value_raw_grad)
-
-    attention_grads, normed_part = lax.optimization_barrier(
+        cosine, sine, head_gains, query_weight, key_weight, value_weight, normed, sum_parts,
+    )
+    expert_sum = expert_sum.reshape(rows, width)
+    attention_grads, normed_part, grad_gate, grad_up, grad_down = lax.optimization_barrier(
         (
-            tuple(v.astype(bf16) for v in (grad_query, grad_key, grad_value, grad_output)),
-            normed_part.astype(bf16),
+            (grad_query, grad_key, grad_value, grad_output.astype(bf16)),
+            normed_part,
+            grad_gate,
+            grad_up,
+            grad_down,
         )
     )
     grad_query, grad_key, grad_value, grad_output = lax.psum(attention_grads, "dp")
@@ -1400,25 +1465,25 @@
     )
     grad_tokens = grad_tokens.reshape(rows, width)
     grad_gains = grad_gains[:4]
-    sum_halves, grad_tokens = lax.optimization_barrier((sum_halves, grad_tokens))
-    sum_first = line_sum_alone(shards, 0, sum_halves)
-    expert_sum = jnp.concatenate(
-        [sum_first.reshape(rows // 2, width), sum_second.reshape(rows // 2, width)], 0
-    )
     output = residual_own + expert_sum
     root_means = jnp.stack([root_mean(attended_own), root_mean(expert_sum), root_mean(output)])
+    grad_gate, grad_up, grad_down = widen(grad_gate, grad_up, grad_down)
+    grad_query, grad_key, grad_value, grad_output = widen(
+        grad_query, grad_key, grad_value, grad_output
+    )
+
     return (
         output.astype(bf16),
         grad_tokens,
         root_means,
-        grad_query.astype(f32),
-        grad_key.astype(f32),
-        grad_value.astype(f32),
-        grad_output.astype(f32),
+        grad_query,
+        grad_key,
+        grad_value,
+        grad_output,
         grad_gains,
-        grad_gate.astype(f32),
-        grad_up.astype(f32),
-        grad_down.astype(f32),
+        grad_gate,
+        grad_up,
+        grad_down,
     )
 
 

time: 756 us -> 709 us (0.938); the launches traced: 741 us -> 706 us
  matrix products: 47.1 us -> 13 us
  other arithmetic: 40.4 us -> 11.6 us
  waiting for transfers between devices: 0.09 us -> 16.6 us
  Pallas kernels: 623 us -> 633 us
    convert_element_type x7 -> x0, other arithmetic: 27.9 us -> none  [the longest x1 6.88 us: per_device(): grad_gate.astype(f32)]
    pallas_call x1, Pallas kernels: 62.5 us -> 90.3 us  [attention_back(): pl.pallas_call(functools.partial(attention_back_kernel, n, steps, width),...]
    dot_general x4 -> x1, matrix products: 29.8 us -> 6.86 us  [dot_nt(): lax.dot_general(a, b, (((1,), (1,)), ((), ())), preferred_element_type=f32)]
    pallas_call x1 -> x2, Pallas kernels: 44.1 us -> 24.3 us  [widen(): pl.pallas_call(functools.partial(widen_kernel, len(flat)), out_shape=[jax...]
    psum x1, waiting for transfers between devices: 0.01 us -> 16.5 us  [per_device(): lax.psum(attention_grads, 'dp')]
    dot_general x7 -> x1, matrix products: 17.3 us -> 6.19 us  [per_device(): lax.dot_general(mixed_all, own_columns, (((1,), (0,)), ((), ())), preferr...]
  transfers between devices with their start and end apart: 4 -> 4, of which waited for: 0 -> 1; matrix products, arithmetic and copies ran while one was open for 7% -> 4% of each run, Pallas kernels for 73% -> 77%
where the time goes in v5:
time: 709 us; the launch traced here: 706 us
  Pallas kernels  633 us (89%)
  local copies, waits for them, and re-layouts  16.9 us (2%)
  waiting for transfers between devices  16.6 us (2%)
  between operations  14.6 us (2%)
  matrix products  13 us (2%)
  other arithmetic  11.6 us (2%)
    pallas_call x2, Pallas kernels, scatter_norm(): pl.pallas_call(functools.partial(scatter_norm_kernel, n, groups, steps, g...  216 us
    pallas_call x1, Pallas kernels, gather_mix(): pl.pallas_call(functools.partial(gather_mix_kernel, n), out_shape=[jax.Sh...  124 us
    pallas_call x1, Pallas kernels, attention_back(): pl.pallas_call(functools.partial(attention_back_kernel, n, steps, width),...  90.3 us
    pallas_call x1, Pallas kernels, gather_project(): pl.pallas_call(functools.partial(gather_project_kernel, n), out_shape=[ja...  81.6 us
    pallas_call x1, Pallas kernels, experts_pass(): pl.pallas_call(experts_kernel, out_shape=[wide, wide, narrow, narrow, nar...  40 us
    pallas_call x2, Pallas kernels, widen(): pl.pallas_call(functools.partial(widen_kernel, len(flat)), out_shape=[jax...  24.3 us
    pallas_call x1, Pallas kernels, gather_line(): pl.pallas_call(functools.partial(gather_line_kernel, n), out_shape=jax.Sh...  20.8 us
    pallas_call x1, Pallas kernels, expert_grads(): pl.pallas_call(expert_grads_kernel, out_shape=[grad, grad, jax.ShapeDtype...  20.4 us
  transfers between devices with their start and end apart: 4, of which 1 were waited for; matrix products, arithmetic and copies ran while one was open for 4% of the time, Pallas kernels for 77%

profile of v5, /device:TPU:12, one launch (start us, length us, event | category | flops | bytes accessed | tf_op | source)
XLA Modules:
  0.0 706.1 jit_solution(2307400178822031920)
XLA Ops:
  7.2 1.5 copy-done
  8.8 0.7 constant_dynamic-slice_fusion.v_hbm
  9.5 20.8 %gather_line.1 = bf16[4,256,512]{2,1,0:T(8,128)(2,1)} custom-call(bf16[256,512]{1,0:T(8,128)(2,1)} %constant_dynamic-slice_fusion.v_hbm), custom_call_target="tpu_custom_call" | custom-call | flops 20000000000 | bytes 2097152 | tf_op jit(solution)/shard_map/gather_line/pallas_call | solution.py:1336
  30.4 2.3 copy.35
  33.5 81.6 %gather_project.1 = (bf16[4,256,2048]{2,1,0:T(8,128)(2,1)}, bf16[4,256,2048]{2,1,0:T(8,128)(2,1)}, f32[4,256,512]{2,1,0:T(8,128)}, f32[4,256,512]{2,1,0:T(8,128)...) custom-call(bf16[256,2048]{1,0:T(8,128)(2,1)} %x_hbm.1, ...), custom_call_target="tpu_custom_call" | custom-call | flops 80000000000 | bytes 33554432 | tf_op jit(solution)/shard_map/gather_project/pallas_call | solution.py:241
  115.8 1.5 fusion.11
  117.3 0.8 slice_bitcast_fusion
  118.1 0.8 rsqrt_bitcast_fusion
  118.8 1.0 copy.30
  120.5 1.0 copy.32
  121.5 1.9 fusion.8
  123.4 1.4 pad_maximum_fusion
  124.8 15.8 %attention.1 = (bf16[1024,512]{1,0:T(8,128)(2,1)}, bf16[1024,512]{1,0:T(8,128)(2,1)}, bf16[1024,512]{1,0:T(8,128)(2,1)}) custom-call(s32[1]{0:T(128)} %copy.44.prefix, f32[1024,512]{1,0:T(8,128)} %bitcast.64, f32[1024,512]{1,0:T(8,128)} %bitcast.66, bf16[1024,512]{1,0:T(8,128)(2,1)} %bitcast.68, f32[1024,2]{1,0:T(8,128)} %bitcast.59, ...), custom_call_target="tpu_custom_call" | custom-call | flops 14000000000 | bytes 16777216 | tf_op jit(solution)/shard_map/attention/pallas_call | solution.py:329
  140.6 123.9 %gather_mix.1 = (bf16[4,1024,512]{2,1,0:T(8,128)(2,1)}, bf16[1024,2048]{1,0:T(8,128)(2,1)}, f32[256,2048]{1,0:T(8,128)}) custom-call(bf16[1024,512]{1,0:T(8,128)(2,1)} %get-tuple-element.69.mixed_hbm, bf16[2048,2048]{1,0:T(8,128)(2,1)} %all-gather.3.cloned.1.call-done.weight_hbm, bf16[1024,2048]{1,0:T(8,128)(2,1)} %bitcast.83, f32[1,2048]{1,0:T(1,128)} %bitcast.73), custom_call_target="tpu_custom_call" | custom-call | flops 99999997952 | bytes 33554432 | tf_op jit(solution)/shard_map/gather_mix/pallas_call | solution.py:997
  264.5 40.0 %experts_pass.1 = (bf16[1024,2048]{1,0:T(8,128)(2,1)}, bf16[1024,2048]{1,0:T(8,128)(2,1)}, bf16[1024,1024]{1,0:T(8,128)(2,1)}, bf16[1024,1024]{1,0:T(8,128)(2,1)}, bf16[1024,1024]{1,0:T(8,128)(2,1)}) custom-call(bf16[1024,2048]{1,0:T(8,128)(2,1)} %get-tuple-element.75.x_ref, bf16[1024,2048]{1,0:T(8,128)(2,1)} %all-gather.5.cloned.1.call-done.g_ref, ...), custom_call_target="tpu_custom_call" | custom-call | flops 25769803776 | bytes 41943040 | tf_op jit(solution)/shard_map/experts_pass/pallas_call | solution.py:1078
  304.6 20.4 %expert_grads.1 = (bf16[4,2048,256]{2,1,0:T(8,128)(2,1)}, bf16[4,2048,256]{2,1,0:T(8,128)(2,1)}, bf16[4,256,2048]{2,1,0:T(8,128)(2,1)}) custom-call(bf16[1024,2048]{1,0:T(8,128)(2,1)} %get-tuple-element.75.x_ref, bf16[1024,2048]{1,0:T(8,128)(2,1)} %all-gather.5.cloned.1.call-done.g_ref, bf16[1024,1024]{1,0:T(8,128)(2,1)} %get-tuple-element.78.hidden, ...), custom_call_target="tpu_custom_call" | custom-call | flops 12884901888 | bytes 27262976 | tf_op jit(solution)/shard_map/expert_grads/pallas_call | solution.py:1216
  325.0 1.1 copy-done.3
  326.2 0.7 copy-done.4
  326.9 1.6 multiply_reduce_fusion.2
  328.4 124.8 %scatter_norm_gather.1 = (f32[16,16,2048]{2,1,0:T(8,128)}, bf16[4,16,16,2048]{3,2,1,0:T(8,128)(2,1)}, f32[8,2048]{1,0:T(8,128)}) custom-call(bf16[4,16,16,2048]{3,2,1,0:T(8,128)(2,1)} %bitcast.53, f32[16,16,2048]{2,1,0:T(8,128)} %bitcast.48, bf16[16,16,2048]{2,1,0:T(8,128)(2,1)} %bitcast.55, f32[1,2048]{1,0:T(1,128)} %bitcast.74), custom_call_target="tpu_custom_call" | custom-call | flops 1000000000 | bytes 1048576 | tf_op jit(solution)/shard_map/scatter_norm_gather/pallas_call | solution.py:851
  453.3 6.9 fusion.2.g_ref
  460.7 90.3 %attention_back.1 = (bf16[2048,512]{1,0:T(8,128)(2,1)}, bf16[2048,512]{1,0:T(8,128)(2,1)}, bf16[2048,512]{1,0:T(8,128)(2,1)}, bf16[1024,2048]{1,0:T(8,128)(2,1)}...) custom-call(s32[8,128]{1,0:T(8,128)} %broadcast_in_dim.27.limit_ref, bf16[1024,512]{1,0:T(8,128)(2,1)} %get-tuple-element.73.q_ref, ...), custom_call_target="tpu_custom_call" | custom-call | flops 2000000000 | bytes 1048576 | tf_op jit(solution)/shard_map/attention_back/pallas_call | solution.py:532
  551.1 6.2 convolution_convert_fusion
  557.3 1.9 multiply_reduce_fusion.1
  559.5 2.8 multiply_reduce_fusion
  562.3 0.6 pad_maximum_fusion.2
  562.9 91.2 %scatter_norm.1 = (f32[8,32,2048]{2,1,0:T(8,128)}, f32[8,512]{1,0:T(8,128)}) custom-call(bf16[4,8,32,2048]{3,2,1,0:T(8,128)(2,1)} %bitcast.52, bf16[8,32,2048]{2,1,0:T(8,128)(2,1)} %bitcast.58, f32[8,32,2048]{2,1,0:T(8,128)} %bitcast.62, f32[1,2048]{1,0:T(1,128)} %bitcast.72, f32[8,2048]{1,0:T(8,128)} %get-tuple-element.99.refs_4_, ...), custom_call_target="tpu_custom_call" | custom-call | flops 1000000000 | bytes 1048576 | tf_op jit(solution)/shard_map/scatter_norm/pallas_call | solution.py:851
  654.1 1.3 slice.31
  655.4 14.3 %widen.3 = (f32[8192,256]{1,0:T(8,128)}, f32[8192,256]{1,0:T(8,128)}, f32[1024,2048]{1,0:T(8,128)}) custom-call(bf16[8192,256]{1,0:T(8,128)(2,1)} %bitcast.49, bf16[8192,256]{1,0:T(8,128)(2,1)} %bitcast.50, bf16[1024,2048]{1,0:T(8,128)(2,1)} %bitcast.51), custom_call_target="tpu_custom_call" | custom-call | bytes 37748736 | tf_op jit(solution)/shard_map/widen/pallas_call | solution.py:1242
  669.7 16.5 %all-reduce.7.cloned.1.call-done = (bf16[2048,512]{1,0:T(8,128)(2,1)}, bf16[2048,512]{1,0:T(8,128)(2,1)}, bf16[2048,512]{1,0:T(8,128)(2,1)}, bf16[2048,512]{1,0:T(8,128)(2,1)}) async-done(((bf16[2048,512]{1,0:T(8,128)(2,1)}, bf16[2048,512]{1,0:T(8,128)(2,1)}, bf16[2048,512]{1,0:T(8,128)(2,1)}, bf16[2048,512]{1,0:T(8,128)(2,1)}), (bf16[2048,512]{1,0:T(8,128)(2,1)}, bf16[2048,512]{1,0:T(8,128)(2,1)}, ...) | async-done | bytes 8388624 | tf_op jit(solution)/shard_map/psum | solution.py:1461
  686.3 10.0 %widen.2 = (f32[2048,512]{1,0:T(8,128)}, f32[2048,512]{1,0:T(8,128)}, f32[2048,512]{1,0:T(8,128)}, f32[2048,512]{1,0:T(8,128)}) custom-call(bf16[2048,512]{1,0:T(8,128)(2,1)} %get-tuple-element.117.refs_0_, bf16[2048,512]{1,0:T(8,128)(2,1)} %get-tuple-element.118.refs_1_, bf16[2048,512]{1,0:T(8,128)(2,1)} %get-tuple-element.119.refs_2_, ...), custom_call_target="tpu_custom_call" | custom-call | bytes 25165824 | tf_op jit(solution)/shard_map/widen/pallas_call | solution.py:1242
  696.3 3.3 copy.45
  (36 shorter events, 2.4 us)
Async XLA Ops:
  7.2 1.6 copy-start
  7.2 133.4 %all-gather.3.cloned.1.call-start = ((), (), s32[]{:S(2)}) async-start(), calls=%async_computation | async-start | bytes 9437184 | tf_op jit(solution)/shard_map/all_gather | solution.py:1407
  30.3 2.5 copy-start.5
  30.3 2.5 copy-start.6
  30.3 2.5 copy-start.7
  32.7 231.8 %all-gather.5.cloned.1.call-start = ((), (), s32[]{:S(2)}) async-start(), calls=%async_computation.1 | async-start | bytes 5242880 | tf_op jit(solution)/shard_map/all_gather | solution.py:1418
  115.1 442.1 %all-reduce.9.cloned.1.call-start = ((), (), s32[]{:S(2)}) async-start(), calls=%async_computation.3 | async-start | bytes 25165824 | tf_op jit(solution)/shard_map/psum | solution.py:1429
  324.9 1.2 copy-start.3
  324.9 1.9 copy-start.4
  325.0 361.3 %all-reduce.7.cloned.1.call-start = ((), (), s32[]{:S(2)}) async-start(), calls=%async_computation.2 | async-start | bytes 16777216 | tf_op jit(solution)/shard_map/psum | solution.py:1461
  557.3 2.2 copy-start.2
  696.3 3.3 copy-start.1
Sparse Core Ops, SparseCore 0:
  32.8 56.3 all-gather.2
  115.2 103.1 all-gather.4
  325.1 180.7 all-reduce.8
  557.4 128.8 all-reduce.6

commit v6 on v5

--- a/solution.py
+++ b/solution.py
@@ -2,6 +2,7 @@
 
 import jax
 import jax.numpy as jnp
+import numpy as np
 from jax import lax
 from jax.experimental import pallas as pl
 from jax.experimental.pallas import tpu as pltpu
@@ -19,11 +20,14 @@
 
 def rotary_tables(row_count):
     half_dim = HEAD_DIM // 2
-    positions = jnp.arange(row_count, dtype=jnp.int32)
-    inverse = ROPE_BASE ** (-jnp.arange(half_dim, dtype=f32) / half_dim)
-    angles = positions.astype(f32)[:, None] * inverse[None, :]
-    cosine, sine = jnp.cos(angles), jnp.sin(angles)
-    return jnp.concatenate([cosine, cosine], 1), jnp.concatenate([-sine, sine], 1)
+    inverse = ROPE_BASE ** (-np.arange(half_dim) / half_dim)
+    angles = np.arange(row_count)[:, None] * inverse.astype(np.float32).astype(np.float64)[None, :]
+    angles = angles.astype(np.float32).astype(np.float64)
+    cosine, sine = np.cos(angles), np.sin(angles)
+    return (
+        jnp.asarray(np.concatenate([cosine, cosine], 1), f32),
+        jnp.asarray(np.concatenate([-sine, sine], 1), f32),
+    )
 
 
 def row_factor(values):
@@ -67,17 +71,90 @@
     return d, z, [(d, lax.rem(z + p, n)) for p in range(1, n)]
 
 
+def line_gather(n, slots, up_sem, down_sem, recv_sem):
+    d, z = lax.axis_index("dp"), lax.axis_index("shard")
+
+    def send_up(o):
+        return pltpu.make_async_remote_copy(
+            src_ref=slots.at[o], dst_ref=slots.at[o], send_sem=up_sem.at[o],
+            recv_sem=recv_sem.at[o], device_id=(d, lax.rem(z + 1, n)), device_id_type=MESH,
+        )
+
+    def send_down(o):
+        return pltpu.make_async_remote_copy(
+            src_ref=slots.at[o], dst_ref=slots.at[o], send_sem=down_sem.at[o],
+            recv_sem=recv_sem.at[o], device_id=(d, lax.rem(z + n - 1, n)), device_id_type=MESH,
+        )
+
+    def begin():
+        @pl.when(z < n - 1)
+        def _():
+            send_up(z).start()
+
+        @pl.when(z > 0)
+        def _():
+            send_down(z).start()
+
+    def hop(s, landed):
+        below, above = z - s, z + s
+
+        @pl.when((s > 0) & (below >= 0))
+        def _():
+            send_up(below).wait_recv()
+
+            @pl.when(z < n - 1)
+            def _():
+                send_up(below).start()
+
+            landed(below)
+
+        @pl.when((s > 0) & (above < n))
+        def _():
+            send_down(above).wait_recv()
+
+            @pl.when(z > 0)
+            def _():
+                send_down(above).start()
+
+            landed(above)
+
+    def drain():
+        def one(o, carry):
+            @pl.when((z < n - 1) & (o <= z))
+            def _():
+                send_up(o).wait_send()
+
+            @pl.when((z > 0) & (o >= z))
+            def _():
+                send_down(o).wait_send()
+
+            return carry
+
+        lax.fori_loop(0, n, one, 0)
+
+    return begin, hop, drain
+
+
 def gather_project_kernel(
-    n, x_hbm, small_ref, wq_hbm, wk_hbm, wv_hbm,
-    x_out, normed_out, q_out, k_out, v_out, small_out, sq_out,
-    xs, nb, qb, kb, vb, wq, wk, wv, sq_all, small_all,
+    n, x_hbm, small_ref, slab_hbm, wq_hbm, wk_hbm, wv_hbm,
+    x_out, normed_out, q_out, k_out, v_out, slab_out, small_out, sq_out,
+    slabs, xs, nb, qb, kb, vb, wq, wk, wv, sq_all, small_all,
     load_sem, out_sem, up_sem, down_sem, recv_sem, small_send, small_recv, sq_send, sq_recv,
+    slab_up, slab_down, slab_recv, slab_sem,
 ):
     T, D = xs.shape[1:]
     C = qb.shape[2]
     d, z, peers = others(n)
+    slab_load = pltpu.make_async_copy(slab_hbm, slabs.at[z], load_sem.at[4])
+    slab_load.start()
     own_load = pltpu.make_async_copy(x_hbm, xs.at[z], load_sem.at[0])
     own_load.start()
+    slab_begin, slab_hop, slab_drain = line_gather(n, slabs, slab_up, slab_down, slab_recv)
+
+    def slab_save(o):
+        c = pl.ds(pl.multiple_of(o * C, C), C)
+        return pltpu.make_async_copy(slabs.at[o], slab_out.at[:, c], slab_sem.at[o])
+
     loads = [
         pltpu.make_async_copy(src, dst, load_sem.at[i + 1])
         for i, (src, dst) in enumerate(((wq_hbm, wq), (wk_hbm, wk), (wv_hbm, wv)))
@@ -98,6 +175,9 @@
             device_id=(d, lax.rem(z + n - 1, n)), device_id_type=MESH,
         )
 
+    slab_load.wait()
+    slab_begin()
+    slab_save(z).start()
     own_load.wait()
     small_copies = []
     for p, peer in enumerate(peers):
@@ -162,6 +242,7 @@
 
     def step(s, carry):
         below, above = z - s, z + s
+        slab_hop(s, lambda o: slab_save(o).start())
 
         @pl.when((s > 0) & (below >= 0))
         def _():
@@ -206,6 +287,7 @@
     def finish(o, carry):
         for copy in outs(o):
             copy.wait()
+        slab_save(o).wait()
 
         @pl.when((z < n - 1) & (o <= z))
         def _():
@@ -218,21 +300,28 @@
         return carry
 
     lax.fori_loop(0, n, finish, 0)
+    slab_drain()
     for p in range(1, n):
         o = lax.rem(z + n - p, n)
         pltpu.make_async_remote_copy(
             src_ref=sq_all.at[o], dst_ref=sq_all.at[o], send_sem=sq_send.at[p - 1],
             recv_sem=sq_recv.at[o], device_id=(d, o), device_id_type=MESH,
         ).wait_recv()
-    total = sq_all[0]
-    for s in range(1, n):
-        total = total + sq_all[s]
-    sq_out[...] = total
+    def turn_factors(i, carry):
+        total = sq_all[0, i]
+        for s in range(1, n):
+            total = total + sq_all[s, i]
+        total = jnp.concatenate([total, jnp.zeros((120, T), f32)], axis=0).T
+        r = pl.ds(pl.multiple_of(i * T, T), T)
+        sq_out[r, :] = lax.rsqrt(total / D + EPSILON)
+        return carry
+
+    lax.fori_loop(0, n, turn_factors, 0)
     for copy in small_copies + sq_copies:
         copy.wait_send()
 
 
-def gather_project(n, tokens, small, wq, wk, wv):
+def gather_project(n, tokens, small, slab, wq, wk, wv):
     T, D = tokens.shape
     C = wq.shape[1]
     hbm = pl.BlockSpec(memory_space=pl.ANY)
@@ -246,12 +335,14 @@
             jax.ShapeDtypeStruct((n, T, C), f32),
             jax.ShapeDtypeStruct((n, T, C), f32),
             jax.ShapeDtypeStruct((n, T, C), bf16),
+            jax.ShapeDtypeStruct((slab.shape[0], D), bf16),
             jax.ShapeDtypeStruct((n,) + small.shape, f32),
-            jax.ShapeDtypeStruct((n, 8, T), f32),
+            jax.ShapeDtypeStruct((n * T, 128), f32),
         ],
-        in_specs=[hbm, vmem, hbm, hbm, hbm],
-        out_specs=[hbm] * 5 + [vmem] * 2,
+        in_specs=[hbm, vmem, hbm, hbm, hbm, hbm],
+        out_specs=[hbm] * 6 + [vmem] * 2,
         scratch_shapes=[
+            pltpu.VMEM((n,) + slab.shape, bf16),
             pltpu.VMEM((n, T, D), bf16),
             pltpu.VMEM((n, T, D), bf16),
             pltpu.VMEM((n, T, C), f32),
@@ -262,8 +353,12 @@
             pltpu.VMEM((D, C), bf16),
             pltpu.VMEM((n, n, 8, T), f32),
             pltpu.VMEM((n,) + small.shape, f32),
-            dma((4,)),
+            dma((5,)),
             dma((5, n)),
+            dma((n,)),
+            dma((n,)),
+            dma((n,)),
+            dma((n,)),
             dma((n,)),
             dma((n,)),
             dma((n,)),
@@ -277,7 +372,7 @@
         ),
         cost_estimate=pl.CostEstimate(flops=80 * 10**9, bytes_accessed=32 * 2**20, transcendentals=0),
         name="gather_project",
-    )(tokens, small, wq, wk, wv)
+    )(tokens, small, slab, wq, wk, wv)
 
 
 def rope(v, cosine, sine):
@@ -295,10 +390,29 @@
     return jnp.where((col <= row) | (col < limit), s, MASKED)
 
 
-def attention_kernel(prefix, q_raw, k_raw, v_ref, factors, cosine, sine, gains, q_out, k_out, mixed):
+def attention_kernel(
+    n, limit_ref, q_raw, k_raw, v_ref, factors, cosine, sine, gains, first_hbm,
+    q_out, k_out, mixed, first_out, slots, load_sem, up_sem, down_sem, recv_sem, out_sem,
+):
     length = q_raw.shape[0]
     block = 256
-    limit = prefix[0]
+    limit = limit_ref[0:1, 0:1]
+    h, heads = pl.program_id(0), pl.num_programs(0)
+    begin, hop, drain = line_gather(n, slots, up_sem, down_sem, recv_sem)
+    z = lax.axis_index("shard")
+
+    def save(o):
+        return pltpu.make_async_copy(slots.at[o], first_out.at[o], out_sem.at[o])
+
+    @pl.when(h == 0)
+    def _():
+        load = pltpu.make_async_copy(first_hbm, slots.at[z], load_sem.at[0])
+        load.start()
+        _, _, peers = others(n)
+        greet(peers)
+        load.wait()
+        begin()
+        save(z).start()
 
     def turn(raw, out, column, gain):
         def part(i, carry):
@@ -319,36 +433,56 @@
         total = jnp.sum(e, axis=1, keepdims=True)
         mixed[r, :] = (dot(e.astype(bf16), v_ref[0:span, :]) / total).astype(bf16)
 
-
-def attention(prefix, q_raw, k_raw, values, factors, cosine, sine, gains):
+    def hops(s, carry):
+        hop(s, lambda o: save(o).start())
+        return carry
+
+    lax.fori_loop(1 + h * (n - 1) // heads, 1 + (h + 1) * (n - 1) // heads, hops, 0)
+
+    @pl.when(h == heads - 1)
+    def _():
+        drain()
+
+        def finish(o, carry):
+            save(o).wait()
+            return carry
+
+        lax.fori_loop(0, n, finish, 0)
+
+
+def attention(n, limit, q_raw, k_raw, values, factors, cosine, sine, gains, first):
     length, local = q_raw.shape
     heads = local // HEAD_DIM
-    head = pl.BlockSpec((length, HEAD_DIM), lambda h, p: (0, h))
-    whole = lambda a: pl.BlockSpec(a.shape, lambda h, p: (0, 0))
+    head = pl.BlockSpec((length, HEAD_DIM), lambda h: (0, h))
+    whole = lambda a: pl.BlockSpec(a.shape, lambda h: (0, 0))
+    hbm = pl.BlockSpec(memory_space=pl.ANY)
     out = jax.ShapeDtypeStruct((length, local), bf16)
+    dma = pltpu.SemaphoreType.DMA
     return pl.pallas_call(
-        attention_kernel,
-        out_shape=[out] * 3,
-        grid_spec=pltpu.PrefetchScalarGridSpec(
-            num_scalar_prefetch=1,
-            grid=(heads,),
-            in_specs=[
-                head, head, head, whole(factors), whole(cosine), whole(sine),
-                pl.BlockSpec((2, HEAD_DIM), lambda h, p: (0, h)),
-            ],
-            out_specs=[head] * 3,
+        functools.partial(attention_kernel, n),
+        out_shape=[out] * 3 + [jax.ShapeDtypeStruct((n,) + first.shape, bf16)],
+        grid=(heads,),
+        in_specs=[
+            whole(limit), head, head, head, whole(factors), whole(cosine), whole(sine),
+            pl.BlockSpec((2, HEAD_DIM), lambda h: (0, h)), hbm,
+        ],
+        out_specs=[head] * 3 + [hbm],
+        scratch_shapes=[pltpu.VMEM((n,) + first.shape, bf16), dma((1,))] + [dma((n,))] * 4,
+        compiler_params=pltpu.CompilerParams(
+            collective_id=7, has_side_effects=True, vmem_limit_bytes=VMEM_LIMIT
         ),
-        compiler_params=pltpu.CompilerParams(vmem_limit_bytes=VMEM_LIMIT),
-        cost_estimate=pl.CostEstimate(flops=14 * 10**9, bytes_accessed=16 * 2**20, transcendentals=0),
+        cost_estimate=pl.CostEstimate(
+            flops=20 * 10**9, bytes_accessed=16 * 2**20, transcendentals=0
+        ),
         name="attention",
-    )(prefix, q_raw, k_raw, values, factors, cosine, sine, gains)
+    )(limit, q_raw, k_raw, values, factors, cosine, sine, gains, first)
 
 
 def attention_back_kernel(
-    n, steps, width, limit_ref, q_ref, k_ref, v_ref, g_ref, q_raw, k_raw, factors, cosine, sine,
-    gains, wq, wk, wv, normed_hbm, sum_hbm, gq_out, gk_out, gv_out, normed_out, gain_out, own_sum,
-    dq_acc, dk_acc, k_acc, v_acc, q_grad, k_grad, v_grad, columns, turned, staged,
-    inner_all, inner_send, inner_recv, column_sem, staged_sem, part, *line,
+    n, steps, width, limit_ref, q_ref, k_ref, v_ref, q_raw, k_raw, factors, cosine, sine,
+    gains, wq, wk, wv, normed_hbm, sum_hbm, grad_hbm, output_hbm, gq_out, gk_out, gv_out, normed_out, gain_out, own_sum,
+    g_ref, output, dq_acc, dk_acc, k_acc, v_acc, q_grad, k_grad, v_grad, columns, turned, staged,
+    inner_all, inner_send, inner_recv, column_sem, staged_sem, grad_sem, part, *line,
 ):
     length, local = q_ref.shape
     strips = width // local
@@ -358,9 +492,20 @@
     scale = HEAD_DIM**-0.5
     load_sem = line[-1]
     turn, drain = line_sum(n, steps, part, own_sum, *line[:-1])
+    d, z, peers = others(n)
     load = pltpu.make_async_copy(sum_hbm, part, load_sem.at[0])
     load.start()
-    d, z, peers = others(n)
+
+    def grad_rows(i):
+        r = pl.ds(pl.multiple_of(i * block, block), block)
+        return pltpu.make_async_copy(
+            grad_hbm.at[r, :], staged.at[lax.rem(i, 2)], grad_sem.at[lax.rem(i, 2)]
+        )
+
+    own_rows = pl.ds(pl.multiple_of(z * local, local), local)
+    output_load = pltpu.make_async_copy(output_hbm.at[own_rows, :], output, grad_sem.at[2])
+    output_load.start()
+    grad_rows(0).start()
     greet(peers)
 
     def strip(b):
@@ -374,7 +519,8 @@
     turns = steps + n - 1
     in_heads, in_parts = 8 * turns // 19, 4 * turns // 19
     slots = -(-in_heads // heads)
-    in_strips = turns - heads * slots - in_parts - 2
+    past = 1 + heads * slots
+    in_strips = turns - past - in_parts - 2
 
     def take(first, count, i, of):
         def one(t, carry):
@@ -390,6 +536,22 @@
         return carry
 
     lax.fori_loop(0, blocks, clear, 0)
+
+    turn(0)
+    output_load.wait()
+
+    def mixed_rows(i, carry):
+        r = pl.ds(pl.multiple_of(i * block, block), block)
+        grad_rows(i).wait()
+
+        @pl.when(i + 1 < blocks)
+        def _():
+            grad_rows(i + 1).start()
+
+        g_ref[r, :] = dot_nt(staged[lax.rem(i, 2)], output[...]).astype(bf16)
+        return carry
+
+    lax.fori_loop(0, blocks, mixed_rows, 0)
 
     def head(h, carry):
         c = pl.ds(pl.multiple_of(h * HEAD_DIM, HEAD_DIM), HEAD_DIM)
@@ -397,7 +559,7 @@
         v_acc[...] = jnp.zeros_like(v_acc)
         for i in range(blocks):
             for j in range(i * slots // blocks, (i + 1) * slots // blocks):
-                turn(h * slots + j)
+                turn(1 + h * slots + j)
             span = key_span(i, block, length)
             r = pl.ds(i * block, block)
             q, g, k, v = q_ref[r, c], g_ref[r, c], k_ref[0:span, c], v_ref[0:span, c]
@@ -448,7 +610,7 @@
         )
         copy.start()
         copies.append(copy)
-    turn(heads * slots)
+    turn(past)
     for p in range(1, n):
         o = lax.rem(z + n - p, n)
         pltpu.make_async_remote_copy(
@@ -469,7 +631,7 @@
         return carry
 
     lax.fori_loop(0, blocks, raw, 0)
-    turn(heads * slots + 1)
+    turn(past + 1)
 
     def save(i):
         r = pl.ds(pl.multiple_of(i * block, block), block)
@@ -490,7 +652,7 @@
             + dot_nt(v_grad[r, :], wv[...])
         ).astype(bf16)
         save(i).start()
-        take(heads * slots + 2, in_parts, i, blocks)
+        take(past + 2, in_parts, i, blocks)
         return carry
 
     lax.fori_loop(0, blocks, rows_back, 0)
@@ -507,7 +669,7 @@
         gq_out[c, :] = dot(turned[...], q_grad[...]).astype(bf16)
         gk_out[c, :] = dot(turned[...], k_grad[...]).astype(bf16)
         gv_out[c, :] = dot(turned[...], v_grad[...]).astype(bf16)
-        take(heads * slots + 2 + in_parts, in_strips, b, strips)
+        take(past + 2 + in_parts, in_strips, b, strips)
         return carry
 
     lax.fori_loop(0, strips, strip_grads, 0)
@@ -519,8 +681,8 @@
 
 
 def attention_back(
-    n, width, limit, q, k, v, g, q_raw, k_raw, factors, cosine, sine, gains, wq, wk, wv, normed,
-    sum_parts,
+    n, width, limit, q, k, v, q_raw, k_raw, factors, cosine, sine, gains, wq, wk, wv, normed,
+    sum_parts, attended_grad, full_output,
 ):
     length, local = q.shape
     _, steps, R, D = sum_parts.shape
@@ -536,9 +698,11 @@
             jax.ShapeDtypeStruct((2, local), f32),
             jax.ShapeDtypeStruct((steps, R, D), f32),
         ],
-        in_specs=[vmem] * 14 + [hbm, hbm],
+        in_specs=[vmem] * 13 + [hbm] * 4,
         out_specs=[vmem, vmem, vmem, hbm, vmem, vmem],
         scratch_shapes=[
+            raw,
+            pltpu.VMEM((local, D), bf16),
             pltpu.VMEM((length, local), f32),
             pltpu.VMEM((length, local), f32),
             pltpu.VMEM((length, HEAD_DIM), f32),
@@ -554,6 +718,7 @@
             dma((n,)),
             dma((2,)),
             dma((2,)),
+            dma((3,)),
         ]
         + line_scratch(n, steps, R, D),
         compiler_params=pltpu.CompilerParams(
@@ -564,17 +729,19 @@
         ),
         name="attention_back",
     )(
-        limit, q, k, v, g, q_raw, k_raw, factors, cosine, sine, gains, wq, wk, wv, normed, sum_parts
+        limit, q, k, v, q_raw, k_raw, factors, cosine, sine, gains, wq, wk, wv, normed, sum_parts,
+        attended_grad, full_output,
     )
 
 
 def scatter_norm_kernel(n, groups, steps, gather, *refs):
-    part, base, addend, gain = refs[:4]
-    refs = refs[4:]
+    part, base, gain = refs[:3]
+    refs = refs[3:]
     if gather:
-        out, all_out, gain_out = refs[:3]
-        alls, ag_up, ag_down, ag_recv, all_sem = refs[3:8]
-        refs = refs[8:]
+        addend, attended_hbm, hidden, g_all = refs[:4]
+        out, all_out, gain_out, down_out = refs[4:8]
+        alls, ag_up, ag_down, ag_recv, all_sem, attended, load_sem = refs[8:15]
+        refs = refs[15:]
     else:
         expert_gains, head_gains, out, gain_out = refs[:4]
         pieces, landed, sums, piece_send, piece_recv, sum_send, sum_recv = refs[4:11]
@@ -584,7 +751,12 @@
     d, z, peers = others(n)
     upper, lower = (d, lax.rem(z + 1, n)), (d, lax.rem(z + n - 1, n))
     alike = [] if gather else [(lax.rem(d + p, groups), z) for p in range(1, groups)]
+    if gather:
+        load = pltpu.make_async_copy(attended_hbm.at[z], attended, load_sem.at[0])
+        load.start()
     greet(peers + alike)
+    if gather:
+        load.wait()
     gain_acc[...] = jnp.zeros_like(gain_acc)
 
     def move_up(src, o, k):
@@ -674,13 +846,17 @@
             part[z, k].astype(f32) + from_below[z, k].astype(f32) + from_above[z, k].astype(f32)
         )
         rows = base[k].astype(f32)
+        if gather:
+            rows = rows + attended[k]
         factor = lax.rsqrt(jnp.sum(rows * rows, axis=1, keepdims=True) / D + EPSILON)
         unit = rows * factor
         along = total * unit
         gain_acc[...] += jnp.sum(along.reshape(R // 8, 8, D), axis=0)
         weighted = along * gain[...]
         mean = jnp.sum(weighted, axis=1, keepdims=True) / D
-        result = addend[k].astype(f32) + factor * (total * gain[...] - unit * mean)
+        result = factor * (total * gain[...] - unit * mean)
+        if gather:
+            result = result + addend[k].astype(f32)
         out[k] = result
         if gather:
             alls[z, k] = result.astype(bf16)
@@ -735,6 +911,13 @@
 
         if gather:
             forward(own_k)
+            experts, units = down_out.shape[:2]
+            e = t - n
+
+            @pl.when((e >= 0) & (e < experts))
+            def _():
+                c = pl.ds(pl.multiple_of(e * units, units), units)
+                down_out[e] = dot_tn(hidden[:, c], g_all[...]).astype(bf16)
 
         return carry
 
@@ -827,8 +1010,8 @@
             copy.wait()
 
 
-def scatter_norm(n, groups, steps, part, base, addend, gain, other_gains=None):
-    gather = other_gains is None
+def scatter_norm(n, groups, steps, part, base, gain, more=None, other_gains=None):
+    gather = more is not None
     T, D = base.shape
     R = T // steps
     C = D // n
@@ -839,9 +1022,15 @@
     rows = jax.ShapeDtypeStruct((steps, R, D), f32)
     sems = dma((n, steps))
     if gather:
-        own = [slots, sems, sems, sems, dma((n,))]
+        addend, attended, hidden, g_all, experts = more
+        units = hidden.shape[1] // experts
+        more = (
+            addend.reshape(steps, R, D), attended.reshape(n, steps, R, D), hidden, g_all,
+        )
+        own = [slots, sems, sems, sems, dma((n,)), pltpu.VMEM((steps, R, D), f32), dma((1,))]
         outs = [rows, jax.ShapeDtypeStruct((n, steps, R, D), bf16)]
         outs += [jax.ShapeDtypeStruct((8, D), f32)]
+        outs += [jax.ShapeDtypeStruct((experts, units, D), bf16)]
     else:
         own = [
             pltpu.VMEM((n, 8, C), f32), pltpu.VMEM((n, 8, C), f32),
@@ -851,8 +1040,8 @@
     return pl.pallas_call(
         functools.partial(scatter_norm_kernel, n, groups, steps, gather),
         out_shape=outs,
-        in_specs=[vmem] * (4 if gather else 6),
-        out_specs=[vmem, hbm, vmem] if gather else [vmem, vmem],
+        in_specs=[vmem] * 4 + [hbm, vmem, vmem] if gather else [vmem] * 5,
+        out_specs=[vmem, hbm, vmem, vmem] if gather else [vmem, vmem],
         scratch_shapes=own + [slots, slots, pltpu.VMEM((8, D), f32), sems, sems, sems, sems],
         compiler_params=pltpu.CompilerParams(
             collective_id=2 if gather else 3, has_side_effects=True, vmem_limit_bytes=VMEM_LIMIT
@@ -864,233 +1053,190 @@
     )(
         part.reshape(n, steps, R, D),
         base.reshape(steps, R, D),
-        addend.reshape(steps, R, D),
         gain,
-        *(() if gather else other_gains),
-    )
-
-
-def gather_mix_kernel(
-    n, mixed_hbm, weight_hbm, x_ref, gain, mixed_out, in_out, own_out,
-    ms, acc, weight, load_sem, up_sem, down_sem, recv_sem, out_sem,
-):
-    L, C = ms.shape[1:]
-    D = weight.shape[1]
-    T = own_out.shape[0]
-    d, z, peers = others(n)
-    own_load = pltpu.make_async_copy(mixed_hbm, ms.at[z], load_sem.at[0])
-    own_load.start()
-    weight_load = pltpu.make_async_copy(weight_hbm, weight, load_sem.at[1])
-    weight_load.start()
-    greet(peers)
-
-    def send_up(o):
-        return pltpu.make_async_remote_copy(
-            src_ref=ms.at[o], dst_ref=ms.at[o], send_sem=up_sem.at[o], recv_sem=recv_sem.at[o],
-            device_id=(d, lax.rem(z + 1, n)), device_id_type=MESH,
-        )
-
-    def send_down(o):
-        return pltpu.make_async_remote_copy(
-            src_ref=ms.at[o], dst_ref=ms.at[o], send_sem=down_sem.at[o], recv_sem=recv_sem.at[o],
-            device_id=(d, lax.rem(z + n - 1, n)), device_id_type=MESH,
-        )
-
-    own_load.wait()
-
-    @pl.when(z < n - 1)
-    def _():
-        send_up(z).start()
-
-    @pl.when(z > 0)
-    def _():
-        send_down(z).start()
-
-    weight_load.wait()
-    block = 256
-
-    def add(o, first):
-        w = weight[pl.ds(pl.multiple_of(o * C, C), C), :]
-
-        def rows(i, carry):
-            r = pl.ds(pl.multiple_of(i * block, block), block)
-            new = jnp.dot(ms[o, r, :], w, preferred_element_type=f32)
-            acc[r, :] = new if first else acc[r, :] + new
-            return carry
-
-        lax.fori_loop(0, L // block, rows, 0)
-
-    def save(o):
-        return pltpu.make_async_copy(ms.at[o], mixed_out.at[o], out_sem.at[o])
-
-    add(z, True)
-    save(z).start()
-
-    def step(s, carry):
-        below, above = z - s, z + s
-
-        @pl.when(below >= 0)
-        def _():
-            send_up(below).wait_recv()
-
-            @pl.when(z < n - 1)
-            def _():
-                send_up(below).start()
-
-        @pl.when(above < n)
-        def _():
-            send_down(above).wait_recv()
-
-            @pl.when(z > 0)
-            def _():
-                send_down(above).start()
-
-        def side(j, inner):
-            o = z - s + 2 * s * j
-
-            @pl.when((o >= 0) & (o < n))
-            def _():
-                add(o, False)
-                save(o).start()
-
-            return inner
-
-        lax.fori_loop(0, 2, side, 0)
-        return carry
-
-    lax.fori_loop(1, n, step, 0)
-    own_rows = pl.ds(pl.multiple_of(z * T, T), T)
-    own_out[...] = acc[own_rows, :]
-    part = 32
-
-    def norm_rows(i, carry):
-        r = pl.ds(pl.multiple_of(i * part, part), part)
-        v = acc[r, :] + x_ref[r, :].astype(f32)
-        factor = lax.rsqrt(jnp.sum(v * v, axis=1, keepdims=True) / D + EPSILON)
-        in_out[r, :] = (v * factor * gain[...]).astype(bf16)
-        return carry
-
-    lax.fori_loop(0, L // part, norm_rows, 0)
-
-    def finish(o, carry):
-        save(o).wait()
-
-        @pl.when((z < n - 1) & (o <= z))
-        def _():
-            send_up(o).wait_send()
-
-        @pl.when((z > 0) & (o >= z))
-        def _():
-            send_down(o).wait_send()
-
-        return carry
-
-    lax.fori_loop(0, n, finish, 0)
-
-
-def gather_mix(n, mixed, weight, x_all, gain, rows):
-    L, C = mixed.shape
-    D = weight.shape[1]
-    hbm = pl.BlockSpec(memory_space=pl.ANY)
-    vmem = pl.BlockSpec(memory_space=pltpu.VMEM)
-    dma = pltpu.SemaphoreType.DMA
-    return pl.pallas_call(
-        functools.partial(gather_mix_kernel, n),
-        out_shape=[
-            jax.ShapeDtypeStruct((n, L, C), bf16),
-            jax.ShapeDtypeStruct((L, D), bf16),
-            jax.ShapeDtypeStruct((rows, D), f32),
-        ],
-        in_specs=[hbm, hbm, vmem, vmem],
-        out_specs=[hbm, vmem, vmem],
-        scratch_shapes=[
-            pltpu.VMEM((n, L, C), bf16),
-            pltpu.VMEM((L, D), f32),
-            pltpu.VMEM((D, D), bf16),
-            dma((2,)),
-            dma((n,)),
-            dma((n,)),
-            dma((n,)),
-            dma((n,)),
-        ],
-        compiler_params=pltpu.CompilerParams(
-            collective_id=1, has_side_effects=True, vmem_limit_bytes=VMEM_LIMIT
-        ),
-        cost_estimate=pl.CostEstimate(flops=100 * 10**9, bytes_accessed=32 * 2**20, transcendentals=0),
-        name="gather_mix",
-    )(mixed, weight, x_all, gain)
-
-
-def experts_kernel(
-    x_ref, g_ref, combine, gate_w, up_w, down_w,
-    sum_out, in_out, hidden_out, gate_out, up_out, sum_acc, in_acc,
+        *(more if gather else other_gains),
+    )
+
+
+def forward_kernel(
+    mixed, weight, x_ref, gain, combine, gate_w, up_w, down_w,
+    attended_out, in_out, gate_out, up_out, hidden_out, sum_out, gate_t, up_t, down_t,
+    sum_acc,
 ):
     e = pl.program_id(1)
     last = pl.num_programs(1) - 1
-    x, g = x_ref[...], g_ref[...]
-    gate_m, up_m, down_m = gate_w[0], up_w[0], down_w[0]
+    D = in_out.shape[1]
+    C = mixed.shape[2]
+
+    @pl.when(e == 0)
+    def _():
+        total = dot(mixed[0], weight[0:C, :])
+        for s in range(1, mixed.shape[0]):
+            total = total + dot(mixed[s], weight[s * C : (s + 1) * C, :])
+        attended_out[...] = total
+        part = 32
+
+        def rows(i, carry):
+            r = pl.ds(pl.multiple_of(i * part, part), part)
+            v = attended_out[r, :] + x_ref[r, :].astype(f32)
+            factor = lax.rsqrt(jnp.sum(v * v, axis=1, keepdims=True) / D + EPSILON)
+            in_out[r, :] = (v * factor * gain[...]).astype(bf16)
+            return carry
+
+        lax.fori_loop(0, in_out.shape[0] // part, rows, 0)
+
     lane = lax.broadcasted_iota(jnp.int32, combine.shape, 1)
-    weight = jnp.sum(jnp.where(lane == e, combine[...], 0.0), axis=1, keepdims=True)
-    gate_part = dot(x, gate_m)
-    up_part = dot(x, up_m)
-    hidden_grad = dot_nt(g, down_m) * weight
+    share = jnp.sum(jnp.where(lane == e, combine[...], 0.0), axis=1, keepdims=True)
+    @pl.when(pl.program_id(0) == 0)
+    def _():
+        gate_t[0] = gate_w[0].T
+        up_t[0] = up_w[0].T
+        down_t[0] = down_w[0].T
+
+    gate_part = dot(in_out[...], gate_w[0])
+    up_part = dot(in_out[...], up_w[0])
     sig = jax.nn.sigmoid(gate_part)
-    silu = gate_part * sig
-    hidden = (silu * up_part * weight).astype(bf16)
+    silu = gate_part * sig * share
+    gate_out[...] = up_part * sig * (1.0 + gate_part * (1.0 - sig)) * share
+    up_out[...] = silu
+    hidden = (silu * up_part).astype(bf16)
     hidden_out[...] = hidden
-    up_grad = (hidden_grad * silu).astype(bf16)
-    up_out[...] = up_grad
-    gate_grad = (hidden_grad * up_part * sig * (1.0 + gate_part * (1.0 - sig))).astype(bf16)
-    gate_out[...] = gate_grad
-    made = dot(hidden, down_m)
-    back = dot_nt(gate_grad, gate_m) + dot_nt(up_grad, up_m)
+    made = dot(hidden, down_w[0])
 
     @pl.when(e == 0)
     def _():
         sum_acc[...] = made
-        in_acc[...] = back
-
-    @pl.when((e > 0) & (e < last))
+
+    @pl.when(e > 0)
     def _():
         sum_acc[...] += made
-        in_acc[...] += back
-
-    @pl.when((e > 0) & (e == last))
+
+    @pl.when(e == last)
     def _():
-        sum_out[...] = (sum_acc[...] + made).astype(bf16)
-        in_out[...] = (in_acc[...] + back).astype(bf16)
-
-    @pl.when((e == 0) & (e == last))
-    def _():
-        sum_out[...] = made.astype(bf16)
-        in_out[...] = back.astype(bf16)
-
-
-def experts_pass(x, g, combine, gate_w, up_w, down_w):
-    L, D = x.shape
+        sum_out[...] = sum_acc[...].astype(bf16)
+
+
+def forward_pass(mixed, weight, x, gain, combine, gate_w, up_w, down_w):
+    n, L, C = mixed.shape
+    D = x.shape[1]
     E, _, F = gate_w.shape
     block = min(512, L)
     rows = pl.BlockSpec((block, D), lambda i, e: (i, 0))
     units = pl.BlockSpec((block, F), lambda i, e: (i, e))
     column = pl.BlockSpec((1, D, F), lambda i, e: (e, 0, 0))
+    once = pl.Buffered(1)
+    turned = pl.BlockSpec((1, F, D), lambda i, e: (jnp.where(i == 0, e, E - 1), 0, 0))
+    turned_down = pl.BlockSpec((1, D, F), lambda i, e: (jnp.where(i == 0, e, E - 1), 0, 0))
+    return pl.pallas_call(
+        forward_kernel,
+        out_shape=[
+            jax.ShapeDtypeStruct((L, D), f32),
+            jax.ShapeDtypeStruct((L, D), bf16),
+            jax.ShapeDtypeStruct((L, E * F), f32),
+            jax.ShapeDtypeStruct((L, E * F), f32),
+            jax.ShapeDtypeStruct((L, E * F), bf16),
+            jax.ShapeDtypeStruct((L, D), bf16),
+            jax.ShapeDtypeStruct((E, F, D), bf16),
+            jax.ShapeDtypeStruct((E, F, D), bf16),
+            jax.ShapeDtypeStruct((E, D, F), bf16),
+        ],
+        grid=(L // block, E),
+        in_specs=[
+            pl.BlockSpec((n, block, C), lambda i, e: (0, i, 0)),
+            pl.BlockSpec((D, D), lambda i, e: (0, 0), pipeline_mode=once),
+            rows,
+            pl.BlockSpec((1, D), lambda i, e: (0, 0)),
+            pl.BlockSpec((block, combine.shape[1]), lambda i, e: (i, 0)),
+            column, column, pl.BlockSpec((1, F, D), lambda i, e: (e, 0, 0)),
+        ],
+        out_specs=[rows, rows, units, units, units, rows, turned, turned, turned_down],
+        scratch_shapes=[pltpu.VMEM((block, D), f32)],
+        compiler_params=pltpu.CompilerParams(vmem_limit_bytes=VMEM_LIMIT),
+        cost_estimate=pl.CostEstimate(
+            flops=6 * L * D * E * F + 2 * L * D * D, bytes_accessed=50 * 2**20,
+            transcendentals=L * E * F,
+        ),
+        name="forward_pass",
+    )(mixed, weight, x, gain, combine, gate_w, up_w, down_w)
+
+
+def backward_kernel(
+    first, rest, gate_ref, up_ref, gate_hbm, up_hbm, down_t,
+    g_out, in_out, gate_out, up_out, both, turned, load_sem,
+):
+    i, e = pl.program_id(0), pl.program_id(1)
+    last = pl.num_programs(1) - 1
+    F = gate_out.shape[1]
+    half = turned.shape[0] // 2
+    loads = [
+        pltpu.make_async_copy(gate_hbm, turned.at[0:half], load_sem.at[0]),
+        pltpu.make_async_copy(up_hbm, turned.at[half : 2 * half], load_sem.at[1]),
+    ]
+
+    @pl.when((i == 0) & (e == 0))
+    def _():
+        for load in loads:
+            load.start()
+
+    @pl.when(e == 0)
+    def _():
+        few, many = first.shape[1], rest.shape[1]
+        for j in range(first.shape[0]):
+            top = j * (few + many)
+            g_out[top : top + few, :] = first[j]
+            g_out[top + few : top + few + many, :] = rest[j]
+
+    hidden_grad = dot(g_out[...], down_t[0])
+    gate_grad = (hidden_grad * gate_ref[...]).astype(bf16)
+    gate_out[...] = gate_grad
+    both[:, pl.ds(pl.multiple_of(e * F, F), F)] = gate_grad
+    up_grad = (hidden_grad * up_ref[...]).astype(bf16)
+    up_out[...] = up_grad
+    both[:, pl.ds(pl.multiple_of(half + e * F, F), F)] = up_grad
+
+    @pl.when((i == 0) & (e == last))
+    def _():
+        for load in loads:
+            load.wait()
+
+    @pl.when(e == last)
+    def _():
+        in_out[...] = dot(both[...], turned[...]).astype(bf16)
+
+
+def backward_pass(first, rest, gate_by, up_by, gate_t, up_t, down_t):
+    n, few, D = first.shape
+    T = few + rest.shape[1]
+    L = n * T
+    E, F, _ = gate_t.shape
+    block = max(T, min(512, L))
+    owners = block // T
+    rows = pl.BlockSpec((block, D), lambda i, e: (i, 0))
+    units = pl.BlockSpec((block, F), lambda i, e: (i, e))
+    hbm = pl.BlockSpec(memory_space=pl.ANY)
     wide = jax.ShapeDtypeStruct((L, D), bf16)
     narrow = jax.ShapeDtypeStruct((L, E * F), bf16)
     return pl.pallas_call(
-        experts_kernel,
-        out_shape=[wide, wide, narrow, narrow, narrow],
+        backward_kernel,
+        out_shape=[wide, wide, narrow, narrow],
         grid=(L // block, E),
         in_specs=[
-            rows, rows, pl.BlockSpec((block, combine.shape[1]), lambda i, e: (i, 0)),
-            column, column, pl.BlockSpec((1, F, D), lambda i, e: (e, 0, 0)),
+            pl.BlockSpec((owners, few, D), lambda i, e: (i, 0, 0)),
+            pl.BlockSpec((owners, T - few, D), lambda i, e: (i, 0, 0)),
+            units, units, hbm, hbm, pl.BlockSpec((1, D, F), lambda i, e: (e, 0, 0)),
         ],
-        out_specs=[rows, rows, units, units, units],
-        scratch_shapes=[pltpu.VMEM((block, D), f32), pltpu.VMEM((block, D), f32)],
+        out_specs=[rows, rows, units, units],
+        scratch_shapes=[
+            pltpu.VMEM((block, 2 * E * F), bf16),
+            pltpu.VMEM((2 * E * F, D), bf16),
+            pltpu.SemaphoreType.DMA((2,)),
+        ],
         compiler_params=pltpu.CompilerParams(vmem_limit_bytes=VMEM_LIMIT),
         cost_estimate=pl.CostEstimate(
-            flops=12 * L * D * E * F, bytes_accessed=40 * 2**20, transcendentals=L * E * F
+            flops=6 * L * D * E * F, bytes_accessed=40 * 2**20, transcendentals=0
         ),
-        name="experts_pass",
-    )(x, g, combine, gate_w, up_w, down_w)
+        name="backward_pass",
+    )(first, rest, gate_by, up_by, gate_t.reshape(E * F, D), up_t.reshape(E * F, D), down_t)
 
 
 def line_sum(n, steps, part, out, landed, up_send, up_recv, down_send, down_recv):
@@ -1196,36 +1342,35 @@
     return slots + [dma((n, steps))] * 4 + [dma((1,))]
 
 
-def expert_grads_kernel(x_ref, g_ref, hidden, gate_grad, up_grad, gate_out, up_out, down_out, xt):
+def expert_grads_kernel(x_ref, gate_grad, up_grad, gate_out, up_out, xt):
     @pl.when(pl.program_id(0) == 0)
     def _():
         xt[...] = x_ref[...].T
 
     gate_out[0] = dot(xt[...], gate_grad[...]).astype(bf16)
     up_out[0] = dot(xt[...], up_grad[...]).astype(bf16)
-    down_out[0] = dot_tn(hidden[...], g_ref[...]).astype(bf16)
-
-
-def expert_grads(x, g, hidden, gate_grad, up_grad, experts):
+
+
+def expert_grads(x, gate_grad, up_grad, experts):
     L, D = x.shape
-    F = hidden.shape[1] // experts
+    F = gate_grad.shape[1] // experts
     whole = pl.BlockSpec((L, D), lambda e: (0, 0))
     units = pl.BlockSpec((L, F), lambda e: (0, e))
     column = pl.BlockSpec((1, D, F), lambda e: (e, 0, 0))
     grad = jax.ShapeDtypeStruct((experts, D, F), bf16)
     return pl.pallas_call(
         expert_grads_kernel,
-        out_shape=[grad, grad, jax.ShapeDtypeStruct((experts, F, D), bf16)],
+        out_shape=[grad, grad],
         grid=(experts,),
-        in_specs=[whole, whole, units, units, units],
-        out_specs=[column, column, pl.BlockSpec((1, F, D), lambda e: (e, 0, 0))],
+        in_specs=[whole, units, units],
+        out_specs=[column, column],
         scratch_shapes=[pltpu.VMEM((D, L), bf16)],
         compiler_params=pltpu.CompilerParams(vmem_limit_bytes=VMEM_LIMIT),
         cost_estimate=pl.CostEstimate(
-            flops=6 * L * D * experts * F, bytes_accessed=26 * 2**20, transcendentals=0
+            flops=4 * L * D * experts * F, bytes_accessed=16 * 2**20, transcendentals=0
         ),
         name="expert_grads",
-    )(x, g, hidden, gate_grad, up_grad)
+    )(x, gate_grad, up_grad)
 
 
 def widen_kernel(count, *refs):
@@ -1345,7 +1490,7 @@
         compiler_params=pltpu.CompilerParams(
             collective_id=collective_id, has_side_effects=True, vmem_limit_bytes=VMEM_LIMIT
         ),
-        cost_estimate=pl.CostEstimate(flops=20 * 10**9, bytes_accessed=2 * 2**20, transcendentals=0),
+        cost_estimate=pl.CostEstimate(flops=70 * 10**9, bytes_accessed=8 * 2**20, transcendentals=0),
         name="gather_line",
     )(v)
 
@@ -1388,50 +1533,51 @@
         ],
         axis=1,
     )
-    x_all_b, normed, query_raw, key_raw, values, small_all, squares = gather_project(
-        shards, tokens, small, query_weight, key_weight, value_weight
-    )
+    slab = width // groups
+    out_slab = lax.dynamic_slice_in_dim(output_weight, group * slab, slab, 0)
+    x_all_b, normed, query_raw, key_raw, values, out_slab, small_all, factors = gather_project(
+        shards, tokens, small, out_slab, query_weight, key_weight, value_weight
+    )
+    full_output = lax.all_gather(out_slab, "dp", axis=0, tiled=True)
     x_all_b = x_all_b.reshape(length, width)
     normed = normed.reshape(length, width)
     query_raw = query_raw.reshape(length, local)
     key_raw = key_raw.reshape(length, local)
     values = values.reshape(length, local)
-    combine = small_all[:, :experts, :rows].transpose(0, 2, 1).reshape(length, experts)
     gain_in = small_all[:, 0, rows:].reshape(width)
-    gain_expert = small_all[:, 1, rows:].reshape(width)
     head_gains = own_gains[1:3]
-    slab = width // groups
-    out_grad_b, squares = lax.optimization_barrier((out_grad, squares))
-    out_slab = lax.dynamic_slice_in_dim(output_weight, group * slab, slab, 0)
-    out_slab = gather_line(shards, out_slab, 4).transpose(1, 0, 2).reshape(slab, width)
-    full_output = lax.all_gather(out_slab, "dp", axis=0, tiled=True)
-
-    factors = lax.rsqrt(squares[:, :2].transpose(0, 2, 1).reshape(length, 2) / width + EPSILON)
     cosine, sine = rotary_tables(length)
-    queries, keys, mixed_own = attention(
-        prefix, query_raw, key_raw, values, factors, cosine, sine, head_gains
-    )
-    mixed_all, expert_in, attended_own = gather_mix(
-        shards, mixed_own, full_output, x_all_b, gain_expert[None, :], rows
-    )
-
-    g_all = lax.all_gather(out_grad_b, "shard", axis=0, tiled=True)
-    sum_part, in_part, hidden, gate_grad, up_grad = experts_pass(
-        expert_in, g_all, combine, expert_gate, expert_up, expert_down
+    limit = jnp.broadcast_to(prefix.reshape(1, 1), (8, 128))
+    few = rows // 4
+    queries, keys, mixed_own, grad_first = attention(
+        shards, limit, query_raw, key_raw, values, factors, cosine, sine, head_gains,
+        out_grad[:few],
+    )
+    mixed_all = gather_line(shards, mixed_own, 1)
+    grad_rest, mixed_all, combine, gain_expert = lax.optimization_barrier(
+        (out_grad[few:], mixed_all, small_all[:, :experts, :rows], small_all[:, 1, rows:])
+    )
+    combine = combine.transpose(0, 2, 1).reshape(length, experts)
+    gain_expert = gain_expert.reshape(width)
+    grad_rest = lax.all_gather(grad_rest, "shard", axis=0)
+    attended, expert_in, gate_by, up_by, hidden, sum_part, gate_t, up_t, down_t = forward_pass(
+        mixed_all, full_output, x_all_b, gain_expert[None, :], combine, expert_gate, expert_up,
+        expert_down,
+    )
+    attended_own = lax.dynamic_slice_in_dim(attended, place * rows, rows, 0)
+    g_all, in_part, gate_grad, up_grad = backward_pass(
+        grad_first, grad_rest, gate_by, up_by, gate_t, up_t, down_t
     )
     sum_parts = sum_part.reshape(shards, 16, rows // 16, width)
-    grad_gate, grad_up, grad_down = expert_grads(
-        expert_in, g_all, hidden, gate_grad, up_grad, experts
-    )
-    in_part, grad_gate, grad_up, grad_down = lax.optimization_barrier(
-        (in_part, grad_gate, grad_up, grad_down)
-    )
-    grad_gate, grad_up, grad_down = lax.psum((grad_gate, grad_up, grad_down), "dp")
+    grad_gate, grad_up = expert_grads(expert_in, gate_grad, up_grad, experts)
+    in_part, grad_gate, grad_up = lax.optimization_barrier((in_part, grad_gate, grad_up))
+    grad_gate, grad_up = lax.psum((grad_gate, grad_up), "dp")
 
     x_own = tokens.astype(f32)
     residual_own = x_own + attended_own
-    residual_grad, attended_grad, gain_grad_res = scatter_norm(
-        shards, groups, 16, in_part, residual_own, out_grad, gain_expert[None, :]
+    residual_grad, attended_grad, gain_grad_res, grad_down = scatter_norm(
+        shards, groups, 16, in_part, tokens, gain_expert[None, :],
+        more=(out_grad, attended, hidden, g_all, experts),
     )
     residual_grad = residual_grad.reshape(rows, width)
     attended_grad = attended_grad.reshape(length, width)
@@ -1440,37 +1586,38 @@
     grad_output = lax.dot_general(
         mixed_all, own_columns, (((1,), (0,)), ((), ())), preferred_element_type=f32
     ).reshape(width, local)
-    mixed_grad = dot_nt(
-        attended_grad, lax.dynamic_slice_in_dim(full_output, place * local, local, 0)
-    ).astype(bf16)
-    limit = jnp.broadcast_to(prefix.reshape(1, 1), (8, 128))
+    grad_output, grad_down, grad_gate, grad_up, attended_grad = lax.optimization_barrier(
+        (grad_output.astype(bf16), grad_down, grad_gate, grad_up, attended_grad)
+    )
+    grad_output, grad_down = lax.psum((grad_output, grad_down), "dp")
     grad_query, grad_key, grad_value, normed_part, gain_grad_heads, expert_sum = attention_back(
-        shards, width, limit, queries, keys, values, mixed_grad, query_raw, key_raw, factors,
-        cosine, sine, head_gains, query_weight, key_weight, value_weight, normed, sum_parts,
+        shards, width, limit, queries, keys, values, query_raw, key_raw, factors, cosine, sine,
+        head_gains, query_weight, key_weight, value_weight, normed, sum_parts, attended_grad,
+        full_output,
     )
     expert_sum = expert_sum.reshape(rows, width)
-    attention_grads, normed_part, grad_gate, grad_up, grad_down = lax.optimization_barrier(
+    expert_sum, grad_gate, grad_up = lax.optimization_barrier((expert_sum, grad_gate, grad_up))
+    grad_gate, grad_up = widen(grad_gate, grad_up)
+    (
+        grad_query, grad_key, grad_value, normed_part, grad_output, grad_down, grad_gate, grad_up,
+    ) = lax.optimization_barrier(
         (
-            (grad_query, grad_key, grad_value, grad_output.astype(bf16)),
-            normed_part,
-            grad_gate,
+            grad_query, grad_key, grad_value, normed_part, grad_output, grad_down, grad_gate,
             grad_up,
-            grad_down,
-        )
-    )
-    grad_query, grad_key, grad_value, grad_output = lax.psum(attention_grads, "dp")
-    grad_tokens, grad_gains = scatter_norm(
-        shards, groups, 8, normed_part, tokens, residual_grad, gain_in[None, :],
-        (gain_grad_res, gain_grad_heads),
-    )
-    grad_tokens = grad_tokens.reshape(rows, width)
+        )
+    )
+    grad_query, grad_key, grad_value = lax.psum((grad_query, grad_key, grad_value), "dp")
+    through_norm, grad_gains = scatter_norm(
+        shards, groups, 16, normed_part, tokens, gain_in[None, :],
+        other_gains=(gain_grad_res, gain_grad_heads),
+    )
+    through_norm, expert_sum = lax.optimization_barrier((through_norm, expert_sum))
+    grad_tokens = residual_grad + through_norm.reshape(rows, width)
     grad_gains = grad_gains[:4]
     output = residual_own + expert_sum
     root_means = jnp.stack([root_mean(attended_own), root_mean(expert_sum), root_mean(output)])
-    grad_gate, grad_up, grad_down = widen(grad_gate, grad_up, grad_down)
-    grad_query, grad_key, grad_value, grad_output = widen(
-        grad_query, grad_key, grad_value, grad_output
-    )
+    grad_down, grad_output = widen(grad_down, grad_output)
+    grad_query, grad_key, grad_value = widen(grad_query, grad_key, grad_value)
 
     return (
         output.astype(bf16),

time: 709 us -> 678 us (0.956)
  Pallas kernels: 633 us -> 616 us
    pallas_call x4, Pallas kernels: 200 us -> 112 us  [the longest x1 49.5 us: forward_pass(): pl.pallas_call(forward_kernel, out_shape=[jax.ShapeDtypeStruct((L, D), f3...]
    pallas_call x1, Pallas kernels: 20.8 us -> 68.8 us  [gather_line(): pl.pallas_call(functools.partial(gather_line_kernel, n), out_shape=jax.Sh...]
    pallas_call x1, Pallas kernels: 81.6 us -> 99.9 us  [gather_project(): pl.pallas_call(functools.partial(gather_project_kernel, n), out_shape=[ja...]
    all_gather x1, waiting for transfers between devices: 0.02 us -> 12.9 us  [per_device(): grad_rest = lax.all_gather(grad_rest, 'shard', axis=0)]
    psum x2 -> x3, waiting for transfers between devices: 16.5 us -> 3.8 us  [the longest x1 3.79 us: per_device(): grad_output, grad_down = lax.psum((grad_output, grad_down), 'dp')]
    pallas_call x2 -> x3, Pallas kernels: 24.3 us -> 27.4 us  [widen(): pl.pallas_call(functools.partial(widen_kernel, len(flat)), out_shape=[jax...]
  transfers between devices with their start and end apart: 4 -> 5, of which waited for: 1 -> 2; matrix products, arithmetic and copies ran while one was open for 4% -> 3% of each run, Pallas kernels for 77% -> 69%
where the time goes in v6:
time: 678 us; the launch traced here: 673 us
  Pallas kernels  616 us (91%)
  waiting for transfers between devices  16.8 us (2%)
  between operations  14.6 us (2%)
  local copies, waits for them, and re-layouts  10.5 us (2%)
  other arithmetic  8.76 us (1%)
    pallas_call x2, Pallas kernels, scatter_norm(): pl.pallas_call(functools.partial(scatter_norm_kernel, n, groups, steps, g...  214 us
    pallas_call x1, Pallas kernels, gather_project(): pl.pallas_call(functools.partial(gather_project_kernel, n), out_shape=[ja...  99.9 us
    pallas_call x1, Pallas kernels, attention_back(): pl.pallas_call(functools.partial(attention_back_kernel, n, steps, width),...  94.2 us
    pallas_call x1, Pallas kernels, gather_line(): pl.pallas_call(functools.partial(gather_line_kernel, n), out_shape=jax.Sh...  68.8 us
    pallas_call x1, Pallas kernels, forward_pass(): pl.pallas_call(forward_kernel, out_shape=[jax.ShapeDtypeStruct((L, D), f3...  49.5 us
    pallas_call x3, Pallas kernels, widen(): pl.pallas_call(functools.partial(widen_kernel, len(flat)), out_shape=[jax...  27.4 us
    pallas_call x1, Pallas kernels, backward_pass(): pl.pallas_call(backward_kernel, out_shape=[wide, wide, narrow, narrow], g...  25.8 us
    pallas_call x1, Pallas kernels, attention(): pl.pallas_call(functools.partial(attention_kernel, n), out_shape=[out] *...  21.8 us
  transfers between devices with their start and end apart: 5, of which 2 were waited for; matrix products, arithmetic and copies ran while one was open for 3% of the time, Pallas kernels for 69%

profile of v6, /device:TPU:12, one launch (start us, length us, event | category | flops | bytes accessed | tf_op | source)
XLA Modules:
  0.0 673.5 jit_solution(5705037536420883465)
XLA Ops:
  7.2 0.8 fusion.5
  8.1 0.7 copy-done
  8.8 0.7 constant_dynamic-slice_fusion.slab_hbm
  9.5 0.7 select_reduce_fusion
  10.3 0.6 select_maximum_fusion.small_ref
  10.9 99.9 %gather_project.1 = (bf16[4,256,2048]{2,1,0:T(8,128)(2,1)}, bf16[4,256,2048]{2,1,0:T(8,128)(2,1)}, f32[4,256,512]{2,1,0:T(8,128)}, f32[4,256,512]{2,1,0:T(8,128)...) custom-call(bf16[256,2048]{1,0:T(8,128)(2,1)} %x_hbm.1, ...), custom_call_target="tpu_custom_call" | custom-call | flops 80000000000 | bytes 33554432 | tf_op jit(solution)/shard_map/gather_project/pallas_call | solution.py:330
  110.9 0.6 slice.38.gains
  111.5 0.7 slice.31.first_hbm
  112.2 1.0 slice.27
  113.8 0.8 slice.32
  114.6 1.5 fusion.4
  116.1 0.6 broadcast_in_dim.23.limit_ref
  116.7 21.8 %attention.1 = (bf16[1024,512]{1,0:T(8,128)(2,1)}, bf16[1024,512]{1,0:T(8,128)(2,1)}, bf16[1024,512]{1,0:T(8,128)(2,1)}, bf16[4,64,2048]{2,1,0:T(8,128)(2,1)}) custom-call(s32[8,128]{1,0:T(8,128)} %broadcast_in_dim.23.limit_ref, f32[1024,512]{1,0:T(8,128)} %bitcast.56, f32[1024,512]{1,0:T(8,128)} %bitcast.58, bf16[1024,512]{1,0:T(8,128)(2,1)} %bitcast.63, ...), custom_call_target="tpu_custom_call" | custom-call | flops 20000000000 | bytes 16777216 | tf_op jit(solution)/shard_map/attention/pallas_call | solution.py:461
  138.5 68.8 %gather_line.1.mixed = bf16[4,1024,512]{2,1,0:T(8,128)(2,1)} custom-call(bf16[1024,512]{1,0:T(8,128)(2,1)} %get-tuple-element.86.v_hbm), custom_call_target="tpu_custom_call" | custom-call | flops 70000001024 | bytes 8388608 | tf_op jit(solution)/shard_map/gather_line/pallas_call | solution.py:1481
  207.6 0.6 copy.34
  208.2 1.0 copy.30
  209.2 49.5 %forward_pass.1 = (f32[1024,2048]{1,0:T(8,128)}, bf16[1024,2048]{1,0:T(8,128)(2,1)}, f32[1024,1024]{1,0:T(8,128)}, f32[1024,1024]{1,0:T(8,128)}, bf16[1024,1024]...) custom-call(bf16[4,1024,512]{2,1,0:T(8,128)(2,1)} %gather_line.1.mix, ...), custom_call_target="tpu_custom_call" | custom-call | flops 21474836480 | bytes 52428800 | tf_op jit(solution)/shard_map/forward_pass/pallas_call | solution.py:1130
  258.7 12.9 %all-gather.6.cloned.1.call-done = bf16[768,2048]{1,0:T(8,128)(2,1)} async-done(((bf16[192,2048]{1,0:T(8,128)(2,1)}), bf16[768,2048]{1,0:T(8,128)(2,1)}) %all-gather.6.cloned.1.call-update) | async-done | bytes 3145744 | tf_op jit(solution)/shard_map/all_gather | solution.py:1562
  271.7 25.8 %backward_pass.1 = (bf16[1024,2048]{1,0:T(8,128)(2,1)}, bf16[1024,2048]{1,0:T(8,128)(2,1)}, bf16[1024,1024]{1,0:T(8,128)(2,1)}, bf16[1024,1024]{1,0:T(8,128)(2,1)}) custom-call(bf16[4,64,2048]{2,1,0:T(8,128)(2,1)} %get-tuple-element.98.first, bf16[4,192,2048]{2,1,0:T(8,128)(2,1)} %bitcast.78, f32[1024,1024]{1,0:T(8,128)} %get-tuple-element.100.gate_ref, ...), custom_call_target="tpu_custom_call" | custom-call | flops 12884901888 | bytes 41943040 | tf_op jit(solution)/shard_map/backward_pass/pallas_call | solution.py:1219
  297.5 15.0 %expert_grads.1 = (bf16[4,2048,256]{2,1,0:T(8,128)(2,1)}, bf16[4,2048,256]{2,1,0:T(8,128)(2,1)}) custom-call(bf16[1024,2048]{1,0:T(8,128)(2,1)} %get-tuple-element.106.x_ref, bf16[1024,1024]{1,0:T(8,128)(2,1)} %get-tuple-element.107.gate_grad, bf16[1024,1024]{1,0:T(8,128)(2,1)} %get-tuple-element.108.up_grad), custom_call_target="tpu_custom_call" | custom-call | flops 8589934592 | bytes 16777216 | tf_op jit(solution)/shard_map/expert_grads/pallas_call | solution.py:1361
  312.6 122.0 %scatter_norm_gather.1 = (f32[16,16,2048]{2,1,0:T(8,128)}, bf16[4,16,16,2048]{3,2,1,0:T(8,128)(2,1)}, f32[8,2048]{1,0:T(8,128)}, bf16[4,256,2048]{2,1,0:T(8,128)(2,1)}) custom-call(bf16[4,16,16,2048]{3,2,1,0:T(8,128)(2,1)} %bitcast.50, bf16[16,16,2048]{2,1,0:T(8,128)(2,1)} %bitcast.44, f32[1,2048]{1,0:T(1,128)} %bitcast.68, bf16[16,16,2048]{2,1,0:T(8,128)(2,1)} %bitcast.51, ...), custom_call_target="tpu_custom_call" | custom-call | flops 1000000000 | bytes 1048576 | tf_op jit(solution)/shard_map/scatter_norm_gather/pallas_call | solution.py:1040
  434.6 6.3 convolution_convert_fusion
  440.9 94.2 %attention_back.1 = (bf16[2048,512]{1,0:T(8,128)(2,1)}, bf16[2048,512]{1,0:T(8,128)(2,1)}, bf16[2048,512]{1,0:T(8,128)(2,1)}, bf16[1024,2048]{1,0:T(8,128)(2,1)}...) custom-call(s32[8,128]{1,0:T(8,128)} %broadcast_in_dim.23.limit_ref, bf16[1024,512]{1,0:T(8,128)(2,1)} %get-tuple-element.94.q_ref, ...), custom_call_target="tpu_custom_call" | custom-call | flops 2000000000 | bytes 1048576 | tf_op jit(solution)/shard_map/attention_back/pallas_call | solution.py:694
  535.1 10.2 %widen.3 = (f32[8192,256]{1,0:T(8,128)}, f32[8192,256]{1,0:T(8,128)}) custom-call(bf16[8192,256]{1,0:T(8,128)(2,1)} %bitcast.53, bf16[8192,256]{1,0:T(8,128)(2,1)} %bitcast.54), custom_call_target="tpu_custom_call" | custom-call | bytes 25165824 | tf_op jit(solution)/shard_map/widen/pallas_call | solution.py:1387
  545.3 3.8 all-reduce.11.cloned.1.call-done
  549.1 91.7 %scatter_norm.1 = (f32[16,16,2048]{2,1,0:T(8,128)}, f32[8,512]{1,0:T(8,128)}) custom-call(bf16[4,16,16,2048]{3,2,1,0:T(8,128)(2,1)} %bitcast.55, bf16[16,16,2048]{2,1,0:T(8,128)(2,1)} %bitcast.45, f32[1,2048]{1,0:T(1,128)} %bitcast.69, f32[8,2048]{1,0:T(8,128)} %get-tuple-element.133.refs_3_, f32[2,512]{1,0:T(2,128)} %get-tuple-element.134.refs_4_), custom_call_target="tpu_custom_call" | custom-call | flops 1000000000 | bytes 1048576 | tf_op jit(solution)/shard_map/scatter_norm/pallas_call | solution.py:1040
  640.8 1.5 slice.35
  642.3 8.7 %widen.5 = (f32[1024,2048]{1,0:T(8,128)}, f32[2048,512]{1,0:T(8,128)}) custom-call(bf16[1024,2048]{1,0:T(8,128)(2,1)} %bitcast.52, bf16[2048,512]{1,0:T(8,128)(2,1)} %get-tuple-element.147.refs_1_), custom_call_target="tpu_custom_call" | custom-call | bytes 18874368 | tf_op jit(solution)/shard_map/widen/pallas_call | solution.py:1387
  651.0 3.4 add.44
  654.4 3.4 multiply_reduce_fusion.2
  657.8 0.6 pad_maximum_fusion
  658.4 8.5 %widen.4 = (f32[2048,512]{1,0:T(8,128)}, f32[2048,512]{1,0:T(8,128)}, f32[2048,512]{1,0:T(8,128)}) custom-call(bf16[2048,512]{1,0:T(8,128)(2,1)} %get-tuple-element.156.refs_0_, bf16[2048,512]{1,0:T(8,128)(2,1)} %get-tuple-element.157.refs_1_, bf16[2048,512]{1,0:T(8,128)(2,1)} %get-tuple-element.158.refs_2_), custom_call_target="tpu_custom_call" | custom-call | bytes 18874368 | tf_op jit(solution)/shard_map/widen/pallas_call | solution.py:1387
  (30 shorter events, 0.5 us)
Async XLA Ops:
  7.2 1.6 copy-start
  7.2 202.0 %all-gather.4.cloned.1.call-start = ((), (), s32[]{:S(2)}) async-start(), calls=%async_computation | async-start | bytes 9437184 | tf_op jit(solution)/shard_map/all_gather | solution.py:1541
  10.9 100.0 %copy-start.6 = (bf16[4,512]{1,0:T(4,128)(2,1)S(1)}, bf16[4,512]{1,0:T(4,128)(2,1)}, u32[]{:S(2)}) copy-start(bf16[4,512]{1,0:T(4,128)(2,1)} %param.24) | copy-start | bytes 12292
  10.9 100.6 %copy-start.3 = (bf16[256,2048]{1,0:T(8,128)(2,1)S(1)}, bf16[256,2048]{1,0:T(8,128)(2,1)}, u32[]{:S(2)}) copy-start(bf16[256,2048]{1,0:T(8,128)(2,1)} %param.16) | copy-start | bytes 3145732
  110.8 160.8 %all-gather.6.cloned.1.call-start = ((), (), s32[]{:S(2)}) async-start(), calls=%async_computation.1 | async-start | bytes 3932160 | tf_op jit(solution)/shard_map/all_gather | solution.py:1562
  207.4 233.5 %all-reduce.13.cloned.1.call-start = ((), (), s32[]{:S(2)}) async-start(), calls=%async_computation.4 | async-start | bytes 16777216 | tf_op jit(solution)/shard_map/psum | solution.py:1574
  312.5 236.6 %all-reduce.11.cloned.1.call-start = ((), (), s32[]{:S(2)}) async-start(), calls=%async_computation.3 | async-start | bytes 12582912 | tf_op jit(solution)/shard_map/psum | solution.py:1592
  440.9 217.5 %all-reduce.9.cloned.1.call-start = ((), (), s32[]{:S(2)}) async-start(), calls=%async_computation.2 | async-start | bytes 12582912 | tf_op jit(solution)/shard_map/psum | solution.py:1609
  640.8 10.1 %copy-start.4 = (f32[16,16,2048]{2,1,0:T(8,128)S(1)}, f32[16,16,2048]{2,1,0:T(8,128)}, u32[]{:S(2)}) copy-start(f32[16,16,2048]{2,1,0:T(8,128)} %get-tuple-element.138) | copy-start | bytes 6291460
  651.0 3.4 copy-start.2
  651.0 3.4 copy-start.5
  654.4 12.6 %copy-start.1 = (bf16[2048,512]{1,0:T(8,128)(2,1)S(1)}, bf16[2048,512]{1,0:T(8,128)(2,1)}, u32[]{:S(2)}) copy-start(bf16[2048,512]{1,0:T(8,128)(2,1)} %param.23) | copy-start | bytes 6291460
Sparse Core Ops, SparseCore 0:
  110.9 55.2 all-gather.3
  207.5 64.1 all-gather.5
  312.6 127.6 all-reduce.12
  444.5 104.5 all-reduce.10
  552.5 105.5 all-reduce.8

commit v7 on v6

--- a/solution.py
+++ b/solution.py
@@ -137,7 +137,7 @@
 
 def gather_project_kernel(
     n, x_hbm, small_ref, slab_hbm, wq_hbm, wk_hbm, wv_hbm,
-    x_out, normed_out, q_out, k_out, v_out, slab_out, small_out, sq_out,
+    x_out, normed_out, q_out, k_out, v_out, slab_out, combine_out, gains_out, sq_out,
     slabs, xs, nb, qb, kb, vb, wq, wk, wv, sq_all, small_all,
     load_sem, out_sem, up_sem, down_sem, recv_sem, small_send, small_recv, sq_send, sq_recv,
     slab_up, slab_down, slab_recv, slab_sem,
@@ -145,7 +145,9 @@
     T, D = xs.shape[1:]
     C = qb.shape[2]
     d, z, peers = others(n)
-    slab_load = pltpu.make_async_copy(slab_hbm, slabs.at[z], load_sem.at[4])
+    S = slabs.shape[1]
+    slab_rows = pl.ds(pl.multiple_of(d * S, S), S)
+    slab_load = pltpu.make_async_copy(slab_hbm.at[slab_rows, :], slabs.at[z], load_sem.at[4])
     slab_load.start()
     own_load = pltpu.make_async_copy(x_hbm, xs.at[z], load_sem.at[0])
     own_load.start()
@@ -282,7 +284,16 @@
         )
         copy.start()
         sq_copies.append(copy)
-    small_out[...] = small_all[...]
+
+    def spread(o, carry):
+        r = pl.ds(pl.multiple_of(o * T, T), T)
+        tall = jnp.concatenate([small_all[o, :, 0:T], jnp.zeros((120, T), f32)], axis=0)
+        combine_out[r, :] = tall.T
+        return carry
+
+    lax.fori_loop(0, n, spread, 0)
+    for s in range(n):
+        gains_out[:, s * C : (s + 1) * C] = small_all[s, :, T:]
 
     def finish(o, carry):
         for copy in outs(o):
@@ -321,9 +332,10 @@
         copy.wait_send()
 
 
-def gather_project(n, tokens, small, slab, wq, wk, wv):
+def gather_project(n, groups, tokens, small, wo, wq, wk, wv):
     T, D = tokens.shape
     C = wq.shape[1]
+    S = D // groups
     hbm = pl.BlockSpec(memory_space=pl.ANY)
     vmem = pl.BlockSpec(memory_space=pltpu.VMEM)
     dma = pltpu.SemaphoreType.DMA
@@ -335,14 +347,15 @@
             jax.ShapeDtypeStruct((n, T, C), f32),
             jax.ShapeDtypeStruct((n, T, C), f32),
             jax.ShapeDtypeStruct((n, T, C), bf16),
-            jax.ShapeDtypeStruct((slab.shape[0], D), bf16),
-            jax.ShapeDtypeStruct((n,) + small.shape, f32),
+            jax.ShapeDtypeStruct((S, D), bf16),
+            jax.ShapeDtypeStruct((n * T, 128), f32),
+            jax.ShapeDtypeStruct((8, D), f32),
             jax.ShapeDtypeStruct((n * T, 128), f32),
         ],
         in_specs=[hbm, vmem, hbm, hbm, hbm, hbm],
-        out_specs=[hbm] * 6 + [vmem] * 2,
+        out_specs=[hbm] * 6 + [vmem] * 3,
         scratch_shapes=[
-            pltpu.VMEM((n,) + slab.shape, bf16),
+            pltpu.VMEM((n, S, C), bf16),
             pltpu.VMEM((n, T, D), bf16),
             pltpu.VMEM((n, T, D), bf16),
             pltpu.VMEM((n, T, C), f32),
@@ -372,7 +385,7 @@
         ),
         cost_estimate=pl.CostEstimate(flops=80 * 10**9, bytes_accessed=32 * 2**20, transcendentals=0),
         name="gather_project",
-    )(tokens, small, slab, wq, wk, wv)
+    )(tokens, small, wo, wq, wk, wv)
 
 
 def rope(v, cosine, sine):
@@ -391,7 +404,7 @@
 
 
 def attention_kernel(
-    n, limit_ref, q_raw, k_raw, v_ref, factors, cosine, sine, gains, first_hbm,
+    n, limit_ref, q_raw, k_raw, v_ref, factors, cosine, sine, gains, grad_hbm,
     q_out, k_out, mixed, first_out, slots, load_sem, up_sem, down_sem, recv_sem, out_sem,
 ):
     length = q_raw.shape[0]
@@ -404,9 +417,11 @@
     def save(o):
         return pltpu.make_async_copy(slots.at[o], first_out.at[o], out_sem.at[o])
 
+    few = slots.shape[1]
+
     @pl.when(h == 0)
     def _():
-        load = pltpu.make_async_copy(first_hbm, slots.at[z], load_sem.at[0])
+        load = pltpu.make_async_copy(grad_hbm.at[0:few], slots.at[z], load_sem.at[0])
         load.start()
         _, _, peers = others(n)
         greet(peers)
@@ -423,8 +438,8 @@
 
         lax.fori_loop(0, length // block, part, 0)
 
-    turn(q_raw, q_out, 0, gains[0:1, :])
-    turn(k_raw, k_out, 1, gains[1:2, :])
+    turn(q_raw, q_out, 0, gains[1:2, :])
+    turn(k_raw, k_out, 1, gains[2:3, :])
     for i in range(length // block):
         span = key_span(i, block, length)
         r = pl.ds(i * block, block)
@@ -450,7 +465,7 @@
         lax.fori_loop(0, n, finish, 0)
 
 
-def attention(n, limit, q_raw, k_raw, values, factors, cosine, sine, gains, first):
+def attention(n, limit, q_raw, k_raw, values, factors, cosine, sine, gains, grad, few):
     length, local = q_raw.shape
     heads = local // HEAD_DIM
     head = pl.BlockSpec((length, HEAD_DIM), lambda h: (0, h))
@@ -460,14 +475,15 @@
     dma = pltpu.SemaphoreType.DMA
     return pl.pallas_call(
         functools.partial(attention_kernel, n),
-        out_shape=[out] * 3 + [jax.ShapeDtypeStruct((n,) + first.shape, bf16)],
+        out_shape=[out] * 3
+        + [jax.ShapeDtypeStruct((n, few, grad.shape[1]), bf16)],
         grid=(heads,),
         in_specs=[
             whole(limit), head, head, head, whole(factors), whole(cosine), whole(sine),
-            pl.BlockSpec((2, HEAD_DIM), lambda h: (0, h)), hbm,
+            pl.BlockSpec((gains.shape[0], HEAD_DIM), lambda h: (0, h)), hbm,
         ],
         out_specs=[head] * 3 + [hbm],
-        scratch_shapes=[pltpu.VMEM((n,) + first.shape, bf16), dma((1,))] + [dma((n,))] * 4,
+        scratch_shapes=[pltpu.VMEM((n, few, grad.shape[1]), bf16), dma((1,))] + [dma((n,))] * 4,
         compiler_params=pltpu.CompilerParams(
             collective_id=7, has_side_effects=True, vmem_limit_bytes=VMEM_LIMIT
         ),
@@ -475,7 +491,7 @@
             flops=20 * 10**9, bytes_accessed=16 * 2**20, transcendentals=0
         ),
         name="attention",
-    )(limit, q_raw, k_raw, values, factors, cosine, sine, gains, first)
+    )(limit, q_raw, k_raw, values, factors, cosine, sine, gains, grad)
 
 
 def attention_back_kernel(
@@ -572,7 +588,7 @@
             k_acc[0:span, :] += dot_tn(ds, q) * scale
             v_acc[0:span, :] += dot_tn(p.astype(bf16), g)
         v_grad[:, c] = v_acc[...].astype(bf16)
-        gain_q, gain_k = gains[0:1, c], gains[1:2, c]
+        gain_q, gain_k = gains[1:2, c], gains[2:3, c]
 
         def back(i, carry):
             gq, gk = carry
@@ -739,9 +755,9 @@
     refs = refs[3:]
     if gather:
         addend, attended_hbm, hidden, g_all = refs[:4]
-        out, all_out, gain_out, down_out = refs[4:8]
-        alls, ag_up, ag_down, ag_recv, all_sem, attended, load_sem = refs[8:15]
-        refs = refs[15:]
+        out, all_out, columns_out, gain_out, down_out = refs[4:9]
+        alls, ag_up, ag_down, ag_recv, all_sem, attended, load_sem = refs[9:16]
+        refs = refs[16:]
     else:
         expert_gains, head_gains, out, gain_out = refs[:4]
         pieces, landed, sums, piece_send, piece_recv, sum_send, sum_recv = refs[4:11]
@@ -852,9 +868,10 @@
         unit = rows * factor
         along = total * unit
         gain_acc[...] += jnp.sum(along.reshape(R // 8, 8, D), axis=0)
-        weighted = along * gain[...]
+        weights = gain[1:2, :] if gather else gain[0:1, :]
+        weighted = along * weights
         mean = jnp.sum(weighted, axis=1, keepdims=True) / D
-        result = factor * (total * gain[...] - unit * mean)
+        result = factor * (total * weights - unit * mean)
         if gather:
             result = result + addend[k].astype(f32)
         out[k] = result
@@ -1003,7 +1020,15 @@
 
     lax.fori_loop(0, n * steps, drain, 0)
     if gather:
-        copies = [pltpu.make_async_copy(alls.at[o], all_out.at[o], all_sem.at[o]) for o in range(n)]
+        C = D // n
+        c = pl.ds(pl.multiple_of(z * C, C), C)
+        copies = []
+        for o in range(n):
+            own_columns = alls.at[o, :, :, c]
+            copies.append(
+                pltpu.make_async_copy(own_columns, columns_out.at[o], all_sem.at[n + o])
+            )
+            copies.append(pltpu.make_async_copy(alls.at[o], all_out.at[o], all_sem.at[o]))
         for copy in copies:
             copy.start()
         for copy in copies:
@@ -1027,8 +1052,9 @@
         more = (
             addend.reshape(steps, R, D), attended.reshape(n, steps, R, D), hidden, g_all,
         )
-        own = [slots, sems, sems, sems, dma((n,)), pltpu.VMEM((steps, R, D), f32), dma((1,))]
+        own = [slots, sems, sems, sems, dma((2 * n,)), pltpu.VMEM((steps, R, D), f32), dma((1,))]
         outs = [rows, jax.ShapeDtypeStruct((n, steps, R, D), bf16)]
+        outs += [jax.ShapeDtypeStruct((n, steps, R, C), bf16)]
         outs += [jax.ShapeDtypeStruct((8, D), f32)]
         outs += [jax.ShapeDtypeStruct((experts, units, D), bf16)]
     else:
@@ -1041,7 +1067,7 @@
         functools.partial(scatter_norm_kernel, n, groups, steps, gather),
         out_shape=outs,
         in_specs=[vmem] * 4 + [hbm, vmem, vmem] if gather else [vmem] * 5,
-        out_specs=[vmem, hbm, vmem, vmem] if gather else [vmem, vmem],
+        out_specs=[vmem, hbm, hbm, vmem, vmem] if gather else [vmem, vmem],
         scratch_shapes=own + [slots, slots, pltpu.VMEM((8, D), f32), sems, sems, sems, sems],
         compiler_params=pltpu.CompilerParams(
             collective_id=2 if gather else 3, has_side_effects=True, vmem_limit_bytes=VMEM_LIMIT
@@ -1060,30 +1086,28 @@
 
 def forward_kernel(
     mixed, weight, x_ref, gain, combine, gate_w, up_w, down_w,
-    attended_out, in_out, gate_out, up_out, hidden_out, sum_out, gate_t, up_t, down_t,
-    sum_acc,
+    attended_out, turned_out, gate_out, up_out, hidden_out, sum_out, gate_t, up_t, down_t,
+    in_out, units,
 ):
     e = pl.program_id(1)
     last = pl.num_programs(1) - 1
     D = in_out.shape[1]
-    C = mixed.shape[2]
+    F = hidden_out.shape[1]
 
     @pl.when(e == 0)
     def _():
-        total = dot(mixed[0], weight[0:C, :])
-        for s in range(1, mixed.shape[0]):
-            total = total + dot(mixed[s], weight[s * C : (s + 1) * C, :])
-        attended_out[...] = total
+        attended_out[...] = dot(mixed[...], weight[...])
         part = 32
 
         def rows(i, carry):
             r = pl.ds(pl.multiple_of(i * part, part), part)
             v = attended_out[r, :] + x_ref[r, :].astype(f32)
             factor = lax.rsqrt(jnp.sum(v * v, axis=1, keepdims=True) / D + EPSILON)
-            in_out[r, :] = (v * factor * gain[...]).astype(bf16)
+            in_out[r, :] = (v * factor * gain[1:2, :]).astype(bf16)
             return carry
 
         lax.fori_loop(0, in_out.shape[0] // part, rows, 0)
+        turned_out[...] = in_out[...].T
 
     lane = lax.broadcasted_iota(jnp.int32, combine.shape, 1)
     share = jnp.sum(jnp.where(lane == e, combine[...], 0.0), axis=1, keepdims=True)
@@ -1091,7 +1115,7 @@
     def _():
         gate_t[0] = gate_w[0].T
         up_t[0] = up_w[0].T
-        down_t[0] = down_w[0].T
+        down_t[0] = down_w[pl.ds(pl.multiple_of(e * F, F), F), :].T
 
     gate_part = dot(in_out[...], gate_w[0])
     up_part = dot(in_out[...], up_w[0])
@@ -1101,27 +1125,19 @@
     up_out[...] = silu
     hidden = (silu * up_part).astype(bf16)
     hidden_out[...] = hidden
-    made = dot(hidden, down_w[0])
-
-    @pl.when(e == 0)
-    def _():
-        sum_acc[...] = made
-
-    @pl.when(e > 0)
-    def _():
-        sum_acc[...] += made
+    units[:, pl.ds(pl.multiple_of(e * F, F), F)] = hidden
 
     @pl.when(e == last)
     def _():
-        sum_out[...] = sum_acc[...].astype(bf16)
+        sum_out[...] = dot(units[...], down_w[...]).astype(bf16)
 
 
 def forward_pass(mixed, weight, x, gain, combine, gate_w, up_w, down_w):
-    n, L, C = mixed.shape
-    D = x.shape[1]
+    L, D = x.shape
     E, _, F = gate_w.shape
     block = min(512, L)
     rows = pl.BlockSpec((block, D), lambda i, e: (i, 0))
+    held = pl.BlockSpec((block, D), lambda i, e: (i, 0), pipeline_mode=pl.Buffered(1))
     units = pl.BlockSpec((block, F), lambda i, e: (i, e))
     column = pl.BlockSpec((1, D, F), lambda i, e: (e, 0, 0))
     once = pl.Buffered(1)
@@ -1131,7 +1147,7 @@
         forward_kernel,
         out_shape=[
             jax.ShapeDtypeStruct((L, D), f32),
-            jax.ShapeDtypeStruct((L, D), bf16),
+            jax.ShapeDtypeStruct((D, L), bf16),
             jax.ShapeDtypeStruct((L, E * F), f32),
             jax.ShapeDtypeStruct((L, E * F), f32),
             jax.ShapeDtypeStruct((L, E * F), bf16),
@@ -1142,22 +1158,26 @@
         ],
         grid=(L // block, E),
         in_specs=[
-            pl.BlockSpec((n, block, C), lambda i, e: (0, i, 0)),
+            held,
             pl.BlockSpec((D, D), lambda i, e: (0, 0), pipeline_mode=once),
-            rows,
-            pl.BlockSpec((1, D), lambda i, e: (0, 0)),
+            held,
+            pl.BlockSpec((8, D), lambda i, e: (0, 0)),
             pl.BlockSpec((block, combine.shape[1]), lambda i, e: (i, 0)),
-            column, column, pl.BlockSpec((1, F, D), lambda i, e: (e, 0, 0)),
+            column, column,
+            pl.BlockSpec((E * F, D), lambda i, e: (0, 0), pipeline_mode=once),
         ],
-        out_specs=[rows, rows, units, units, units, rows, turned, turned, turned_down],
-        scratch_shapes=[pltpu.VMEM((block, D), f32)],
+        out_specs=[
+            rows, pl.BlockSpec((D, block), lambda i, e: (0, i)), units, units, units, rows, turned,
+            turned, turned_down,
+        ],
+        scratch_shapes=[pltpu.VMEM((block, D), bf16), pltpu.VMEM((block, E * F), bf16)],
         compiler_params=pltpu.CompilerParams(vmem_limit_bytes=VMEM_LIMIT),
         cost_estimate=pl.CostEstimate(
             flops=6 * L * D * E * F + 2 * L * D * D, bytes_accessed=50 * 2**20,
             transcendentals=L * E * F,
         ),
         name="forward_pass",
-    )(mixed, weight, x, gain, combine, gate_w, up_w, down_w)
+    )(mixed, weight, x, gain, combine, gate_w, up_w, down_w.reshape(E * F, D))
 
 
 def backward_kernel(
@@ -1342,19 +1362,15 @@
     return slots + [dma((n, steps))] * 4 + [dma((1,))]
 
 
-def expert_grads_kernel(x_ref, gate_grad, up_grad, gate_out, up_out, xt):
-    @pl.when(pl.program_id(0) == 0)
-    def _():
-        xt[...] = x_ref[...].T
-
+def expert_grads_kernel(xt, gate_grad, up_grad, gate_out, up_out):
     gate_out[0] = dot(xt[...], gate_grad[...]).astype(bf16)
     up_out[0] = dot(xt[...], up_grad[...]).astype(bf16)
 
 
-def expert_grads(x, gate_grad, up_grad, experts):
-    L, D = x.shape
+def expert_grads(turned, gate_grad, up_grad, experts):
+    D, L = turned.shape
     F = gate_grad.shape[1] // experts
-    whole = pl.BlockSpec((L, D), lambda e: (0, 0))
+    whole = pl.BlockSpec((D, L), lambda e: (0, 0))
     units = pl.BlockSpec((L, F), lambda e: (0, e))
     column = pl.BlockSpec((1, D, F), lambda e: (e, 0, 0))
     grad = jax.ShapeDtypeStruct((experts, D, F), bf16)
@@ -1364,13 +1380,12 @@
         grid=(experts,),
         in_specs=[whole, units, units],
         out_specs=[column, column],
-        scratch_shapes=[pltpu.VMEM((D, L), bf16)],
         compiler_params=pltpu.CompilerParams(vmem_limit_bytes=VMEM_LIMIT),
         cost_estimate=pl.CostEstimate(
             flops=4 * L * D * experts * F, bytes_accessed=16 * 2**20, transcendentals=0
         ),
         name="expert_grads",
-    )(x, gate_grad, up_grad)
+    )(turned, gate_grad, up_grad)
 
 
 def widen_kernel(count, *refs):
@@ -1427,8 +1442,11 @@
     def _():
         send_down(z).start()
 
+    C = slots.shape[2]
+
     def save(o):
-        return pltpu.make_async_copy(slots.at[o], out.at[o], out_sem.at[o])
+        c = pl.ds(pl.multiple_of(o * C, C), C)
+        return pltpu.make_async_copy(slots.at[o], out.at[:, c], out_sem.at[o])
 
     save(z).start()
 
@@ -1480,7 +1498,7 @@
     dma = pltpu.SemaphoreType.DMA
     return pl.pallas_call(
         functools.partial(gather_line_kernel, n),
-        out_shape=jax.ShapeDtypeStruct((n,) + v.shape, v.dtype),
+        out_shape=jax.ShapeDtypeStruct((v.shape[0], n * v.shape[1]), v.dtype),
         in_specs=[hbm],
         out_specs=hbm,
         scratch_shapes=[
@@ -1533,10 +1551,10 @@
         ],
         axis=1,
     )
-    slab = width // groups
-    out_slab = lax.dynamic_slice_in_dim(output_weight, group * slab, slab, 0)
-    x_all_b, normed, query_raw, key_raw, values, out_slab, small_all, factors = gather_project(
-        shards, tokens, small, out_slab, query_weight, key_weight, value_weight
+    x_all_b, normed, query_raw, key_raw, values, out_slab, combine, gains, factors = (
+        gather_project(
+            shards, groups, tokens, small, output_weight, query_weight, key_weight, value_weight
+        )
     )
     full_output = lax.all_gather(out_slab, "dp", axis=0, tiled=True)
     x_all_b = x_all_b.reshape(length, width)
@@ -1544,55 +1562,44 @@
     query_raw = query_raw.reshape(length, local)
     key_raw = key_raw.reshape(length, local)
     values = values.reshape(length, local)
-    gain_in = small_all[:, 0, rows:].reshape(width)
-    head_gains = own_gains[1:3]
     cosine, sine = rotary_tables(length)
     limit = jnp.broadcast_to(prefix.reshape(1, 1), (8, 128))
     few = rows // 4
     queries, keys, mixed_own, grad_first = attention(
-        shards, limit, query_raw, key_raw, values, factors, cosine, sine, head_gains,
-        out_grad[:few],
+        shards, limit, query_raw, key_raw, values, factors, cosine, sine, own_gains, out_grad, few
     )
     mixed_all = gather_line(shards, mixed_own, 1)
-    grad_rest, mixed_all, combine, gain_expert = lax.optimization_barrier(
-        (out_grad[few:], mixed_all, small_all[:, :experts, :rows], small_all[:, 1, rows:])
-    )
-    combine = combine.transpose(0, 2, 1).reshape(length, experts)
-    gain_expert = gain_expert.reshape(width)
+    grad_rest, mixed_all = lax.optimization_barrier((out_grad[few:], mixed_all))
     grad_rest = lax.all_gather(grad_rest, "shard", axis=0)
-    attended, expert_in, gate_by, up_by, hidden, sum_part, gate_t, up_t, down_t = forward_pass(
-        mixed_all, full_output, x_all_b, gain_expert[None, :], combine, expert_gate, expert_up,
-        expert_down,
+    attended, expert_turned, gate_by, up_by, hidden, sum_part, gate_t, up_t, down_t = forward_pass(
+        mixed_all, full_output, x_all_b, gains, combine, expert_gate, expert_up, expert_down
     )
     attended_own = lax.dynamic_slice_in_dim(attended, place * rows, rows, 0)
     g_all, in_part, gate_grad, up_grad = backward_pass(
         grad_first, grad_rest, gate_by, up_by, gate_t, up_t, down_t
     )
     sum_parts = sum_part.reshape(shards, 16, rows // 16, width)
-    grad_gate, grad_up = expert_grads(expert_in, gate_grad, up_grad, experts)
+    grad_gate, grad_up = expert_grads(expert_turned, gate_grad, up_grad, experts)
     in_part, grad_gate, grad_up = lax.optimization_barrier((in_part, grad_gate, grad_up))
     grad_gate, grad_up = lax.psum((grad_gate, grad_up), "dp")
 
     x_own = tokens.astype(f32)
     residual_own = x_own + attended_own
-    residual_grad, attended_grad, gain_grad_res, grad_down = scatter_norm(
-        shards, groups, 16, in_part, tokens, gain_expert[None, :],
+    residual_grad, attended_grad, own_columns, gain_grad_res, grad_down = scatter_norm(
+        shards, groups, 16, in_part, tokens, gains,
         more=(out_grad, attended, hidden, g_all, experts),
     )
     residual_grad = residual_grad.reshape(rows, width)
     attended_grad = attended_grad.reshape(length, width)
 
-    own_columns = lax.dynamic_slice_in_dim(attended_grad, place * local, local, 1)
-    grad_output = lax.dot_general(
-        mixed_all, own_columns, (((1,), (0,)), ((), ())), preferred_element_type=f32
-    ).reshape(width, local)
+    grad_output = dot_tn(mixed_all, own_columns.reshape(length, local))
     grad_output, grad_down, grad_gate, grad_up, attended_grad = lax.optimization_barrier(
         (grad_output.astype(bf16), grad_down, grad_gate, grad_up, attended_grad)
     )
     grad_output, grad_down = lax.psum((grad_output, grad_down), "dp")
     grad_query, grad_key, grad_value, normed_part, gain_grad_heads, expert_sum = attention_back(
         shards, width, limit, queries, keys, values, query_raw, key_raw, factors, cosine, sine,
-        head_gains, query_weight, key_weight, value_weight, normed, sum_parts, attended_grad,
+        own_gains, query_weight, key_weight, value_weight, normed, sum_parts, attended_grad,
         full_output,
     )
     expert_sum = expert_sum.reshape(rows, width)
@@ -1608,7 +1615,7 @@
     )
     grad_query, grad_key, grad_value = lax.psum((grad_query, grad_key, grad_value), "dp")
     through_norm, grad_gains = scatter_norm(
-        shards, groups, 16, normed_part, tokens, gain_in[None, :],
+        shards, groups, 16, normed_part, tokens, gains,
         other_gains=(gain_grad_res, gain_grad_heads),
     )
     through_norm, expert_sum = lax.optimization_barrier((through_norm, expert_sum))

time: 678 us -> 672 us (level)
  transfers between devices with their start and end apart: 5 -> 5, of which waited for: 2 -> 2; matrix products, arithmetic and copies ran while one was open for 3% -> 3% of each run, Pallas kernels for 69% -> 71%
where the time goes in v7:
time: 672 us; the launch traced here: 667 us
  Pallas kernels  620 us (92%)
  between operations  14.6 us (2%)
  waiting for transfers between devices  13.4 us (2%)
  other arithmetic  9.22 us (1%)
    pallas_call x2, Pallas kernels, scatter_norm(): pl.pallas_call(functools.partial(scatter_norm_kernel, n, groups, steps, g...  214 us
    pallas_call x1, Pallas kernels, gather_project(): pl.pallas_call(functools.partial(gather_project_kernel, n), out_shape=[ja...  100 us
    pallas_call x1, Pallas kernels, attention_back(): pl.pallas_call(functools.partial(attention_back_kernel, n, steps, width),...  94.4 us
    pallas_call x1, Pallas kernels, gather_line(): pl.pallas_call(functools.partial(gather_line_kernel, n), out_shape=jax.Sh...  68.8 us
    pallas_call x1, Pallas kernels, forward_pass(): pl.pallas_call(forward_kernel, out_shape=[jax.ShapeDtypeStruct((L, D), f3...  53.8 us
    pallas_call x3, Pallas kernels, widen(): pl.pallas_call(functools.partial(widen_kernel, len(flat)), out_shape=[jax...  27.3 us
    pallas_call x1, Pallas kernels, backward_pass(): pl.pallas_call(backward_kernel, out_shape=[wide, wide, narrow, narrow], g...  25.9 us
    pallas_call x1, Pallas kernels, attention(): pl.pallas_call(functools.partial(attention_kernel, n), out_shape=[out] *...  21.8 us
  transfers between devices with their start and end apart: 5, of which 2 were waited for; matrix products, arithmetic and copies ran while one was open for 3% of the time, Pallas kernels for 71%

profile of v7, /device:TPU:12, one launch (start us, length us, event | category | flops | bytes accessed | tf_op | source)
XLA Modules:
  0.0 667.4 jit_solution(6239409187081759552)
XLA Ops:
  7.2 0.0 all-gather.4.cloned.1.call-start
  7.2 0.8 fusion.1
  8.0 0.7 select_reduce_fusion
  8.7 0.6 select_maximum_fusion.small_ref
  9.3 100.1 %gather_project.1 = (bf16[4,256,2048]{2,1,0:T(8,128)(2,1)}, bf16[4,256,2048]{2,1,0:T(8,128)(2,1)}, f32[4,256,512]{2,1,0:T(8,128)}, f32[4,256,512]{2,1,0:T(8,128)...) custom-call(bf16[256,2048]{1,0:T(8,128)(2,1)} %x_hbm.1, ...), custom_call_target="tpu_custom_call" | custom-call | flops 80000000000 | bytes 33554432 | tf_op jit(solution)/shard_map/gather_project/pallas_call | solution.py:342
  109.4 0.0 all-gather.4.cloned.1.call-update
  109.5 0.0 all-gather.6.cloned.1.call-start
  109.5 0.6 convert_element_type.17.gains
  110.8 0.9 slice.12
  111.7 0.6 broadcast_in_dim.23.limit_ref
  112.3 21.8 %attention.1 = (bf16[1024,512]{1,0:T(8,128)(2,1)}, bf16[1024,512]{1,0:T(8,128)(2,1)}, bf16[1024,512]{1,0:T(8,128)(2,1)}, bf16[4,64,2048]{2,1,0:T(8,128)(2,1)}) custom-call(s32[8,128]{1,0:T(8,128)} %broadcast_in_dim.23.limit_ref, f32[1024,512]{1,0:T(8,128)} %bitcast.47, f32[1024,512]{1,0:T(8,128)} %bitcast.49, bf16[1024,512]{1,0:T(8,128)(2,1)} %bitcast.51, ...), custom_call_target="tpu_custom_call" | custom-call | flops 20000000000 | bytes 16777216 | tf_op jit(solution)/shard_map/attention/pallas_call | solution.py:476
  134.1 68.8 %gather_line.1.mixed = bf16[1024,2048]{1,0:T(8,128)(2,1)} custom-call(bf16[1024,512]{1,0:T(8,128)(2,1)} %get-tuple-element.86.v_hbm), custom_call_target="tpu_custom_call" | custom-call | flops 70000001024 | bytes 8388608 | tf_op jit(solution)/shard_map/gather_line/pallas_call | solution.py:1499
  202.9 0.2 all-reduce.13.cloned.1.call-start
  203.2 0.0 all-gather.4.cloned.1.call-done.weight.output_hbm
  203.2 53.8 %forward_pass.1 = (f32[1024,2048]{1,0:T(8,128)}, bf16[2048,1024]{1,0:T(8,128)(2,1)}, f32[1024,1024]{1,0:T(8,128)}, f32[1024,1024]{1,0:T(8,128)}, bf16[1024,1024]...) custom-call(bf16[1024,2048]{1,0:T(8,128)(2,1)} %gather_line.1.mixed,, ...), custom_call_target="tpu_custom_call" | custom-call | flops 21474836480 | bytes 52428800 | tf_op jit(solution)/shard_map/forward_pass/pallas_call | solution.py:1146
  257.0 10.3 %all-gather.6.cloned.1.call-done = bf16[768,2048]{1,0:T(8,128)(2,1)} async-done(((bf16[192,2048]{1,0:T(8,128)(2,1)}), bf16[768,2048]{1,0:T(8,128)(2,1)}) %all-gather.6.cloned.1.call-update) | async-done | bytes 3145744 | tf_op jit(solution)/shard_map/all_gather | solution.py:1573
  267.3 25.9 %backward_pass.1 = (bf16[1024,2048]{1,0:T(8,128)(2,1)}, bf16[1024,2048]{1,0:T(8,128)(2,1)}, bf16[1024,1024]{1,0:T(8,128)(2,1)}, bf16[1024,1024]{1,0:T(8,128)(2,1)}) custom-call(bf16[4,64,2048]{2,1,0:T(8,128)(2,1)} %get-tuple-element.97.first, bf16[4,192,2048]{2,1,0:T(8,128)(2,1)} %bitcast.61, f32[1024,1024]{1,0:T(8,128)} %get-tuple-element.99.gate_ref, ...), custom_call_target="tpu_custom_call" | custom-call | flops 12884901888 | bytes 41943040 | tf_op jit(solution)/shard_map/backward_pass/pallas_call | solution.py:1239
  293.1 13.3 %expert_grads.1 = (bf16[4,2048,256]{2,1,0:T(8,128)(2,1)}, bf16[4,2048,256]{2,1,0:T(8,128)(2,1)}) custom-call(bf16[2048,1024]{1,0:T(8,128)(2,1)} %get-tuple-element.105.xt, bf16[1024,1024]{1,0:T(8,128)(2,1)} %get-tuple-element.106.gate_grad, bf16[1024,1024]{1,0:T(8,128)(2,1)} %get-tuple-element.107.up_grad), custom_call_target="tpu_custom_call" | custom-call | flops 8589934592 | bytes 16777216 | tf_op jit(solution)/shard_map/expert_grads/pallas_call | solution.py:1377
  306.5 0.3 all-reduce.11.cloned.1.call-start
  306.8 122.5 %scatter_norm_gather.1 = (f32[16,16,2048]{2,1,0:T(8,128)}, bf16[4,16,16,2048]{3,2,1,0:T(8,128)(2,1)}, bf16[4,16,16,512]{3,2,1,0:T(8,128)(2,1)}, f32[8,2048]{1,0:T(8,128)}, bf16[4,256,2048]{2,1,0:T(8,128)(2,1)}) custom-call(bf16[4,16,16,2048]{3,2,1,0:T(8,128)(2,1)} %bitcast.36, bf16[16,16,2048]{2,1,0:T(8,128)(2,1)} %bitcast.34, ...), custom_call_target="tpu_custom_call" | custom-call | flops 1000000000 | bytes 1048576 | tf_op jit(solution)/shard_map/scatter_norm_gather/pallas_call | solution.py:1066
  429.3 6.2 convolution_convert_fusion
  435.5 0.0 all-reduce.9.cloned.1.call-start
  435.6 94.4 %attention_back.1 = (bf16[2048,512]{1,0:T(8,128)(2,1)}, bf16[2048,512]{1,0:T(8,128)(2,1)}, bf16[2048,512]{1,0:T(8,128)(2,1)}, bf16[1024,2048]{1,0:T(8,128)(2,1)}...) custom-call(s32[8,128]{1,0:T(8,128)} %broadcast_in_dim.23.limit_ref, bf16[1024,512]{1,0:T(8,128)(2,1)} %get-tuple-element.93.q_ref, ...), custom_call_target="tpu_custom_call" | custom-call | flops 2000000000 | bytes 1048576 | tf_op jit(solution)/shard_map/attention_back/pallas_call | solution.py:710
  530.0 10.1 %widen.3 = (f32[8192,256]{1,0:T(8,128)}, f32[8192,256]{1,0:T(8,128)}) custom-call(bf16[8192,256]{1,0:T(8,128)(2,1)} %bitcast.38, bf16[8192,256]{1,0:T(8,128)(2,1)} %bitcast.39), custom_call_target="tpu_custom_call" | custom-call | bytes 25165824 | tf_op jit(solution)/shard_map/widen/pallas_call | solution.py:1402
  540.0 3.0 all-reduce.11.cloned.1.call-done
  543.1 91.8 %scatter_norm.1 = (f32[16,16,2048]{2,1,0:T(8,128)}, f32[8,512]{1,0:T(8,128)}) custom-call(bf16[4,16,16,2048]{3,2,1,0:T(8,128)(2,1)} %bitcast.40, bf16[16,16,2048]{2,1,0:T(8,128)(2,1)} %bitcast.35, f32[8,2048]{1,0:T(8,128)} %get-tuple-element.90.gain.refs_2_, f32[8,2048]{1,0:T(8,128)} %get-tuple-element.133.refs_3_, f32[2,512]{1,0:T(2,128)} %get-tuple-element.134.refs_4_), custom_call_target="tpu_custom_call" | custom-call | flops 1000000000 | bytes 1048576 | tf_op jit(solution)/shard_map/scatter_norm/pallas_call | solution.py:1066
  634.9 1.5 slice.15
  636.3 8.7 %widen.5 = (f32[1024,2048]{1,0:T(8,128)}, f32[2048,512]{1,0:T(8,128)}) custom-call(bf16[1024,2048]{1,0:T(8,128)(2,1)} %bitcast.37, bf16[2048,512]{1,0:T(8,128)(2,1)} %get-tuple-element.147.refs_1_), custom_call_target="tpu_custom_call" | custom-call | bytes 18874368 | tf_op jit(solution)/shard_map/widen/pallas_call | solution.py:1402
  645.1 3.4 add.36
  648.5 3.3 multiply_reduce_fusion.2
  651.8 0.6 pad_maximum_fusion
  652.4 8.5 %widen.4 = (f32[2048,512]{1,0:T(8,128)}, f32[2048,512]{1,0:T(8,128)}, f32[2048,512]{1,0:T(8,128)}) custom-call(bf16[2048,512]{1,0:T(8,128)(2,1)} %get-tuple-element.156.refs_0_, bf16[2048,512]{1,0:T(8,128)(2,1)} %get-tuple-element.157.refs_1_, bf16[2048,512]{1,0:T(8,128)(2,1)} %get-tuple-element.158.refs_2_), custom_call_target="tpu_custom_call" | custom-call | bytes 18874368 | tf_op jit(solution)/shard_map/widen/pallas_call | solution.py:1402
  (19 shorter events, 0.1 us)
Async XLA Ops:
  7.2 196.0 %all-gather.4.cloned.1.call-start = ((), (), s32[]{:S(2)}) async-start(), calls=%async_computation | async-start | bytes 9437184 | tf_op jit(solution)/shard_map/all_gather | solution.py:1559
  9.3 100.2 %copy-start.4 = (bf16[4,512]{1,0:T(4,128)(2,1)S(1)}, bf16[4,512]{1,0:T(4,128)(2,1)}, u32[]{:S(2)}) copy-start(bf16[4,512]{1,0:T(4,128)(2,1)} %param.24) | copy-start | bytes 12292
  9.3 101.4 %copy-start.1 = (bf16[256,2048]{1,0:T(8,128)(2,1)S(1)}, bf16[256,2048]{1,0:T(8,128)(2,1)}, u32[]{:S(2)}) copy-start(bf16[256,2048]{1,0:T(8,128)(2,1)} %grad_hbm.1) | copy-start | bytes 3145732
  109.5 157.8 %all-gather.6.cloned.1.call-start = ((), (), s32[]{:S(2)}) async-start(), calls=%async_computation.1 | async-start | bytes 3932160 | tf_op jit(solution)/shard_map/all_gather | solution.py:1573
  202.9 232.5 %all-reduce.13.cloned.1.call-start = ((), (), s32[]{:S(2)}) async-start(), calls=%async_computation.4 | async-start | bytes 16777216 | tf_op jit(solution)/shard_map/psum | solution.py:1584
  306.5 236.5 %all-reduce.11.cloned.1.call-start = ((), (), s32[]{:S(2)}) async-start(), calls=%async_computation.3 | async-start | bytes 12582912 | tf_op jit(solution)/shard_map/psum | solution.py:1599
  435.5 216.8 %all-reduce.9.cloned.1.call-start = ((), (), s32[]{:S(2)}) async-start(), calls=%async_computation.2 | async-start | bytes 12582912 | tf_op jit(solution)/shard_map/psum | solution.py:1616
  634.9 10.2 %copy-start.2 = (f32[16,16,2048]{2,1,0:T(8,128)S(1)}, f32[16,16,2048]{2,1,0:T(8,128)}, u32[]{:S(2)}) copy-start(f32[16,16,2048]{2,1,0:T(8,128)} %get-tuple-element.138) | copy-start | bytes 6291460
  645.1 3.4 copy-start
  645.1 3.4 copy-start.3
Sparse Core Ops, SparseCore 0:
  109.6 55.2 all-gather.3
  203.1 64.1 all-gather.5
  306.6 127.5 all-reduce.12
  438.4 104.5 all-reduce.10
  546.5 105.5 all-reduce.8

commit v8 on v7

--- a/solution.py
+++ b/solution.py
@@ -177,9 +177,6 @@
             device_id=(d, lax.rem(z + n - 1, n)), device_id_type=MESH,
         )
 
-    slab_load.wait()
-    slab_begin()
-    slab_save(z).start()
     own_load.wait()
     small_copies = []
     for p, peer in enumerate(peers):
@@ -244,7 +241,6 @@
 
     def step(s, carry):
         below, above = z - s, z + s
-        slab_hop(s, lambda o: slab_save(o).start())
 
         @pl.when((s > 0) & (below >= 0))
         def _():
@@ -261,6 +257,12 @@
             @pl.when(z > 0)
             def _():
                 send_down(above).start()
+
+        @pl.when(s == n - 1)
+        def _():
+            slab_load.wait()
+            slab_begin()
+            slab_save(z).start()
 
         def side(j, inner):
             o = z - s + 2 * s * j
@@ -284,6 +286,12 @@
         )
         copy.start()
         sq_copies.append(copy)
+
+    def slab_hops(s, carry):
+        slab_hop(s, lambda o: slab_save(o).start())
+        return carry
+
+    lax.fori_loop(1, n, slab_hops, 0)
 
     def spread(o, carry):
         r = pl.ds(pl.multiple_of(o * T, T), T)
@@ -751,13 +759,29 @@
 
 
 def scatter_norm_kernel(n, groups, steps, gather, *refs):
-    part, base, gain = refs[:3]
-    refs = refs[3:]
+    part_hbm, base, gain = refs[:3]
+    part, part_sem = refs[-2:]
+    refs = refs[3:-2]
+    steps_first = 2
+    part_loads = [
+        pltpu.make_async_copy(part_hbm.at[:, c], part.at[:, c], part_sem.at[i])
+        for i, c in enumerate((slice(0, steps_first), slice(steps_first, steps)))
+    ]
+    for part_load in part_loads:
+        part_load.start()
     if gather:
-        addend, attended_hbm, hidden, g_all = refs[:4]
+        addend, attended_hbm, hidden_hbm, g_hbm = refs[:4]
         out, all_out, columns_out, gain_out, down_out = refs[4:9]
         alls, ag_up, ag_down, ag_recv, all_sem, attended, load_sem = refs[9:16]
-        refs = refs[16:]
+        hidden, g_all, down, down_sem = refs[16:20]
+        refs = refs[20:]
+        later_loads = [
+            pltpu.make_async_copy(hidden_hbm, hidden, load_sem.at[1]),
+            pltpu.make_async_copy(g_hbm, g_all, load_sem.at[2]),
+        ]
+
+        def down_save(e):
+            return pltpu.make_async_copy(down.at[e], down_out.at[e], down_sem.at[e])
     else:
         expert_gains, head_gains, out, gain_out = refs[:4]
         pieces, landed, sums, piece_send, piece_recv, sum_send, sum_recv = refs[4:11]
@@ -773,6 +797,9 @@
     greet(peers + alike)
     if gather:
         load.wait()
+        for later_load in later_loads:
+            later_load.start()
+    part_loads[0].wait()
     gain_acc[...] = jnp.zeros_like(gain_acc)
 
     def move_up(src, o, k):
@@ -914,6 +941,10 @@
     def turn(t, carry):
         up_k, down_k, own_k = t - z, t - (n - 1 - z), t - (n - 1)
 
+        @pl.when(t == steps_first)
+        def _():
+            part_loads[1].wait()
+
         @pl.when((up_k >= 0) & (up_k < steps))
         def _():
             pass_up(up_k)
@@ -928,13 +959,19 @@
 
         if gather:
             forward(own_k)
-            experts, units = down_out.shape[:2]
+            experts, units = down.shape[:2]
             e = t - n
 
+            @pl.when(e == 0)
+            def _():
+                for later_load in later_loads:
+                    later_load.wait()
+
             @pl.when((e >= 0) & (e < experts))
             def _():
                 c = pl.ds(pl.multiple_of(e * units, units), units)
-                down_out[e] = dot_tn(hidden[:, c], g_all[...]).astype(bf16)
+                down[e] = dot_tn(hidden[:, c], g_all[...]).astype(bf16)
+                down_save(e).start()
 
         return carry
 
@@ -1031,6 +1068,8 @@
             copies.append(pltpu.make_async_copy(alls.at[o], all_out.at[o], all_sem.at[o]))
         for copy in copies:
             copy.start()
+        for e in range(down.shape[0]):
+            down_save(e).wait()
         for copy in copies:
             copy.wait()
 
@@ -1052,7 +1091,9 @@
         more = (
             addend.reshape(steps, R, D), attended.reshape(n, steps, R, D), hidden, g_all,
         )
-        own = [slots, sems, sems, sems, dma((2 * n,)), pltpu.VMEM((steps, R, D), f32), dma((1,))]
+        own = [slots, sems, sems, sems, dma((2 * n,)), pltpu.VMEM((steps, R, D), f32), dma((3,))]
+        own += [pltpu.VMEM(hidden.shape, bf16), pltpu.VMEM(g_all.shape, bf16)]
+        own += [pltpu.VMEM((experts, units, D), bf16), dma((experts,))]
         outs = [rows, jax.ShapeDtypeStruct((n, steps, R, D), bf16)]
         outs += [jax.ShapeDtypeStruct((n, steps, R, C), bf16)]
         outs += [jax.ShapeDtypeStruct((8, D), f32)]
@@ -1066,9 +1107,10 @@
     return pl.pallas_call(
         functools.partial(scatter_norm_kernel, n, groups, steps, gather),
         out_shape=outs,
-        in_specs=[vmem] * 4 + [hbm, vmem, vmem] if gather else [vmem] * 5,
-        out_specs=[vmem, hbm, hbm, vmem, vmem] if gather else [vmem, vmem],
-        scratch_shapes=own + [slots, slots, pltpu.VMEM((8, D), f32), sems, sems, sems, sems],
+        in_specs=[hbm] + ([vmem] * 3 + [hbm] * 3 if gather else [vmem] * 4),
+        out_specs=[vmem, hbm, hbm, vmem, hbm] if gather else [vmem, vmem],
+        scratch_shapes=own
+        + [slots, slots, pltpu.VMEM((8, D), f32), sems, sems, sems, sems, slots, dma((2,))],
         compiler_params=pltpu.CompilerParams(
             collective_id=2 if gather else 3, has_side_effects=True, vmem_limit_bytes=VMEM_LIMIT
         ),

time: 672 us -> 667 us (level)
  Pallas kernels: 620 us -> 609 us
  transfers between devices with their start and end apart: 5 -> 5, of which waited for: 2 -> 4; matrix products, arithmetic and copies ran while one was open for 3% -> 3% of each run, Pallas kernels for 71% -> 70%
where the time goes in v8:
time: 667 us; the launch traced here: 663 us
  Pallas kernels  609 us (91%)
  waiting for transfers between devices  19.1 us (3%)
  between operations  14.6 us (2%)
  other arithmetic  9.29 us (1%)
    pallas_call x2, Pallas kernels, scatter_norm(): pl.pallas_call(functools.partial(scatter_norm_kernel, n, groups, steps, g...  210 us
    pallas_call x1, Pallas kernels, gather_project(): pl.pallas_call(functools.partial(gather_project_kernel, n), out_shape=[ja...  95.3 us
    pallas_call x1, Pallas kernels, attention_back(): pl.pallas_call(functools.partial(attention_back_kernel, n, steps, width),...  92.8 us
    pallas_call x1, Pallas kernels, gather_line(): pl.pallas_call(functools.partial(gather_line_kernel, n), out_shape=jax.Sh...  68.7 us
    pallas_call x1, Pallas kernels, forward_pass(): pl.pallas_call(forward_kernel, out_shape=[jax.ShapeDtypeStruct((L, D), f3...  53.8 us
    pallas_call x3, Pallas kernels, widen(): pl.pallas_call(functools.partial(widen_kernel, len(flat)), out_shape=[jax...  27.3 us
    pallas_call x1, Pallas kernels, backward_pass(): pl.pallas_call(backward_kernel, out_shape=[wide, wide, narrow, narrow], g...  25.9 us
    pallas_call x1, Pallas kernels, attention(): pl.pallas_call(functools.partial(attention_kernel, n), out_shape=[out] *...  22.9 us
  transfers between devices with their start and end apart: 5, of which 4 were waited for; matrix products, arithmetic and copies ran while one was open for 3% of the time, Pallas kernels for 70%

profile of v8, /device:TPU:12, one launch (start us, length us, event | category | flops | bytes accessed | tf_op | source)
XLA Modules:
  0.0 663.1 jit_solution(18154933017211800535)
XLA Ops:
  7.2 0.0 all-gather.4.cloned.1.call-start
  7.2 0.8 fusion.1
  8.0 0.7 select_reduce_fusion
  8.7 0.6 select_maximum_fusion.small_ref
  9.3 95.3 %gather_project.1 = (bf16[4,256,2048]{2,1,0:T(8,128)(2,1)}, bf16[4,256,2048]{2,1,0:T(8,128)(2,1)}, f32[4,256,512]{2,1,0:T(8,128)}, f32[4,256,512]{2,1,0:T(8,128)...) custom-call(bf16[256,2048]{1,0:T(8,128)(2,1)} %x_hbm.1, ...), custom_call_target="tpu_custom_call" | custom-call | flops 80000000000 | bytes 33554432 | tf_op jit(solution)/shard_map/gather_project/pallas_call | solution.py:350
  104.6 0.0 all-gather.6.cloned.1.call-start
  104.7 0.6 convert_element_type.17.gains
  106.0 0.9 slice.12
  106.9 0.6 broadcast_in_dim.23.limit_ref
  107.5 22.9 %attention.1 = (bf16[1024,512]{1,0:T(8,128)(2,1)}, bf16[1024,512]{1,0:T(8,128)(2,1)}, bf16[1024,512]{1,0:T(8,128)(2,1)}, bf16[4,64,2048]{2,1,0:T(8,128)(2,1)}) custom-call(s32[8,128]{1,0:T(8,128)} %broadcast_in_dim.23.limit_ref, f32[1024,512]{1,0:T(8,128)} %bitcast.47, f32[1024,512]{1,0:T(8,128)} %bitcast.49, bf16[1024,512]{1,0:T(8,128)(2,1)} %bitcast.51, ...), custom_call_target="tpu_custom_call" | custom-call | flops 20000000000 | bytes 16777216 | tf_op jit(solution)/shard_map/attention/pallas_call | solution.py:484
  130.4 68.7 %gather_line.1.mixed = bf16[1024,2048]{1,0:T(8,128)(2,1)} custom-call(bf16[1024,512]{1,0:T(8,128)(2,1)} %get-tuple-element.86.v_hbm), custom_call_target="tpu_custom_call" | custom-call | flops 70000001024 | bytes 8388608 | tf_op jit(solution)/shard_map/gather_line/pallas_call | solution.py:1541
  199.1 0.2 all-reduce.13.cloned.1.call-start
  199.3 53.8 %forward_pass.1 = (f32[1024,2048]{1,0:T(8,128)}, bf16[2048,1024]{1,0:T(8,128)(2,1)}, f32[1024,1024]{1,0:T(8,128)}, f32[1024,1024]{1,0:T(8,128)}, bf16[1024,1024]...) custom-call(bf16[1024,2048]{1,0:T(8,128)(2,1)} %gather_line.1.mixed,, ...), custom_call_target="tpu_custom_call" | custom-call | flops 21474836480 | bytes 52428800 | tf_op jit(solution)/shard_map/forward_pass/pallas_call | solution.py:1188
  253.1 10.2 %all-gather.6.cloned.1.call-done = bf16[768,2048]{1,0:T(8,128)(2,1)} async-done(((bf16[192,2048]{1,0:T(8,128)(2,1)}), bf16[768,2048]{1,0:T(8,128)(2,1)}) %all-gather.6.cloned.1.call-update) | async-done | bytes 3145744 | tf_op jit(solution)/shard_map/all_gather | solution.py:1615
  263.3 25.9 %backward_pass.1 = (bf16[1024,2048]{1,0:T(8,128)(2,1)}, bf16[1024,2048]{1,0:T(8,128)(2,1)}, bf16[1024,1024]{1,0:T(8,128)(2,1)}, bf16[1024,1024]{1,0:T(8,128)(2,1)}) custom-call(bf16[4,64,2048]{2,1,0:T(8,128)(2,1)} %get-tuple-element.97.first, bf16[4,192,2048]{2,1,0:T(8,128)(2,1)} %bitcast.61, f32[1024,1024]{1,0:T(8,128)} %get-tuple-element.99.gate_ref, ...), custom_call_target="tpu_custom_call" | custom-call | flops 12884901888 | bytes 41943040 | tf_op jit(solution)/shard_map/backward_pass/pallas_call | solution.py:1281
  289.2 13.4 %expert_grads.1 = (bf16[4,2048,256]{2,1,0:T(8,128)(2,1)}, bf16[4,2048,256]{2,1,0:T(8,128)(2,1)}) custom-call(bf16[2048,1024]{1,0:T(8,128)(2,1)} %get-tuple-element.105.xt, bf16[1024,1024]{1,0:T(8,128)(2,1)} %get-tuple-element.106.gate_grad, bf16[1024,1024]{1,0:T(8,128)(2,1)} %get-tuple-element.107.up_grad), custom_call_target="tpu_custom_call" | custom-call | flops 8589934592 | bytes 16777216 | tf_op jit(solution)/shard_map/expert_grads/pallas_call | solution.py:1419
  302.6 0.3 all-reduce.11.cloned.1.call-start
  302.9 119.1 %scatter_norm_gather.1 = (f32[16,16,2048]{2,1,0:T(8,128)}, bf16[4,16,16,2048]{3,2,1,0:T(8,128)(2,1)}, bf16[4,16,16,512]{3,2,1,0:T(8,128)(2,1)}, f32[8,2048]{1,0:T(8,128)}, bf16[4,256,2048]{2,1,0:T(8,128)(2,1)}) custom-call(bf16[4,16,16,2048]{3,2,1,0:T(8,128)(2,1)} %bitcast.36, bf16[16,16,2048]{2,1,0:T(8,128)(2,1)} %bitcast.34, ...), custom_call_target="tpu_custom_call" | custom-call | flops 1000000000 | bytes 1048576 | tf_op jit(solution)/shard_map/scatter_norm_gather/pallas_call | solution.py:1107
  421.9 6.3 convolution_convert_fusion
  428.3 2.1 all-reduce.13.cloned.1.call-done
  430.4 0.0 all-reduce.9.cloned.1.call-start
  430.4 92.8 %attention_back.1 = (bf16[2048,512]{1,0:T(8,128)(2,1)}, bf16[2048,512]{1,0:T(8,128)(2,1)}, bf16[2048,512]{1,0:T(8,128)(2,1)}, bf16[1024,2048]{1,0:T(8,128)(2,1)}...) custom-call(s32[8,128]{1,0:T(8,128)} %broadcast_in_dim.23.limit_ref, bf16[1024,512]{1,0:T(8,128)(2,1)} %get-tuple-element.93.q_ref, ...), custom_call_target="tpu_custom_call" | custom-call | flops 2000000000 | bytes 1048576 | tf_op jit(solution)/shard_map/attention_back/pallas_call | solution.py:718
  523.2 10.2 %widen.3 = (f32[8192,256]{1,0:T(8,128)}, f32[8192,256]{1,0:T(8,128)}) custom-call(bf16[8192,256]{1,0:T(8,128)(2,1)} %bitcast.38, bf16[8192,256]{1,0:T(8,128)(2,1)} %bitcast.39), custom_call_target="tpu_custom_call" | custom-call | bytes 25165824 | tf_op jit(solution)/shard_map/widen/pallas_call | solution.py:1444
  533.4 5.8 all-reduce.11.cloned.1.call-done
  539.2 90.4 %scatter_norm.1 = (f32[16,16,2048]{2,1,0:T(8,128)}, f32[8,512]{1,0:T(8,128)}) custom-call(bf16[4,16,16,2048]{3,2,1,0:T(8,128)(2,1)} %bitcast.40, bf16[16,16,2048]{2,1,0:T(8,128)(2,1)} %bitcast.35, f32[8,2048]{1,0:T(8,128)} %get-tuple-element.90.gain.refs_2_, f32[8,2048]{1,0:T(8,128)} %get-tuple-element.133.refs_3_, f32[2,512]{1,0:T(2,128)} %get-tuple-element.134.refs_4_), custom_call_target="tpu_custom_call" | custom-call | flops 1000000000 | bytes 1048576 | tf_op jit(solution)/shard_map/scatter_norm/pallas_call | solution.py:1107
  629.7 1.5 slice.15
  631.1 8.6 %widen.5 = (f32[1024,2048]{1,0:T(8,128)}, f32[2048,512]{1,0:T(8,128)}) custom-call(bf16[1024,2048]{1,0:T(8,128)(2,1)} %bitcast.37, bf16[2048,512]{1,0:T(8,128)(2,1)} %get-tuple-element.147.refs_1_), custom_call_target="tpu_custom_call" | custom-call | bytes 18874368 | tf_op jit(solution)/shard_map/widen/pallas_call | solution.py:1444
  639.7 3.5 add.36
  643.2 3.3 multiply_reduce_fusion.2
  646.5 0.6 pad_maximum_fusion
  647.1 1.0 all-reduce.9.cloned.1.call-done
  648.1 8.5 %widen.4 = (f32[2048,512]{1,0:T(8,128)}, f32[2048,512]{1,0:T(8,128)}, f32[2048,512]{1,0:T(8,128)}) custom-call(bf16[2048,512]{1,0:T(8,128)(2,1)} %get-tuple-element.156.refs_0_, bf16[2048,512]{1,0:T(8,128)(2,1)} %get-tuple-element.157.refs_1_, bf16[2048,512]{1,0:T(8,128)(2,1)} %get-tuple-element.158.refs_2_), custom_call_target="tpu_custom_call" | custom-call | bytes 18874368 | tf_op jit(solution)/shard_map/widen/pallas_call | solution.py:1444
  (19 shorter events, 0.1 us)
Async XLA Ops:
  7.2 192.2 %all-gather.4.cloned.1.call-start = ((), (), s32[]{:S(2)}) async-start(), calls=%async_computation | async-start | bytes 9437184 | tf_op jit(solution)/shard_map/all_gather | solution.py:1601
  9.3 95.4 %copy-start.4 = (bf16[4,512]{1,0:T(4,128)(2,1)S(1)}, bf16[4,512]{1,0:T(4,128)(2,1)}, u32[]{:S(2)}) copy-start(bf16[4,512]{1,0:T(4,128)(2,1)} %param.24) | copy-start | bytes 12292
  9.3 96.6 %copy-start.1 = (bf16[256,2048]{1,0:T(8,128)(2,1)S(1)}, bf16[256,2048]{1,0:T(8,128)(2,1)}, u32[]{:S(2)}) copy-start(bf16[256,2048]{1,0:T(8,128)(2,1)} %grad_hbm.1) | copy-start | bytes 3145732
  104.6 158.7 %all-gather.6.cloned.1.call-start = ((), (), s32[]{:S(2)}) async-start(), calls=%async_computation.1 | async-start | bytes 3932160 | tf_op jit(solution)/shard_map/all_gather | solution.py:1615
  199.1 231.3 %all-reduce.13.cloned.1.call-start = ((), (), s32[]{:S(2)}) async-start(), calls=%async_computation.4 | async-start | bytes 16777216 | tf_op jit(solution)/shard_map/psum | solution.py:1626
  302.6 236.6 %all-reduce.11.cloned.1.call-start = ((), (), s32[]{:S(2)}) async-start(), calls=%async_computation.3 | async-start | bytes 12582912 | tf_op jit(solution)/shard_map/psum | solution.py:1641
  430.4 217.7 %all-reduce.9.cloned.1.call-start = ((), (), s32[]{:S(2)}) async-start(), calls=%async_computation.2 | async-start | bytes 12582912 | tf_op jit(solution)/shard_map/psum | solution.py:1658
  629.6 10.1 %copy-start.2 = (f32[16,16,2048]{2,1,0:T(8,128)S(1)}, f32[16,16,2048]{2,1,0:T(8,128)}, u32[]{:S(2)}) copy-start(f32[16,16,2048]{2,1,0:T(8,128)} %get-tuple-element.138) | copy-start | bytes 6291460
  639.7 3.5 copy-start
  639.7 3.5 copy-start.3
Sparse Core Ops, SparseCore 0:
  104.8 56.3 all-gather.3
  199.2 64.0 all-gather.5
  302.7 127.5 all-reduce.12
  434.5 104.6 all-reduce.10
  542.6 105.4 all-reduce.8

commit v9 on v8

--- a/solution.py
+++ b/solution.py
@@ -258,11 +258,15 @@
             def _():
                 send_down(above).start()
 
-        @pl.when(s == n - 1)
+        @pl.when(s == n - 2)
         def _():
             slab_load.wait()
             slab_begin()
             slab_save(z).start()
+
+        @pl.when(s == n - 1)
+        def _():
+            slab_hop(1, lambda o: slab_save(o).start())
 
         def side(j, inner):
             o = z - s + 2 * s * j
@@ -291,7 +295,7 @@
         slab_hop(s, lambda o: slab_save(o).start())
         return carry
 
-    lax.fori_loop(1, n, slab_hops, 0)
+    lax.fori_loop(2, n - 1, slab_hops, 0)
 
     def spread(o, carry):
         r = pl.ds(pl.multiple_of(o * T, T), T)
@@ -303,23 +307,6 @@
     for s in range(n):
         gains_out[:, s * C : (s + 1) * C] = small_all[s, :, T:]
 
-    def finish(o, carry):
-        for copy in outs(o):
-            copy.wait()
-        slab_save(o).wait()
-
-        @pl.when((z < n - 1) & (o <= z))
-        def _():
-            send_up(o).wait_send()
-
-        @pl.when((z > 0) & (o >= z))
-        def _():
-            send_down(o).wait_send()
-
-        return carry
-
-    lax.fori_loop(0, n, finish, 0)
-    slab_drain()
     for p in range(1, n):
         o = lax.rem(z + n - p, n)
         pltpu.make_async_remote_copy(
@@ -336,6 +323,25 @@
         return carry
 
     lax.fori_loop(0, n, turn_factors, 0)
+    lax.fori_loop(max(2, n - 1), n, slab_hops, 0)
+
+    def finish(o, carry):
+        for copy in outs(o):
+            copy.wait()
+        slab_save(o).wait()
+
+        @pl.when((z < n - 1) & (o <= z))
+        def _():
+            send_up(o).wait_send()
+
+        @pl.when((z > 0) & (o >= z))
+        def _():
+            send_down(o).wait_send()
+
+        return carry
+
+    lax.fori_loop(0, n, finish, 0)
+    slab_drain()
     for copy in small_copies + sq_copies:
         copy.wait_send()
 
@@ -1437,7 +1443,7 @@
 
 def widen(*arrays):
     flat = [v.reshape(-1, v.shape[-1]) for v in arrays]
-    steps = 8
+    steps = 4
     specs = [
         pl.BlockSpec((v.shape[0] // steps, v.shape[1]), lambda i: (i, 0)) for v in flat
     ]

time: 667 us -> 664 us (level)
  no operation moved by 1% of the time
where the time goes in v9:
time: 664 us; the launch traced here: 661 us
  Pallas kernels  606 us (91%)
  waiting for transfers between devices  20.7 us (3%)
  between operations  14.6 us (2%)
  other arithmetic  9.22 us (1%)
    pallas_call x2, Pallas kernels, scatter_norm(): pl.pallas_call(functools.partial(scatter_norm_kernel, n, groups, steps, g...  209 us
    pallas_call x1, Pallas kernels, gather_project(): pl.pallas_call(functools.partial(gather_project_kernel, n), out_shape=[ja...  94.5 us
    pallas_call x1, Pallas kernels, attention_back(): pl.pallas_call(functools.partial(attention_back_kernel, n, steps, width),...  92.7 us
    pallas_call x1, Pallas kernels, gather_line(): pl.pallas_call(functools.partial(gather_line_kernel, n), out_shape=jax.Sh...  68.9 us
    pallas_call x1, Pallas kernels, forward_pass(): pl.pallas_call(forward_kernel, out_shape=[jax.ShapeDtypeStruct((L, D), f3...  53.8 us
    pallas_call x1, Pallas kernels, backward_pass(): pl.pallas_call(backward_kernel, out_shape=[wide, wide, narrow, narrow], g...  25.9 us
    pallas_call x3, Pallas kernels, widen(): pl.pallas_call(functools.partial(widen_kernel, len(flat)), out_shape=[jax...  24.6 us
    pallas_call x1, Pallas kernels, attention(): pl.pallas_call(functools.partial(attention_kernel, n), out_shape=[out] *...  22.7 us
  transfers between devices with their start and end apart: 5, of which 4 were waited for; matrix products, arithmetic and copies ran while one was open for 3% of the time, Pallas kernels for 70%

profile of v9, /device:TPU:12, one launch (start us, length us, event | category | flops | bytes accessed | tf_op | source)
XLA Modules:
  0.0 661.2 jit_solution(13114729084879476267)
XLA Ops:
  7.2 0.0 all-gather.4.cloned.1.call-start
  7.2 0.8 fusion.1
  8.0 0.7 select_reduce_fusion
  8.7 0.6 select_maximum_fusion.small_ref
  9.3 94.5 %gather_project.1 = (bf16[4,256,2048]{2,1,0:T(8,128)(2,1)}, bf16[4,256,2048]{2,1,0:T(8,128)(2,1)}, f32[4,256,512]{2,1,0:T(8,128)}, f32[4,256,512]{2,1,0:T(8,128)...) custom-call(bf16[256,2048]{1,0:T(8,128)(2,1)} %x_hbm.1, ...), custom_call_target="tpu_custom_call" | custom-call | flops 80000000000 | bytes 33554432 | tf_op jit(solution)/shard_map/gather_project/pallas_call | solution.py:356
  103.9 0.0 all-gather.6.cloned.1.call-start
  103.9 0.6 convert_element_type.17.gains
  105.2 0.9 slice.12
  106.1 0.6 broadcast_in_dim.23.limit_ref
  106.7 22.7 %attention.1 = (bf16[1024,512]{1,0:T(8,128)(2,1)}, bf16[1024,512]{1,0:T(8,128)(2,1)}, bf16[1024,512]{1,0:T(8,128)(2,1)}, bf16[4,64,2048]{2,1,0:T(8,128)(2,1)}) custom-call(s32[8,128]{1,0:T(8,128)} %broadcast_in_dim.23.limit_ref, f32[1024,512]{1,0:T(8,128)} %bitcast.47, f32[1024,512]{1,0:T(8,128)} %bitcast.49, bf16[1024,512]{1,0:T(8,128)(2,1)} %bitcast.51, ...), custom_call_target="tpu_custom_call" | custom-call | flops 20000000000 | bytes 16777216 | tf_op jit(solution)/shard_map/attention/pallas_call | solution.py:490
  129.5 68.9 %gather_line.1.mixed = bf16[1024,2048]{1,0:T(8,128)(2,1)} custom-call(bf16[1024,512]{1,0:T(8,128)(2,1)} %get-tuple-element.86.v_hbm), custom_call_target="tpu_custom_call" | custom-call | flops 70000001024 | bytes 8388608 | tf_op jit(solution)/shard_map/gather_line/pallas_call | solution.py:1547
  198.5 0.2 all-reduce.13.cloned.1.call-start
  198.7 53.8 %forward_pass.1 = (f32[1024,2048]{1,0:T(8,128)}, bf16[2048,1024]{1,0:T(8,128)(2,1)}, f32[1024,1024]{1,0:T(8,128)}, f32[1024,1024]{1,0:T(8,128)}, bf16[1024,1024]...) custom-call(bf16[1024,2048]{1,0:T(8,128)(2,1)} %gather_line.1.mixed,, ...), custom_call_target="tpu_custom_call" | custom-call | flops 21474836480 | bytes 52428800 | tf_op jit(solution)/shard_map/forward_pass/pallas_call | solution.py:1194
  252.5 9.8 %all-gather.6.cloned.1.call-done = bf16[768,2048]{1,0:T(8,128)(2,1)} async-done(((bf16[192,2048]{1,0:T(8,128)(2,1)}), bf16[768,2048]{1,0:T(8,128)(2,1)}) %all-gather.6.cloned.1.call-update) | async-done | bytes 3145744 | tf_op jit(solution)/shard_map/all_gather | solution.py:1621
  262.3 25.9 %backward_pass.1 = (bf16[1024,2048]{1,0:T(8,128)(2,1)}, bf16[1024,2048]{1,0:T(8,128)(2,1)}, bf16[1024,1024]{1,0:T(8,128)(2,1)}, bf16[1024,1024]{1,0:T(8,128)(2,1)}) custom-call(bf16[4,64,2048]{2,1,0:T(8,128)(2,1)} %get-tuple-element.97.first, bf16[4,192,2048]{2,1,0:T(8,128)(2,1)} %bitcast.61, f32[1024,1024]{1,0:T(8,128)} %get-tuple-element.99.gate_ref, ...), custom_call_target="tpu_custom_call" | custom-call | flops 12884901888 | bytes 41943040 | tf_op jit(solution)/shard_map/backward_pass/pallas_call | solution.py:1287
  288.2 13.3 %expert_grads.1 = (bf16[4,2048,256]{2,1,0:T(8,128)(2,1)}, bf16[4,2048,256]{2,1,0:T(8,128)(2,1)}) custom-call(bf16[2048,1024]{1,0:T(8,128)(2,1)} %get-tuple-element.105.xt, bf16[1024,1024]{1,0:T(8,128)(2,1)} %get-tuple-element.106.gate_grad, bf16[1024,1024]{1,0:T(8,128)(2,1)} %get-tuple-element.107.up_grad), custom_call_target="tpu_custom_call" | custom-call | flops 8589934592 | bytes 16777216 | tf_op jit(solution)/shard_map/expert_grads/pallas_call | solution.py:1425
  301.6 0.3 all-reduce.11.cloned.1.call-start
  301.8 119.0 %scatter_norm_gather.1 = (f32[16,16,2048]{2,1,0:T(8,128)}, bf16[4,16,16,2048]{3,2,1,0:T(8,128)(2,1)}, bf16[4,16,16,512]{3,2,1,0:T(8,128)(2,1)}, f32[8,2048]{1,0:T(8,128)}, bf16[4,256,2048]{2,1,0:T(8,128)(2,1)}) custom-call(bf16[4,16,16,2048]{3,2,1,0:T(8,128)(2,1)} %bitcast.36, bf16[16,16,2048]{2,1,0:T(8,128)(2,1)} %bitcast.34, ...), custom_call_target="tpu_custom_call" | custom-call | flops 1000000000 | bytes 1048576 | tf_op jit(solution)/shard_map/scatter_norm_gather/pallas_call | solution.py:1113
  420.9 6.3 convolution_convert_fusion
  427.2 2.2 all-reduce.13.cloned.1.call-done
  429.4 0.0 all-reduce.9.cloned.1.call-start
  429.4 92.7 %attention_back.1 = (bf16[2048,512]{1,0:T(8,128)(2,1)}, bf16[2048,512]{1,0:T(8,128)(2,1)}, bf16[2048,512]{1,0:T(8,128)(2,1)}, bf16[1024,2048]{1,0:T(8,128)(2,1)}...) custom-call(s32[8,128]{1,0:T(8,128)} %broadcast_in_dim.23.limit_ref, bf16[1024,512]{1,0:T(8,128)(2,1)} %get-tuple-element.93.q_ref, ...), custom_call_target="tpu_custom_call" | custom-call | flops 2000000000 | bytes 1048576 | tf_op jit(solution)/shard_map/attention_back/pallas_call | solution.py:724
  522.1 9.3 %widen.3 = (f32[8192,256]{1,0:T(8,128)}, f32[8192,256]{1,0:T(8,128)}) custom-call(bf16[8192,256]{1,0:T(8,128)(2,1)} %bitcast.38, bf16[8192,256]{1,0:T(8,128)(2,1)} %bitcast.39), custom_call_target="tpu_custom_call" | custom-call | bytes 25165824 | tf_op jit(solution)/shard_map/widen/pallas_call | solution.py:1450
  531.4 6.8 %all-reduce.11.cloned.1.call-done = (bf16[2048,512]{1,0:T(8,128)(2,1)}, bf16[4,256,2048]{2,1,0:T(8,128)(2,1)}) async-done(((bf16[2048,512]{1,0:T(8,128)(2,1)}, bf16[4,256,2048]{2,1,0:T(8,128)(2,1)}), (bf16[2048,512]{1,0:T(8,128)(2,1)}, bf16[4,256,2048]{2,1,0:T(8,128)(2,1)})) %all-reduce.11.cloned.1.call-update) | async-done | bytes 6291472 | tf_op jit(solution)/shard_map/psum | solution.py:1647
  538.2 90.5 %scatter_norm.1 = (f32[16,16,2048]{2,1,0:T(8,128)}, f32[8,512]{1,0:T(8,128)}) custom-call(bf16[4,16,16,2048]{3,2,1,0:T(8,128)(2,1)} %bitcast.40, bf16[16,16,2048]{2,1,0:T(8,128)(2,1)} %bitcast.35, f32[8,2048]{1,0:T(8,128)} %get-tuple-element.90.gain.refs_2_, f32[8,2048]{1,0:T(8,128)} %get-tuple-element.133.refs_3_, f32[2,512]{1,0:T(2,128)} %get-tuple-element.134.refs_4_), custom_call_target="tpu_custom_call" | custom-call | flops 1000000000 | bytes 1048576 | tf_op jit(solution)/shard_map/scatter_norm/pallas_call | solution.py:1113
  628.7 1.5 slice.15
  630.2 7.8 %widen.5 = (f32[1024,2048]{1,0:T(8,128)}, f32[2048,512]{1,0:T(8,128)}) custom-call(bf16[1024,2048]{1,0:T(8,128)(2,1)} %bitcast.37, bf16[2048,512]{1,0:T(8,128)(2,1)} %get-tuple-element.147.refs_1_), custom_call_target="tpu_custom_call" | custom-call | bytes 18874368 | tf_op jit(solution)/shard_map/widen/pallas_call | solution.py:1450
  637.9 3.4 add.36
  641.3 3.3 multiply_reduce_fusion.2
  644.6 0.6 pad_maximum_fusion
  645.2 1.9 all-reduce.9.cloned.1.call-done
  647.1 7.5 %widen.4 = (f32[2048,512]{1,0:T(8,128)}, f32[2048,512]{1,0:T(8,128)}, f32[2048,512]{1,0:T(8,128)}) custom-call(bf16[2048,512]{1,0:T(8,128)(2,1)} %get-tuple-element.156.refs_0_, bf16[2048,512]{1,0:T(8,128)(2,1)} %get-tuple-element.157.refs_1_, bf16[2048,512]{1,0:T(8,128)(2,1)} %get-tuple-element.158.refs_2_), custom_call_target="tpu_custom_call" | custom-call | bytes 18874368 | tf_op jit(solution)/shard_map/widen/pallas_call | solution.py:1450
  (19 shorter events, 0.1 us)
Async XLA Ops:
  7.2 191.5 %all-gather.4.cloned.1.call-start = ((), (), s32[]{:S(2)}) async-start(), calls=%async_computation | async-start | bytes 9437184 | tf_op jit(solution)/shard_map/all_gather | solution.py:1607
  9.3 94.6 %copy-start.4 = (bf16[4,512]{1,0:T(4,128)(2,1)S(1)}, bf16[4,512]{1,0:T(4,128)(2,1)}, u32[]{:S(2)}) copy-start(bf16[4,512]{1,0:T(4,128)(2,1)} %param.24) | copy-start | bytes 12292
  9.3 95.9 %copy-start.1 = (bf16[256,2048]{1,0:T(8,128)(2,1)S(1)}, bf16[256,2048]{1,0:T(8,128)(2,1)}, u32[]{:S(2)}) copy-start(bf16[256,2048]{1,0:T(8,128)(2,1)} %grad_hbm.1) | copy-start | bytes 3145732
  103.9 158.4 %all-gather.6.cloned.1.call-start = ((), (), s32[]{:S(2)}) async-start(), calls=%async_computation.1 | async-start | bytes 3932160 | tf_op jit(solution)/shard_map/all_gather | solution.py:1621
  198.5 230.9 %all-reduce.13.cloned.1.call-start = ((), (), s32[]{:S(2)}) async-start(), calls=%async_computation.4 | async-start | bytes 16777216 | tf_op jit(solution)/shard_map/psum | solution.py:1632
  301.6 236.6 %all-reduce.11.cloned.1.call-start = ((), (), s32[]{:S(2)}) async-start(), calls=%async_computation.3 | async-start | bytes 12582912 | tf_op jit(solution)/shard_map/psum | solution.py:1647
  429.4 217.7 %all-reduce.9.cloned.1.call-start = ((), (), s32[]{:S(2)}) async-start(), calls=%async_computation.2 | async-start | bytes 12582912 | tf_op jit(solution)/shard_map/psum | solution.py:1664
  628.7 9.2 %copy-start.2 = (f32[16,16,2048]{2,1,0:T(8,128)S(1)}, f32[16,16,2048]{2,1,0:T(8,128)}, u32[]{:S(2)}) copy-start(f32[16,16,2048]{2,1,0:T(8,128)} %get-tuple-element.138) | copy-start | bytes 6291460
  637.9 3.4 copy-start
  637.9 3.4 copy-start.3
Sparse Core Ops, SparseCore 0:
  104.0 56.2 all-gather.3
  198.6 63.6 all-gather.5
  301.7 127.6 all-reduce.12
  433.5 104.6 all-reduce.10
  541.6 105.4 all-reduce.8

commit v10 on v9

--- a/solution.py
+++ b/solution.py
@@ -1277,7 +1277,7 @@
     T = few + rest.shape[1]
     L = n * T
     E, F, _ = gate_t.shape
-    block = max(T, min(512, L))
+    block = max(T, min(1024, L))
     owners = block // T
     rows = pl.BlockSpec((block, D), lambda i, e: (i, 0))
     units = pl.BlockSpec((block, F), lambda i, e: (i, e))

time: 664 us -> 662 us (level)
  no operation moved by 1% of the time
where the time goes in v10:
time: 662 us; the launch traced here: 659 us
  Pallas kernels  604 us (91%)
  waiting for transfers between devices  21.4 us (3%)
  between operations  14.6 us (2%)
  other arithmetic  9.22 us (1%)
    pallas_call x2, Pallas kernels, scatter_norm(): pl.pallas_call(functools.partial(scatter_norm_kernel, n, groups, steps, g...  209 us
    pallas_call x1, Pallas kernels, gather_project(): pl.pallas_call(functools.partial(gather_project_kernel, n), out_shape=[ja...  94.5 us
    pallas_call x1, Pallas kernels, attention_back(): pl.pallas_call(functools.partial(attention_back_kernel, n, steps, width),...  92.3 us
    pallas_call x1, Pallas kernels, gather_line(): pl.pallas_call(functools.partial(gather_line_kernel, n), out_shape=jax.Sh...  68.9 us
    pallas_call x1, Pallas kernels, forward_pass(): pl.pallas_call(forward_kernel, out_shape=[jax.ShapeDtypeStruct((L, D), f3...  54 us
    pallas_call x3, Pallas kernels, widen(): pl.pallas_call(functools.partial(widen_kernel, len(flat)), out_shape=[jax...  24.6 us
    pallas_call x1, Pallas kernels, backward_pass(): pl.pallas_call(backward_kernel, out_shape=[wide, wide, narrow, narrow], g...  24 us
    pallas_call x1, Pallas kernels, attention(): pl.pallas_call(functools.partial(attention_kernel, n), out_shape=[out] *...  22.7 us
  transfers between devices with their start and end apart: 5, of which 4 were waited for; matrix products, arithmetic and copies ran while one was open for 3% of the time, Pallas kernels for 70%

profile of v10, /device:TPU:12, one launch (start us, length us, event | category | flops | bytes accessed | tf_op | source)
XLA Modules:
  0.0 659.5 jit_solution(1348880746638789617)
XLA Ops:
  7.2 0.0 all-gather.4.cloned.1.call-start
  7.2 0.8 fusion.1
  8.0 0.7 select_reduce_fusion
  8.7 0.6 select_maximum_fusion.small_ref
  9.3 94.5 %gather_project.1 = (bf16[4,256,2048]{2,1,0:T(8,128)(2,1)}, bf16[4,256,2048]{2,1,0:T(8,128)(2,1)}, f32[4,256,512]{2,1,0:T(8,128)}, f32[4,256,512]{2,1,0:T(8,128)...) custom-call(bf16[256,2048]{1,0:T(8,128)(2,1)} %x_hbm.1, ...), custom_call_target="tpu_custom_call" | custom-call | flops 80000000000 | bytes 33554432 | tf_op jit(solution)/shard_map/gather_project/pallas_call | solution.py:356
  103.9 0.0 all-gather.6.cloned.1.call-start
  103.9 0.6 convert_element_type.17.gains
  105.2 0.9 slice.12
  106.1 0.6 broadcast_in_dim.23.limit_ref
  106.7 22.7 %attention.1 = (bf16[1024,512]{1,0:T(8,128)(2,1)}, bf16[1024,512]{1,0:T(8,128)(2,1)}, bf16[1024,512]{1,0:T(8,128)(2,1)}, bf16[4,64,2048]{2,1,0:T(8,128)(2,1)}) custom-call(s32[8,128]{1,0:T(8,128)} %broadcast_in_dim.23.limit_ref, f32[1024,512]{1,0:T(8,128)} %bitcast.47, f32[1024,512]{1,0:T(8,128)} %bitcast.49, bf16[1024,512]{1,0:T(8,128)(2,1)} %bitcast.51, ...), custom_call_target="tpu_custom_call" | custom-call | flops 20000000000 | bytes 16777216 | tf_op jit(solution)/shard_map/attention/pallas_call | solution.py:490
  129.5 68.9 %gather_line.1.mixed = bf16[1024,2048]{1,0:T(8,128)(2,1)} custom-call(bf16[1024,512]{1,0:T(8,128)(2,1)} %get-tuple-element.86.v_hbm), custom_call_target="tpu_custom_call" | custom-call | flops 70000001024 | bytes 8388608 | tf_op jit(solution)/shard_map/gather_line/pallas_call | solution.py:1547
  198.5 0.0 all-reduce.13.cloned.1.call-start
  198.5 54.0 %forward_pass.1 = (f32[1024,2048]{1,0:T(8,128)}, bf16[2048,1024]{1,0:T(8,128)(2,1)}, f32[1024,1024]{1,0:T(8,128)}, f32[1024,1024]{1,0:T(8,128)}, bf16[1024,1024]...) custom-call(bf16[1024,2048]{1,0:T(8,128)(2,1)} %gather_line.1.mixed,, ...), custom_call_target="tpu_custom_call" | custom-call | flops 21474836480 | bytes 52428800 | tf_op jit(solution)/shard_map/forward_pass/pallas_call | solution.py:1194
  252.5 9.8 %all-gather.6.cloned.1.call-done = bf16[768,2048]{1,0:T(8,128)(2,1)} async-done(((bf16[192,2048]{1,0:T(8,128)(2,1)}), bf16[768,2048]{1,0:T(8,128)(2,1)}) %all-gather.6.cloned.1.call-update) | async-done | bytes 3145744 | tf_op jit(solution)/shard_map/all_gather | solution.py:1621
  262.3 24.0 %backward_pass.1 = (bf16[1024,2048]{1,0:T(8,128)(2,1)}, bf16[1024,2048]{1,0:T(8,128)(2,1)}, bf16[1024,1024]{1,0:T(8,128)(2,1)}, bf16[1024,1024]{1,0:T(8,128)(2,1)}) custom-call(bf16[4,64,2048]{2,1,0:T(8,128)(2,1)} %get-tuple-element.97.first, bf16[4,192,2048]{2,1,0:T(8,128)(2,1)} %bitcast.61, f32[1024,1024]{1,0:T(8,128)} %get-tuple-element.99.gate_ref, ...), custom_call_target="tpu_custom_call" | custom-call | flops 12884901888 | bytes 41943040 | tf_op jit(solution)/shard_map/backward_pass/pallas_call | solution.py:1287
  286.3 13.6 %expert_grads.1 = (bf16[4,2048,256]{2,1,0:T(8,128)(2,1)}, bf16[4,2048,256]{2,1,0:T(8,128)(2,1)}) custom-call(bf16[2048,1024]{1,0:T(8,128)(2,1)} %get-tuple-element.105.xt, bf16[1024,1024]{1,0:T(8,128)(2,1)} %get-tuple-element.106.gate_grad, bf16[1024,1024]{1,0:T(8,128)(2,1)} %get-tuple-element.107.up_grad), custom_call_target="tpu_custom_call" | custom-call | flops 8589934592 | bytes 16777216 | tf_op jit(solution)/shard_map/expert_grads/pallas_call | solution.py:1425
  299.9 0.0 all-reduce.11.cloned.1.call-start
  300.0 118.9 %scatter_norm_gather.1 = (f32[16,16,2048]{2,1,0:T(8,128)}, bf16[4,16,16,2048]{3,2,1,0:T(8,128)(2,1)}, bf16[4,16,16,512]{3,2,1,0:T(8,128)(2,1)}, f32[8,2048]{1,0:T(8,128)}, bf16[4,256,2048]{2,1,0:T(8,128)(2,1)}) custom-call(bf16[4,16,16,2048]{3,2,1,0:T(8,128)(2,1)} %bitcast.36, bf16[16,16,2048]{2,1,0:T(8,128)(2,1)} %bitcast.34, ...), custom_call_target="tpu_custom_call" | custom-call | flops 1000000000 | bytes 1048576 | tf_op jit(solution)/shard_map/scatter_norm_gather/pallas_call | solution.py:1113
  418.9 6.3 convolution_convert_fusion
  425.2 2.5 all-reduce.13.cloned.1.call-done
  427.7 0.0 all-reduce.9.cloned.1.call-start
  427.8 92.3 %attention_back.1 = (bf16[2048,512]{1,0:T(8,128)(2,1)}, bf16[2048,512]{1,0:T(8,128)(2,1)}, bf16[2048,512]{1,0:T(8,128)(2,1)}, bf16[1024,2048]{1,0:T(8,128)(2,1)}...) custom-call(s32[8,128]{1,0:T(8,128)} %broadcast_in_dim.23.limit_ref, bf16[1024,512]{1,0:T(8,128)(2,1)} %get-tuple-element.93.q_ref, ...), custom_call_target="tpu_custom_call" | custom-call | flops 2000000000 | bytes 1048576 | tf_op jit(solution)/shard_map/attention_back/pallas_call | solution.py:724
  520.0 9.3 %widen.3 = (f32[8192,256]{1,0:T(8,128)}, f32[8192,256]{1,0:T(8,128)}) custom-call(bf16[8192,256]{1,0:T(8,128)(2,1)} %bitcast.38, bf16[8192,256]{1,0:T(8,128)(2,1)} %bitcast.39), custom_call_target="tpu_custom_call" | custom-call | bytes 25165824 | tf_op jit(solution)/shard_map/widen/pallas_call | solution.py:1450
  529.4 7.1 %all-reduce.11.cloned.1.call-done = (bf16[2048,512]{1,0:T(8,128)(2,1)}, bf16[4,256,2048]{2,1,0:T(8,128)(2,1)}) async-done(((bf16[2048,512]{1,0:T(8,128)(2,1)}, bf16[4,256,2048]{2,1,0:T(8,128)(2,1)}), (bf16[2048,512]{1,0:T(8,128)(2,1)}, bf16[4,256,2048]{2,1,0:T(8,128)(2,1)})) %all-reduce.11.cloned.1.call-update) | async-done | bytes 6291472 | tf_op jit(solution)/shard_map/psum | solution.py:1647
  536.5 90.4 %scatter_norm.1 = (f32[16,16,2048]{2,1,0:T(8,128)}, f32[8,512]{1,0:T(8,128)}) custom-call(bf16[4,16,16,2048]{3,2,1,0:T(8,128)(2,1)} %bitcast.40, bf16[16,16,2048]{2,1,0:T(8,128)(2,1)} %bitcast.35, f32[8,2048]{1,0:T(8,128)} %get-tuple-element.90.gain.refs_2_, f32[8,2048]{1,0:T(8,128)} %get-tuple-element.133.refs_3_, f32[2,512]{1,0:T(2,128)} %get-tuple-element.134.refs_4_), custom_call_target="tpu_custom_call" | custom-call | flops 1000000000 | bytes 1048576 | tf_op jit(solution)/shard_map/scatter_norm/pallas_call | solution.py:1113
  627.0 1.5 slice.15
  628.5 7.8 %widen.5 = (f32[1024,2048]{1,0:T(8,128)}, f32[2048,512]{1,0:T(8,128)}) custom-call(bf16[1024,2048]{1,0:T(8,128)(2,1)} %bitcast.37, bf16[2048,512]{1,0:T(8,128)(2,1)} %get-tuple-element.147.refs_1_), custom_call_target="tpu_custom_call" | custom-call | bytes 18874368 | tf_op jit(solution)/shard_map/widen/pallas_call | solution.py:1450
  636.2 3.4 add.36
  639.6 3.3 multiply_reduce_fusion.2
  642.9 0.6 pad_maximum_fusion
  643.5 1.9 all-reduce.9.cloned.1.call-done
  645.4 7.5 %widen.4 = (f32[2048,512]{1,0:T(8,128)}, f32[2048,512]{1,0:T(8,128)}, f32[2048,512]{1,0:T(8,128)}) custom-call(bf16[2048,512]{1,0:T(8,128)(2,1)} %get-tuple-element.156.refs_0_, bf16[2048,512]{1,0:T(8,128)(2,1)} %get-tuple-element.157.refs_1_, bf16[2048,512]{1,0:T(8,128)(2,1)} %get-tuple-element.158.refs_2_), custom_call_target="tpu_custom_call" | custom-call | bytes 18874368 | tf_op jit(solution)/shard_map/widen/pallas_call | solution.py:1450
  (19 shorter events, 0.1 us)
Async XLA Ops:
  7.2 191.3 %all-gather.4.cloned.1.call-start = ((), (), s32[]{:S(2)}) async-start(), calls=%async_computation | async-start | bytes 9437184 | tf_op jit(solution)/shard_map/all_gather | solution.py:1607
  9.3 94.6 %copy-start.4 = (bf16[4,512]{1,0:T(4,128)(2,1)S(1)}, bf16[4,512]{1,0:T(4,128)(2,1)}, u32[]{:S(2)}) copy-start(bf16[4,512]{1,0:T(4,128)(2,1)} %param.24) | copy-start | bytes 12292
  9.3 95.9 %copy-start.1 = (bf16[256,2048]{1,0:T(8,128)(2,1)S(1)}, bf16[256,2048]{1,0:T(8,128)(2,1)}, u32[]{:S(2)}) copy-start(bf16[256,2048]{1,0:T(8,128)(2,1)} %grad_hbm.1) | copy-start | bytes 3145732
  103.9 158.4 %all-gather.6.cloned.1.call-start = ((), (), s32[]{:S(2)}) async-start(), calls=%async_computation.1 | async-start | bytes 3932160 | tf_op jit(solution)/shard_map/all_gather | solution.py:1621
  198.5 229.2 %all-reduce.13.cloned.1.call-start = ((), (), s32[]{:S(2)}) async-start(), calls=%async_computation.4 | async-start | bytes 16777216 | tf_op jit(solution)/shard_map/psum | solution.py:1632
  299.9 236.6 %all-reduce.11.cloned.1.call-start = ((), (), s32[]{:S(2)}) async-start(), calls=%async_computation.3 | async-start | bytes 12582912 | tf_op jit(solution)/shard_map/psum | solution.py:1647
  427.7 217.7 %all-reduce.9.cloned.1.call-start = ((), (), s32[]{:S(2)}) async-start(), calls=%async_computation.2 | async-start | bytes 12582912 | tf_op jit(solution)/shard_map/psum | solution.py:1664
  627.0 9.3 %copy-start.2 = (f32[16,16,2048]{2,1,0:T(8,128)S(1)}, f32[16,16,2048]{2,1,0:T(8,128)}, u32[]{:S(2)}) copy-start(f32[16,16,2048]{2,1,0:T(8,128)} %get-tuple-element.138) | copy-start | bytes 6291460
  636.2 3.4 copy-start
  636.2 3.4 copy-start.3
Sparse Core Ops, SparseCore 0:
  104.0 56.2 all-gather.3
  198.6 63.6 all-gather.5
  300.0 127.6 all-reduce.12
  431.8 104.6 all-reduce.10
  539.9 105.4 all-reduce.8
